TPU v7x, 32 devices: a whole 2x2x4 slice. The times are simulated.
32 devices in a mesh: depth: 4 (over y, x), row: 8 (over z, core).
Axes of the slice: x: 2, y: 2, z: 4, core: 2. Of those that a mesh axis runs over, the one named last changes fastest.
Arguments:
- index_volume: bfloat16 [4, 128, 2048], P('depth', 'row'), may hold values from -4 to 4
- angles: int32 [2], replicated, may hold values from 0 to 15
- offsets: int32 [4], P('depth'), may hold values from -4 to 4, as said below
- measured: bfloat16 [2, 128, 2048], P(None, 'row'), may hold values from 0 to 2
Outputs:
- gradient: float32 [4, 128, 2048], P('depth', 'row')
Inputs may be any that keep to these rules, and one draw needn't show every extreme that they name: `offsets`: each of -4 and 4 is taken by at least one slice.
All inputs are finite; a program needn't handle non-finite values.
Results may differ from a plain program's by a relative error of at most 0.0003.
Values may be sent and summed in bfloat16 or wider, within the bound.
No kernel may reach another device: no remote copies, remote signals or barrier semaphores. Data moves between devices by JAX's collectives and lax.ppermute only.
A program may use at most 64 MiB of HBM per device.

v0:
```python
import math

import jax
import jax.numpy as jnp
from jax import lax
from jax.sharding import PartitionSpec as P

TILTS = 16
HALF = 10
SHIFT = 4
HALFCOL = 64
COLBLK = 128


PHASE_SCALE = 0.5
CHIRP_ROW = 1.3
CHIRP_COL = 1.7


def padded_2(shard, sides, width):
    for axis, dim in sides:
        size, length = (lax.axis_size(axis), shard.shape[dim])
        up = [(i, (i + 1) % size) for i in range(size - 1)]
        down = [(j, i) for i, j in up]
        last = lax.slice_in_dim(shard, length - width, length, axis=dim)
        initial = lax.slice_in_dim(shard, 0, width, axis=dim)
        before = lax.ppermute(last, axis, up)
        after = lax.ppermute(initial, axis, down)
        shard = jnp.concatenate([before, shard, after], axis=dim)
    return shard


def from_behind(shard, axis, by):
    length = lax.axis_size(axis)
    pairs = [(i, i + by) for i in range(length) if 0 <= i + by < length]
    return lax.ppermute(shard, axis, pairs)


def kernel_values(distance, radius, chirp_rate):
    inside = jnp.abs(distance) <= radius
    phase_arg = chirp_rate / radius * distance * distance
    weight = 1.0 / math.sqrt(2 * radius + 1)
    real_part = jnp.where(inside, jnp.cos(phase_arg) * weight, 0.0)
    imag_part = jnp.where(inside, jnp.sin(phase_arg) * weight, 0.0)
    return (real_part, imag_part)


def row_band(offset, height, margin, conjugate):
    extent = (height, height + 2 * margin)
    target = lax.broadcasted_iota(jnp.int32, extent, 0)
    source = lax.broadcasted_iota(jnp.int32, extent, 1)
    offset_used = -offset if conjugate else offset
    distance = (source - target - margin - offset_used).astype(jnp.float32)
    real_part, imag_part = kernel_values(distance, HALF, CHIRP_ROW)
    return (real_part, -imag_part) if conjugate else (real_part, imag_part)


def column_band(conjugate, block_width):
    extent = (block_width + 2 * HALFCOL, block_width)
    source = lax.broadcasted_iota(jnp.int32, extent, 0)
    target = lax.broadcasted_iota(jnp.int32, extent, 1)
    distance = (source - target - HALFCOL).astype(jnp.float32)
    real_part, imag_part = kernel_values(distance, HALFCOL, CHIRP_COL)
    return (real_part, -imag_part) if conjugate else (real_part, imag_part)


def mix_rows(band, extended):

    def product(matrix, operand):
        return jnp.einsum("ij,mjc->mic", matrix, operand, precision=lax.Precision.HIGHEST)

    real_part = product(band[0], extended[:, 0]) - product(band[1], extended[:, 1])
    imag_part = product(band[0], extended[:, 1]) + product(band[1], extended[:, 0])
    return jnp.stack([real_part, imag_part], axis=1)


def block_product(window, band):

    def product(operand, matrix):
        return jnp.einsum("mrbj,ji->mrbi", operand, matrix, precision=lax.Precision.HIGHEST)

    real_part = product(window[:, 0], band[0]) - product(window[:, 1], band[1])
    imag_part = product(window[:, 1], band[0]) + product(window[:, 0], band[1])
    return jnp.stack([real_part, imag_part], axis=1)


def mix_columns(band, field):
    amount, _, height, columns = field.shape
    blocks = columns // COLBLK
    padded = jnp.pad(field, ((0, 0), (0, 0), (0, 0), (HALFCOL, COLBLK - HALFCOL)))
    middle = padded[..., :columns].reshape(amount, 2, height, blocks, COLBLK)
    beyond = padded[..., COLBLK : columns + COLBLK].reshape(amount, 2, height, blocks, COLBLK)
    window = jnp.concatenate([middle, beyond], axis=4)
    return block_product(window, band).reshape(amount, 2, height, columns)


def rotate(field, cosine, sine):
    real_part = cosine * field[:, 0] - sine * field[:, 1]
    imag_part = cosine * field[:, 1] + sine * field[:, 0]
    return jnp.stack([real_part, imag_part], axis=1)


def slab_forward(field, index_volume, offsets, active):
    margin = HALF + SHIFT
    height = field.shape[2]
    col_band = column_band(False, COLBLK)
    phase_arg = PHASE_SCALE * index_volume[0].astype(jnp.float32)
    transmitted = rotate(field, jnp.cos(phase_arg), jnp.sin(phase_arg))
    stored_fields = [transmitted]
    extended = padded_2(transmitted, (("row", 2),), margin)
    band = row_band(offsets[0], height, margin, False)

    def advance(operand, band=band):
        return mix_columns(col_band, mix_rows(band, operand))

    def remain(operand):
        return operand[:, :, margin : margin + height, :]

    field = lax.cond(active, advance, remain, extended)
    return (field, jnp.stack(stored_fields, axis=0))


def slab_adjoint(adjoint, stored, index_volume, offsets, active):
    margin = HALF + SHIFT
    height = adjoint.shape[2]
    col_band = column_band(True, COLBLK)
    layers = index_volume.shape[0]
    slab_grads = [None] * layers

    def column_step(operand):
        return mix_columns(col_band, operand)

    def unchanged(operand):
        return operand

    def remain(operand):
        return operand[:, :, margin : margin + height, :]

    for layer_no in reversed(range(layers)):
        returned = lax.cond(active, column_step, unchanged, adjoint)
        extended = padded_2(returned, (("row", 2),), margin)
        band = row_band(offsets[layer_no], height, margin, True)

        def row_step(operand, band=band):
            return mix_rows(band, operand)

        returned = lax.cond(active, row_step, remain, extended)
        transmitted = stored[layer_no]
        slab_grads[layer_no] = PHASE_SCALE * jnp.sum(
            transmitted[:, 0] * returned[:, 1] - transmitted[:, 1] * returned[:, 0], axis=0
        )
        phase_arg = PHASE_SCALE * index_volume[layer_no].astype(jnp.float32)
        adjoint = rotate(returned, jnp.cos(phase_arg), -jnp.sin(phase_arg))
    return (adjoint, jnp.stack(slab_grads, axis=0))


def plane_waves(angles, row_start, height, columns, total_rows, total_cols):
    across = angles - TILTS // 2
    along = jnp.mod(3 * angles, TILTS) - TILTS // 2
    row_index = row_start + lax.broadcasted_iota(jnp.int32, (height, columns), 0)
    col_index = lax.broadcasted_iota(jnp.int32, (height, columns), 1)
    period = total_cols * total_rows
    cycles_int = jnp.mod(
        across[:, None, None] * col_index[None] * total_rows
        + along[:, None, None] * row_index[None] * total_cols,
        period,
    )
    phase_arg = 2.0 * math.pi / period * cycles_int.astype(jnp.float32)
    return jnp.stack([jnp.cos(phase_arg), jnp.sin(phase_arg)], axis=1)


def body(index_volume, angles, offsets, measured):
    sections = lax.axis_size("depth")
    section_no = lax.axis_index("depth")
    number = angles.shape[0]
    layers = index_volume.shape[0]
    height = index_volume.shape[1]
    columns = index_volume.shape[2]
    row_start = lax.axis_index("row") * height
    total_rows = height * lax.axis_size("row")
    intensity = measured.astype(jnp.float32)
    grad_init = jnp.zeros((layers, height, columns), jnp.float32)
    incident = plane_waves(angles, row_start, height, columns, total_rows, columns)
    kept_init = jnp.zeros((layers,) + incident.shape, jnp.float32)

    def forward_compute(counter, received, stored, exit_field):
        angle_no = counter - section_no
        active = (angle_no >= 0) & (angle_no < number)
        chosen = jnp.clip(angle_no, 0, number - 1)
        entering = jnp.where(
            section_no == 0, lax.dynamic_slice_in_dim(incident, chosen, 1, 0), received
        )
        result, kept = slab_forward(entering, index_volume, offsets, active)
        placed_kept = lax.dynamic_update_slice_in_dim(stored, kept, chosen, 1)
        stored = jnp.where(active, placed_kept, stored)
        placed = lax.dynamic_update_slice_in_dim(exit_field, result, chosen, 0)
        exit_field = jnp.where(active, placed, exit_field)
        return (result, stored, exit_field)

    def forward_turn(counter, carried):
        result, stored, exit_field = forward_compute(counter, carried[0], carried[1], carried[2])
        return (from_behind(result, "depth", 1), stored, exit_field)

    zero_single = jnp.zeros((1,) + incident.shape[1:], jnp.float32)
    turns = sections + number - 1
    received, stored, exit_field = lax.fori_loop(
        0, turns - 1, forward_turn, (zero_single, kept_init, jnp.zeros_like(incident))
    )
    leftover, stored, exit_field = forward_compute(turns - 1, received, stored, exit_field)
    errors = exit_field[:, 0] * exit_field[:, 0] + exit_field[:, 1] * exit_field[:, 1] - intensity
    exit_adjoint = 2.0 * errors[:, None] * exit_field

    def backward_compute(counter, received, gradient):
        angle_no = counter - (sections - 1 - section_no)
        active = (angle_no >= 0) & (angle_no < number)
        chosen = jnp.clip(angle_no, 0, number - 1)
        entering = jnp.where(
            section_no == sections - 1,
            lax.dynamic_slice_in_dim(exit_adjoint, chosen, 1, 0),
            received,
        )
        result, slab_terms = slab_adjoint(
            entering, lax.dynamic_slice_in_dim(stored, chosen, 1, 1), index_volume, offsets, active
        )
        return (result, jnp.where(active, gradient + slab_terms, gradient))

    def backward_turn(counter, carried):
        result, gradient = backward_compute(counter, carried[0], carried[1])
        return (from_behind(result, "depth", -1), gradient)

    received, gradient = lax.fori_loop(0, turns - 1, backward_turn, (zero_single, grad_init))
    leftover, gradient = backward_compute(turns - 1, received, gradient)
    return gradient


def solution(mesh):
    in_specs = (P("depth", "row", None), P(), P("depth"), P(None, "row", None))
    out_specs = P("depth", "row", None)
    return jax.shard_map(body, mesh=mesh, in_specs=in_specs, out_specs=out_specs, check_vma=False)
```

profile of v0, /device:TPU:1, one launch (start us, length us, event | category | flops | bytes accessed | tf_op | source)
XLA Modules:
  0.0 232.1 jit_solution(331485065117592520)
XLA Ops:
  2.8 94.0 %while.37 = (s32[]{:T(128)}, f32[1,2,16,2048]{3,2,1,0:T(8,128)S(1)}, f32[1,2,2,16,2048]{4,3,2,1,0:T(8,128)S(1)}, f32[2,2,16,2048]{3,2,1,0:T(8,128)S(1)}, s32[]{:...) while((s32[]{:T(128)}, ...), condition=%wide.region_3.4_spmd, body=%wide.region_0.3_spmd.sunk | while | flops 474623232 | bytes 22334636 | solution.py:206
  5.6 4.6 %collective-permute-start.1 = (f32[1,2,14,2048]{3,2,1,0:T(8,128)S(1)}, f32[1,2,14,2048]{3,2,1,0:T(8,128)}, u32[]{:S(2)}, u32[]{:S(2)}) collective-permute-start(f32[1,2,14,2048]{3,2,1,0:T(8,128)S(1)} %get-tuple-element.1061), channel_id=1, source_target_pairs={{0,1},{1,2},{2,3},{3,4},{4,5},{5,6},{6,7},{8,9},{9,10},{10,11},{11... | collective-permute-start | bytes 688136 | tf_op jit(solution)/shard_map/while/body/eval_jaxpr/ppermute | solution.py:27
  14.5 5.2 %conditional.14 = (f32[1,2,16,2048]{3,2,1,0:T(8,128)S(1)}) conditional(s32[]{:T(128)} %convert_element_type.275, f32[1,2,16,2048]{3,2,1,0:T(8,128)S(1)} %pad_maximum_fusion.18, (f32[16,44]{1,0:T(8,128)S(1)}, f32[1,2,44,2048]{3,2,1,0:T(8,128)S(1)}, f32[256,128]{1,0:T(8,128)S(1)}, f32[256,128]{1,0:T(8,128)S(1)}, f32[256,128]{1,0:T(8,128)S(1)}, ...), branch_computations={%region_1.1_spmd, %region_2.2_spmd} | conditional | flops 473276928 | bytes 9486344 | solution.py:119
  27.2 6.3 %collective-permute-start.1 = (f32[1,2,14,2048]{3,2,1,0:T(8,128)S(1)}, f32[1,2,14,2048]{3,2,1,0:T(8,128)}, u32[]{:S(2)}, u32[]{:S(2)}) collective-permute-start(f32[1,2,14,2048]{3,2,1,0:T(8,128)S(1)} %get-tuple-element.1061), channel_id=1, source_target_pairs={{0,1},{1,2},{2,3},{3,4},{4,5},{5,6},{6,7},{8,9},{9,10},{10,11},{11... | collective-permute-start | bytes 688136 | tf_op jit(solution)/shard_map/while/body/eval_jaxpr/ppermute | solution.py:27
  37.8 5.2 %conditional.14 = (f32[1,2,16,2048]{3,2,1,0:T(8,128)S(1)}) conditional(s32[]{:T(128)} %convert_element_type.275, f32[1,2,16,2048]{3,2,1,0:T(8,128)S(1)} %pad_maximum_fusion.18, (f32[16,44]{1,0:T(8,128)S(1)}, f32[1,2,44,2048]{3,2,1,0:T(8,128)S(1)}, f32[256,128]{1,0:T(8,128)S(1)}, f32[256,128]{1,0:T(8,128)S(1)}, f32[256,128]{1,0:T(8,128)S(1)}, ...), branch_computations={%region_1.1_spmd, %region_2.2_spmd} | conditional | flops 473276928 | bytes 9486344 | solution.py:119
  43.0 4.3 %collective-permute-start.2 = (f32[1,2,16,2048]{3,2,1,0:T(8,128)S(1)}, f32[1,2,16,2048]{3,2,1,0:T(8,128)S(1)}, u32[]{:S(2)}, u32[]{:S(2)}) collective-permute-start(f32[1,2,16,2048]{3,2,1,0:T(8,128)S(1)} %get-tuple-element.1153), channel_id=1, source_target_pairs={{0,8},{8,16},{16,24},{1,9},{9,17},{17,25},{2,10},{10,18},{18,26},{... | collective-permute-start | bytes 786440 | tf_op jit(solution)/shard_map/while/body/eval_jaxpr/ppermute | solution.py:36
  53.3 6.3 %collective-permute-start.1 = (f32[1,2,14,2048]{3,2,1,0:T(8,128)S(1)}, f32[1,2,14,2048]{3,2,1,0:T(8,128)}, u32[]{:S(2)}, u32[]{:S(2)}) collective-permute-start(f32[1,2,14,2048]{3,2,1,0:T(8,128)S(1)} %get-tuple-element.1061), channel_id=1, source_target_pairs={{0,1},{1,2},{2,3},{3,4},{4,5},{5,6},{6,7},{8,9},{9,10},{10,11},{11... | collective-permute-start | bytes 688136 | tf_op jit(solution)/shard_map/while/body/eval_jaxpr/ppermute | solution.py:27
  64.0 9.4 %collective-permute-start.2 = (f32[1,2,16,2048]{3,2,1,0:T(8,128)S(1)}, f32[1,2,16,2048]{3,2,1,0:T(8,128)S(1)}, u32[]{:S(2)}, u32[]{:S(2)}) collective-permute-start(f32[1,2,16,2048]{3,2,1,0:T(8,128)S(1)} %get-tuple-element.1153), channel_id=1, source_target_pairs={{0,8},{8,16},{16,24},{1,9},{9,17},{17,25},{2,10},{10,18},{18,26},{... | collective-permute-start | bytes 786440 | tf_op jit(solution)/shard_map/while/body/eval_jaxpr/ppermute | solution.py:36
  79.5 5.4 %collective-permute-start.1 = (f32[1,2,14,2048]{3,2,1,0:T(8,128)S(1)}, f32[1,2,14,2048]{3,2,1,0:T(8,128)}, u32[]{:S(2)}, u32[]{:S(2)}) collective-permute-start(f32[1,2,14,2048]{3,2,1,0:T(8,128)S(1)} %get-tuple-element.1061), channel_id=1, source_target_pairs={{0,1},{1,2},{2,3},{3,4},{4,5},{5,6},{6,7},{8,9},{9,10},{10,11},{11... | collective-permute-start | bytes 688136 | tf_op jit(solution)/shard_map/while/body/eval_jaxpr/ppermute | solution.py:27
  89.2 4.3 %collective-permute-start.2 = (f32[1,2,16,2048]{3,2,1,0:T(8,128)S(1)}, f32[1,2,16,2048]{3,2,1,0:T(8,128)S(1)}, u32[]{:S(2)}, u32[]{:S(2)}) collective-permute-start(f32[1,2,16,2048]{3,2,1,0:T(8,128)S(1)} %get-tuple-element.1153), channel_id=1, source_target_pairs={{0,8},{8,16},{16,24},{1,9},{9,17},{17,25},{2,10},{10,18},{18,26},{... | collective-permute-start | bytes 786440 | tf_op jit(solution)/shard_map/while/body/eval_jaxpr/ppermute | solution.py:36
  97.4 5.3 %collective-permute-start.6 = (f32[1,2,14,2048]{3,2,1,0:T(8,128)S(1)}, f32[1,2,14,2048]{3,2,1,0:T(8,128)S(1)}, u32[]{:S(2)}, u32[]{:S(2)}) collective-permute-start(f32[1,2,14,2048]{3,2,1,0:T(8,128)S(1)} %get-tuple-element.941), channel_id=1, source_target_pairs={{0,1},{1,2},{2,3},{3,4},{4,5},{5,6},{6,7},{8,9},{9,10},{10,11},{11... | collective-permute-start | bytes 688136 | tf_op jit(solution)/shard_map/ppermute | solution.py:27
  106.0 4.4 %collective-permute-done.7 = f32[1,2,14,2048]{3,2,1,0:T(8,128)S(1)} collective-permute-done((f32[1,2,14,2048]{3,2,1,0:T(8,128)S(1)}, f32[1,2,14,2048]{3,2,1,0:T(8,128)S(1)}, u32[]{:S(2)}, u32[]{:S(2)}) %collective-permute-start.7) | collective-permute-done | bytes 229408 | tf_op jit(solution)/shard_map/ppermute | solution.py:28
  111.8 101.9 %while.38 = (s32[]{:T(128)}, f32[1,2,16,2048]{3,2,1,0:T(8,128)S(1)}, f32[1,16,2048]{2,1,0:T(8,128)S(1)}, bf16[1,16,2048]{2,1,0:T(8,128)(2,1)S(1)}, s32[]{:T(128)...) while((s32[]{:T(128)}, ...), condition=%wide.region_11.12_spmd.clone, body=%wide.region_6.11_spmd.clone.sunk | while | flops 473715328 | bytes 18484388 | solution.py:231
  113.9 3.6 %collective-permute-start.4 = (f32[1,2,14,2048]{3,2,1,0:T(8,128)S(1)}, f32[1,2,14,2048]{3,2,1,0:T(8,128)S(1)}, u32[]{:S(2)}, u32[]{:S(2)}) collective-permute-start(f32[1,2,14,2048]{3,2,1,0:T(8,128)S(1)} %get-tuple-element.1072), channel_id=1, source_target_pairs={{0,1},{1,2},{2,3},{3,4},{4,5},{5,6},{6,7},{8,9},{9,10},{10,11},{11... | collective-permute-start | bytes 688136 | tf_op jit(solution)/shard_map/while/body/eval_jaxpr/ppermute | solution.py:27
  122.9 11.3 %collective-permute-done.5 = f32[1,2,16,2048]{3,2,1,0:T(8,128)S(1)} collective-permute-done((f32[1,2,16,2048]{3,2,1,0:T(8,128)S(1)}, f32[1,2,16,2048]{3,2,1,0:T(8,128)S(1)}, u32[]{:S(2)}, u32[]{:S(2)}) %collective-permute-start.5) | collective-permute-done | bytes 262176 | tf_op jit(solution)/shard_map/while/body/eval_jaxpr/ppermute | solution.py:36
  136.2 5.4 %collective-permute-start.4 = (f32[1,2,14,2048]{3,2,1,0:T(8,128)S(1)}, f32[1,2,14,2048]{3,2,1,0:T(8,128)S(1)}, u32[]{:S(2)}, u32[]{:S(2)}) collective-permute-start(f32[1,2,14,2048]{3,2,1,0:T(8,128)S(1)} %get-tuple-element.1072), channel_id=1, source_target_pairs={{0,1},{1,2},{2,3},{3,4},{4,5},{5,6},{6,7},{8,9},{9,10},{10,11},{11... | collective-permute-start | bytes 688136 | tf_op jit(solution)/shard_map/while/body/eval_jaxpr/ppermute | solution.py:27
  147.0 7.4 %collective-permute-done.5 = f32[1,2,16,2048]{3,2,1,0:T(8,128)S(1)} collective-permute-done((f32[1,2,16,2048]{3,2,1,0:T(8,128)S(1)}, f32[1,2,16,2048]{3,2,1,0:T(8,128)S(1)}, u32[]{:S(2)}, u32[]{:S(2)}) %collective-permute-start.5) | collective-permute-done | bytes 262176 | tf_op jit(solution)/shard_map/while/body/eval_jaxpr/ppermute | solution.py:36
  156.4 5.4 %collective-permute-start.4 = (f32[1,2,14,2048]{3,2,1,0:T(8,128)S(1)}, f32[1,2,14,2048]{3,2,1,0:T(8,128)S(1)}, u32[]{:S(2)}, u32[]{:S(2)}) collective-permute-start(f32[1,2,14,2048]{3,2,1,0:T(8,128)S(1)} %get-tuple-element.1072), channel_id=1, source_target_pairs={{0,1},{1,2},{2,3},{3,4},{4,5},{5,6},{6,7},{8,9},{9,10},{10,11},{11... | collective-permute-start | bytes 688136 | tf_op jit(solution)/shard_map/while/body/eval_jaxpr/ppermute | solution.py:27
  167.1 21.7 %collective-permute-done.5 = f32[1,2,16,2048]{3,2,1,0:T(8,128)S(1)} collective-permute-done((f32[1,2,16,2048]{3,2,1,0:T(8,128)S(1)}, f32[1,2,16,2048]{3,2,1,0:T(8,128)S(1)}, u32[]{:S(2)}, u32[]{:S(2)}) %collective-permute-start.5) | collective-permute-done | bytes 262176 | tf_op jit(solution)/shard_map/while/body/eval_jaxpr/ppermute | solution.py:36
  189.0 3.8 %conditional.15 = (f32[1,2,16,2048]{3,2,1,0:T(8,128)S(1)}) conditional(s32[]{:T(128)} %convert_element_type.279, f32[1,2,16,2048]{3,2,1,0:T(8,128)S(1)} %dynamic-slice_select_fusion.6, (f32[1,2,16,2048]{3,2,1,0:T(8,128)S(1)}, f32[256,128]{1,0:T(8,128)S(1)}, f32[256,128]{1,0:T(8,128)S(1)}, f32[]{:T(128)}, f32[256,128]{1,0:T(8,128)S(1)}) %tuple.224), branch_computations={%region_7.7_spmd, %region_8.8_spmd.clone.clone} | conditional | flops 403243008 | bytes 6979608 | solution.py:140
  194.8 5.4 %collective-permute-start.4 = (f32[1,2,14,2048]{3,2,1,0:T(8,128)S(1)}, f32[1,2,14,2048]{3,2,1,0:T(8,128)S(1)}, u32[]{:S(2)}, u32[]{:S(2)}) collective-permute-start(f32[1,2,14,2048]{3,2,1,0:T(8,128)S(1)} %get-tuple-element.1072), channel_id=1, source_target_pairs={{0,1},{1,2},{2,3},{3,4},{4,5},{5,6},{6,7},{8,9},{9,10},{10,11},{11... | collective-permute-start | bytes 688136 | tf_op jit(solution)/shard_map/while/body/eval_jaxpr/ppermute | solution.py:27
  207.0 6.8 %collective-permute-done.5 = f32[1,2,16,2048]{3,2,1,0:T(8,128)S(1)} collective-permute-done((f32[1,2,16,2048]{3,2,1,0:T(8,128)S(1)}, f32[1,2,16,2048]{3,2,1,0:T(8,128)S(1)}, u32[]{:S(2)}, u32[]{:S(2)}) %collective-permute-start.5) | collective-permute-done | bytes 262176 | tf_op jit(solution)/shard_map/while/body/eval_jaxpr/ppermute | solution.py:36
  216.7 5.4 %collective-permute-start.8 = (f32[1,2,14,2048]{3,2,1,0:T(8,128)S(1)}, f32[1,2,14,2048]{3,2,1,0:T(8,128)S(1)}, u32[]{:S(2)}, u32[]{:S(2)}) collective-permute-start(f32[1,2,14,2048]{3,2,1,0:T(8,128)S(1)} %get-tuple-element.939), channel_id=1, source_target_pairs={{0,1},{1,2},{2,3},{3,4},{4,5},{5,6},{6,7},{8,9},{9,10},{10,11},{11... | collective-permute-start | bytes 688136 | tf_op jit(solution)/shard_map/ppermute | solution.py:27
  225.5 4.4 %collective-permute-done.9 = f32[1,2,14,2048]{3,2,1,0:T(8,128)S(1)} collective-permute-done((f32[1,2,14,2048]{3,2,1,0:T(8,128)S(1)}, f32[1,2,14,2048]{3,2,1,0:T(8,128)S(1)}, u32[]{:S(2)}, u32[]{:S(2)}) %collective-permute-start.9) | collective-permute-done | bytes 229408 | tf_op jit(solution)/shard_map/ppermute | solution.py:28
  (252 shorter events, 107.6 us)
Async XLA Ops:
  3.6 8.6 %collective-permute-start = (f32[1,2,14,2048]{3,2,1,0:T(8,128)S(1)}, f32[1,2,14,2048]{3,2,1,0:T(8,128)S(1)}, u32[]{:S(2)}, u32[]{:S(2)}) collective-permute-start(f32[1,2,14,2048]{3,2,1,0:T(8,128)S(1)} %get-tuple-element.1060), channel_id=1, source_target_pairs={{1,0},{2,1},{3,2},{4,3},{5,4},{6,5},{7,6},{9,8},{10,9},{11,10},{12... | collective-permute-start | bytes 688136 | tf_op jit(solution)/shard_map/while/body/eval_jaxpr/ppermute | solution.py:28
  5.6 7.9 %collective-permute-start.1 = (f32[1,2,14,2048]{3,2,1,0:T(8,128)S(1)}, f32[1,2,14,2048]{3,2,1,0:T(8,128)}, u32[]{:S(2)}, u32[]{:S(2)}) collective-permute-start(f32[1,2,14,2048]{3,2,1,0:T(8,128)S(1)} %get-tuple-element.1061), channel_id=1, source_target_pairs={{0,1},{1,2},{2,3},{3,4},{4,5},{5,6},{6,7},{8,9},{9,10},{10,11},{11... | collective-permute-start | bytes 688136 | tf_op jit(solution)/shard_map/while/body/eval_jaxpr/ppermute | solution.py:27
  25.3 10.3 %collective-permute-start = (f32[1,2,14,2048]{3,2,1,0:T(8,128)S(1)}, f32[1,2,14,2048]{3,2,1,0:T(8,128)S(1)}, u32[]{:S(2)}, u32[]{:S(2)}) collective-permute-start(f32[1,2,14,2048]{3,2,1,0:T(8,128)S(1)} %get-tuple-element.1060), channel_id=1, source_target_pairs={{1,0},{2,1},{3,2},{4,3},{5,4},{6,5},{7,6},{9,8},{10,9},{11,10},{12... | collective-permute-start | bytes 688136 | tf_op jit(solution)/shard_map/while/body/eval_jaxpr/ppermute | solution.py:28
  27.2 9.6 %collective-permute-start.1 = (f32[1,2,14,2048]{3,2,1,0:T(8,128)S(1)}, f32[1,2,14,2048]{3,2,1,0:T(8,128)}, u32[]{:S(2)}, u32[]{:S(2)}) collective-permute-start(f32[1,2,14,2048]{3,2,1,0:T(8,128)S(1)} %get-tuple-element.1061), channel_id=1, source_target_pairs={{0,1},{1,2},{2,3},{3,4},{4,5},{5,6},{6,7},{8,9},{9,10},{10,11},{11... | collective-permute-start | bytes 688136 | tf_op jit(solution)/shard_map/while/body/eval_jaxpr/ppermute | solution.py:27
  51.4 10.4 %collective-permute-start = (f32[1,2,14,2048]{3,2,1,0:T(8,128)S(1)}, f32[1,2,14,2048]{3,2,1,0:T(8,128)S(1)}, u32[]{:S(2)}, u32[]{:S(2)}) collective-permute-start(f32[1,2,14,2048]{3,2,1,0:T(8,128)S(1)} %get-tuple-element.1060), channel_id=1, source_target_pairs={{1,0},{2,1},{3,2},{4,3},{5,4},{6,5},{7,6},{9,8},{10,9},{11,10},{12... | collective-permute-start | bytes 688136 | tf_op jit(solution)/shard_map/while/body/eval_jaxpr/ppermute | solution.py:28
  53.3 9.6 %collective-permute-start.1 = (f32[1,2,14,2048]{3,2,1,0:T(8,128)S(1)}, f32[1,2,14,2048]{3,2,1,0:T(8,128)}, u32[]{:S(2)}, u32[]{:S(2)}) collective-permute-start(f32[1,2,14,2048]{3,2,1,0:T(8,128)S(1)} %get-tuple-element.1061), channel_id=1, source_target_pairs={{0,1},{1,2},{2,3},{3,4},{4,5},{5,6},{6,7},{8,9},{9,10},{10,11},{11... | collective-permute-start | bytes 688136 | tf_op jit(solution)/shard_map/while/body/eval_jaxpr/ppermute | solution.py:27
  64.0 12.7 %collective-permute-start.2 = (f32[1,2,16,2048]{3,2,1,0:T(8,128)S(1)}, f32[1,2,16,2048]{3,2,1,0:T(8,128)S(1)}, u32[]{:S(2)}, u32[]{:S(2)}) collective-permute-start(f32[1,2,16,2048]{3,2,1,0:T(8,128)S(1)} %get-tuple-element.1153), channel_id=1, source_target_pairs={{0,8},{8,16},{16,24},{1,9},{9,17},{17,25},{2,10},{10,18},{18,26},{... | collective-permute-start | bytes 786440 | tf_op jit(solution)/shard_map/while/body/eval_jaxpr/ppermute | solution.py:36
  77.6 9.4 %collective-permute-start = (f32[1,2,14,2048]{3,2,1,0:T(8,128)S(1)}, f32[1,2,14,2048]{3,2,1,0:T(8,128)S(1)}, u32[]{:S(2)}, u32[]{:S(2)}) collective-permute-start(f32[1,2,14,2048]{3,2,1,0:T(8,128)S(1)} %get-tuple-element.1060), channel_id=1, source_target_pairs={{1,0},{2,1},{3,2},{4,3},{5,4},{6,5},{7,6},{9,8},{10,9},{11,10},{12... | collective-permute-start | bytes 688136 | tf_op jit(solution)/shard_map/while/body/eval_jaxpr/ppermute | solution.py:28
  79.5 8.7 %collective-permute-start.1 = (f32[1,2,14,2048]{3,2,1,0:T(8,128)S(1)}, f32[1,2,14,2048]{3,2,1,0:T(8,128)}, u32[]{:S(2)}, u32[]{:S(2)}) collective-permute-start(f32[1,2,14,2048]{3,2,1,0:T(8,128)S(1)} %get-tuple-element.1061), channel_id=1, source_target_pairs={{0,1},{1,2},{2,3},{3,4},{4,5},{5,6},{6,7},{8,9},{9,10},{10,11},{11... | collective-permute-start | bytes 688136 | tf_op jit(solution)/shard_map/while/body/eval_jaxpr/ppermute | solution.py:27
  97.4 8.7 %collective-permute-start.6 = (f32[1,2,14,2048]{3,2,1,0:T(8,128)S(1)}, f32[1,2,14,2048]{3,2,1,0:T(8,128)S(1)}, u32[]{:S(2)}, u32[]{:S(2)}) collective-permute-start(f32[1,2,14,2048]{3,2,1,0:T(8,128)S(1)} %get-tuple-element.941), channel_id=1, source_target_pairs={{0,1},{1,2},{2,3},{3,4},{4,5},{5,6},{6,7},{8,9},{9,10},{10,11},{11... | collective-permute-start | bytes 688136 | tf_op jit(solution)/shard_map/ppermute | solution.py:27
  102.7 7.7 %collective-permute-start.7 = (f32[1,2,14,2048]{3,2,1,0:T(8,128)S(1)}, f32[1,2,14,2048]{3,2,1,0:T(8,128)S(1)}, u32[]{:S(2)}, u32[]{:S(2)}) collective-permute-start(f32[1,2,14,2048]{3,2,1,0:T(8,128)S(1)} %get-tuple-element.942), channel_id=1, source_target_pairs={{1,0},{2,1},{3,2},{4,3},{5,4},{6,5},{7,6},{9,8},{10,9},{11,10},{12... | collective-permute-start | bytes 688136 | tf_op jit(solution)/shard_map/ppermute | solution.py:28
  112.0 7.7 %collective-permute-start.3 = (f32[1,2,14,2048]{3,2,1,0:T(8,128)S(1)}, f32[1,2,14,2048]{3,2,1,0:T(8,128)S(1)}, u32[]{:S(2)}, u32[]{:S(2)}) collective-permute-start(f32[1,2,14,2048]{3,2,1,0:T(8,128)S(1)} %get-tuple-element.1071), channel_id=1, source_target_pairs={{1,0},{2,1},{3,2},{4,3},{5,4},{6,5},{7,6},{9,8},{10,9},{11,10},{12... | collective-permute-start | bytes 688136 | tf_op jit(solution)/shard_map/while/body/eval_jaxpr/ppermute | solution.py:28
  121.5 12.7 %collective-permute-start.5 = (f32[1,2,16,2048]{3,2,1,0:T(8,128)S(1)}, f32[1,2,16,2048]{3,2,1,0:T(8,128)S(1)}, u32[]{:S(2)}, u32[]{:S(2)}) collective-permute-start(f32[1,2,16,2048]{3,2,1,0:T(8,128)S(1)} %pad_maximum_fusion.21), channel_id=1, source_target_pairs={{8,0},{16,8},{24,16},{9,1},{17,9},{25,17},{10,2},{18,10},{26,18},{... | collective-permute-start | bytes 786440 | tf_op jit(solution)/shard_map/while/body/eval_jaxpr/ppermute | solution.py:36
  134.3 9.5 %collective-permute-start.3 = (f32[1,2,14,2048]{3,2,1,0:T(8,128)S(1)}, f32[1,2,14,2048]{3,2,1,0:T(8,128)S(1)}, u32[]{:S(2)}, u32[]{:S(2)}) collective-permute-start(f32[1,2,14,2048]{3,2,1,0:T(8,128)S(1)} %get-tuple-element.1071), channel_id=1, source_target_pairs={{1,0},{2,1},{3,2},{4,3},{5,4},{6,5},{7,6},{9,8},{10,9},{11,10},{12... | collective-permute-start | bytes 688136 | tf_op jit(solution)/shard_map/while/body/eval_jaxpr/ppermute | solution.py:28
  136.2 8.7 %collective-permute-start.4 = (f32[1,2,14,2048]{3,2,1,0:T(8,128)S(1)}, f32[1,2,14,2048]{3,2,1,0:T(8,128)S(1)}, u32[]{:S(2)}, u32[]{:S(2)}) collective-permute-start(f32[1,2,14,2048]{3,2,1,0:T(8,128)S(1)} %get-tuple-element.1072), channel_id=1, source_target_pairs={{0,1},{1,2},{2,3},{3,4},{4,5},{5,6},{6,7},{8,9},{9,10},{10,11},{11... | collective-permute-start | bytes 688136 | tf_op jit(solution)/shard_map/while/body/eval_jaxpr/ppermute | solution.py:27
  145.6 8.8 %collective-permute-start.5 = (f32[1,2,16,2048]{3,2,1,0:T(8,128)S(1)}, f32[1,2,16,2048]{3,2,1,0:T(8,128)S(1)}, u32[]{:S(2)}, u32[]{:S(2)}) collective-permute-start(f32[1,2,16,2048]{3,2,1,0:T(8,128)S(1)} %pad_maximum_fusion.21), channel_id=1, source_target_pairs={{8,0},{16,8},{24,16},{9,1},{17,9},{25,17},{10,2},{18,10},{26,18},{... | collective-permute-start | bytes 786440 | tf_op jit(solution)/shard_map/while/body/eval_jaxpr/ppermute | solution.py:36
  154.5 9.5 %collective-permute-start.3 = (f32[1,2,14,2048]{3,2,1,0:T(8,128)S(1)}, f32[1,2,14,2048]{3,2,1,0:T(8,128)S(1)}, u32[]{:S(2)}, u32[]{:S(2)}) collective-permute-start(f32[1,2,14,2048]{3,2,1,0:T(8,128)S(1)} %get-tuple-element.1071), channel_id=1, source_target_pairs={{1,0},{2,1},{3,2},{4,3},{5,4},{6,5},{7,6},{9,8},{10,9},{11,10},{12... | collective-permute-start | bytes 688136 | tf_op jit(solution)/shard_map/while/body/eval_jaxpr/ppermute | solution.py:28
  156.4 8.7 %collective-permute-start.4 = (f32[1,2,14,2048]{3,2,1,0:T(8,128)S(1)}, f32[1,2,14,2048]{3,2,1,0:T(8,128)S(1)}, u32[]{:S(2)}, u32[]{:S(2)}) collective-permute-start(f32[1,2,14,2048]{3,2,1,0:T(8,128)S(1)} %get-tuple-element.1072), channel_id=1, source_target_pairs={{0,1},{1,2},{2,3},{3,4},{4,5},{5,6},{6,7},{8,9},{9,10},{10,11},{11... | collective-permute-start | bytes 688136 | tf_op jit(solution)/shard_map/while/body/eval_jaxpr/ppermute | solution.py:27
  165.8 23.1 %collective-permute-start.5 = (f32[1,2,16,2048]{3,2,1,0:T(8,128)S(1)}, f32[1,2,16,2048]{3,2,1,0:T(8,128)S(1)}, u32[]{:S(2)}, u32[]{:S(2)}) collective-permute-start(f32[1,2,16,2048]{3,2,1,0:T(8,128)S(1)} %pad_maximum_fusion.21), channel_id=1, source_target_pairs={{8,0},{16,8},{24,16},{9,1},{17,9},{25,17},{10,2},{18,10},{26,18},{... | collective-permute-start | bytes 786440 | tf_op jit(solution)/shard_map/while/body/eval_jaxpr/ppermute | solution.py:36
  192.8 9.5 %collective-permute-start.3 = (f32[1,2,14,2048]{3,2,1,0:T(8,128)S(1)}, f32[1,2,14,2048]{3,2,1,0:T(8,128)S(1)}, u32[]{:S(2)}, u32[]{:S(2)}) collective-permute-start(f32[1,2,14,2048]{3,2,1,0:T(8,128)S(1)} %get-tuple-element.1071), channel_id=1, source_target_pairs={{1,0},{2,1},{3,2},{4,3},{5,4},{6,5},{7,6},{9,8},{10,9},{11,10},{12... | collective-permute-start | bytes 688136 | tf_op jit(solution)/shard_map/while/body/eval_jaxpr/ppermute | solution.py:28
  194.8 8.7 %collective-permute-start.4 = (f32[1,2,14,2048]{3,2,1,0:T(8,128)S(1)}, f32[1,2,14,2048]{3,2,1,0:T(8,128)S(1)}, u32[]{:S(2)}, u32[]{:S(2)}) collective-permute-start(f32[1,2,14,2048]{3,2,1,0:T(8,128)S(1)} %get-tuple-element.1072), channel_id=1, source_target_pairs={{0,1},{1,2},{2,3},{3,4},{4,5},{5,6},{6,7},{8,9},{9,10},{10,11},{11... | collective-permute-start | bytes 688136 | tf_op jit(solution)/shard_map/while/body/eval_jaxpr/ppermute | solution.py:27
  205.6 8.1 %collective-permute-start.5 = (f32[1,2,16,2048]{3,2,1,0:T(8,128)S(1)}, f32[1,2,16,2048]{3,2,1,0:T(8,128)S(1)}, u32[]{:S(2)}, u32[]{:S(2)}) collective-permute-start(f32[1,2,16,2048]{3,2,1,0:T(8,128)S(1)} %pad_maximum_fusion.21), channel_id=1, source_target_pairs={{8,0},{16,8},{24,16},{9,1},{17,9},{25,17},{10,2},{18,10},{26,18},{... | collective-permute-start | bytes 786440 | tf_op jit(solution)/shard_map/while/body/eval_jaxpr/ppermute | solution.py:36
  216.7 8.7 %collective-permute-start.8 = (f32[1,2,14,2048]{3,2,1,0:T(8,128)S(1)}, f32[1,2,14,2048]{3,2,1,0:T(8,128)S(1)}, u32[]{:S(2)}, u32[]{:S(2)}) collective-permute-start(f32[1,2,14,2048]{3,2,1,0:T(8,128)S(1)} %get-tuple-element.939), channel_id=1, source_target_pairs={{0,1},{1,2},{2,3},{3,4},{4,5},{5,6},{6,7},{8,9},{9,10},{10,11},{11... | collective-permute-start | bytes 688136 | tf_op jit(solution)/shard_map/ppermute | solution.py:27
  222.2 7.7 %collective-permute-start.9 = (f32[1,2,14,2048]{3,2,1,0:T(8,128)S(1)}, f32[1,2,14,2048]{3,2,1,0:T(8,128)S(1)}, u32[]{:S(2)}, u32[]{:S(2)}) collective-permute-start(f32[1,2,14,2048]{3,2,1,0:T(8,128)S(1)} %get-tuple-element.940), channel_id=1, source_target_pairs={{1,0},{2,1},{3,2},{4,3},{5,4},{6,5},{7,6},{9,8},{10,9},{11,10},{12... | collective-permute-start | bytes 688136 | tf_op jit(solution)/shard_map/ppermute | solution.py:28
  (19 other events, 77.6 us)
where the time goes:
time: 233 us; the launch traced here: 232 us
  starting transfers between devices  96.9 us (42%)
  waiting for transfers between devices  93.1 us (40%)
  matrix products  16.8 us (7%)
  other arithmetic  16.5 us (7%)
  local copies, waits for them, and re-layouts  6.01 us (3%)
    ppermute x8, waiting for transfers between devices, from_behind(): return lax.ppermute(shard, axis, pairs)  60 us
    ppermute x10, starting transfers between devices, padded_2(): before = lax.ppermute(last, axis, up)  53.1 us
    ppermute x8, starting transfers between devices, from_behind(): return lax.ppermute(shard, axis, pairs)  24.5 us
    ppermute x10, waiting for transfers between devices, padded_2(): after = lax.ppermute(initial, axis, down)  22.3 us
    ppermute x10, starting transfers between devices, padded_2(): after = lax.ppermute(initial, axis, down)  19.3 us
    dot_general x16, matrix products, product(): jnp.einsum('mrbj,ji->mrbi', operand, matrix, precision=lax.Precision.HIGH...  11.3 us
    ppermute x10, waiting for transfers between devices, padded_2(): before = lax.ppermute(last, axis, up)  10.8 us
    dot_general x16, matrix products, product(): jnp.einsum('ij,mjc->mic', matrix, operand, precision=lax.Precision.HIGHEST)  5.44 us
  transfers between devices with their start and end apart: 28, of which 27 were waited for; matrix products, arithmetic and copies ran while one was open for 2% of the time, Pallas kernels for 0%

commit v1 on v0

--- a/solution.py
+++ b/solution.py
@@ -1,8 +1,12 @@
+import functools
 import math
 
 import jax
 import jax.numpy as jnp
+import numpy as np
 from jax import lax
+from jax.experimental import pallas as pl
+from jax.experimental.pallas import tpu as pltpu
 from jax.sharding import PartitionSpec as P
 
 TILTS = 16
@@ -233,7 +237,292 @@
     return gradient
 
 
+def taps_of(radius, chirp_rate):
+    distance = np.arange(-radius, radius + 1, dtype=np.float64)
+    phase_arg = chirp_rate / radius * distance * distance
+    weight = 1.0 / math.sqrt(2 * radius + 1)
+    return (np.cos(phase_arg) * weight, np.sin(phase_arg) * weight)
+
+
+def split_constant(matrix):
+    high = matrix.astype(jnp.bfloat16)
+    low = (matrix - high.astype(np.float64)).astype(jnp.bfloat16)
+    return (high, low)
+
+
+def column_weights(conjugate):
+    taps = taps_of(HALFCOL, CHIRP_COL)
+    source = np.arange(COLBLK + 2 * HALFCOL)[:, None]
+    target = np.arange(COLBLK)[None, :]
+    place = source - target
+    inside = (place >= 0) & (place <= 2 * HALFCOL)
+    real_part, imag_part = [np.where(inside, t[np.clip(place, 0, 2 * HALFCOL)], 0.0) for t in taps]
+    if conjugate:
+        imag_part = -imag_part
+    from_real = split_constant(np.concatenate([real_part, imag_part], axis=1))
+    from_imag = split_constant(np.concatenate([-imag_part, real_part], axis=1))
+    return np.stack(from_real + from_imag)
+
+
+def series(kind):
+    nodes = np.cos((np.arange(40) + 0.5) * np.pi / 40) * 8.0 + 8.0
+    x = np.sqrt(nodes)
+    values = np.cos(PHASE_SCALE * x) if kind == "cos" else np.sin(PHASE_SCALE * x) / x
+    fitted = np.polynomial.chebyshev.Chebyshev.fit(nodes, values, 6, domain=[0.0, 16.0])
+    return [float(v) for v in fitted.convert(kind=np.polynomial.Polynomial).coef]
+
+
+COS_SERIES = series("cos")
+SIN_SERIES = series("sin")
+
+
+def evaluate(coefficients, x):
+    total = x * coefficients[-1] + coefficients[-2]
+    for value in coefficients[-3::-1]:
+        total = total * x + value
+    return total
+
+
+def split(x):
+    high = x.astype(jnp.bfloat16)
+    return (high, (x - high.astype(jnp.float32)).astype(jnp.bfloat16))
+
+
+def dot(a, b):
+    return jnp.dot(a, b, preferred_element_type=jnp.float32)
+
+
+def row_factor(rows_of, rows_across, offset):
+    n = rows_of.shape[0]
+    distance = jnp.abs(rows_across - rows_of - offset)
+    cosines, sines = taps_of(HALF, CHIRP_ROW)
+    real_part = jnp.zeros((n, n), jnp.float32)
+    imag_part = jnp.zeros((n, n), jnp.float32)
+    for k in range(HALF + 1):
+        hit = distance == k
+        real_part = jnp.where(hit, float(cosines[HALF + k]), real_part)
+        imag_part = jnp.where(hit, float(sines[HALF + k]), imag_part)
+    return (real_part, imag_part)
+
+
+def complex_form(real_part, imag_part):
+    upper = jnp.concatenate([real_part, -imag_part], axis=1)
+    lower = jnp.concatenate([imag_part, real_part], axis=1)
+    return jnp.concatenate([upper, lower], axis=0)
+
+
+def sweep(sizes, where, own, other, measured, forward_cols, adjoint_cols, out, cosine, sine, field, windows, kept):
+    slices, planes, height, blocks, columns = sizes
+    half = planes * height
+    rows = 2 * half
+    across, along, block, plane, core, place = [where[i] for i in range(6)]
+
+    def row_numbers(axis):
+        i = lax.broadcasted_iota(jnp.int32, (rows, rows), axis)
+        side = i // half
+        step = (i - side * half) // height
+        return 2 * height * (plane ^ step) + height * (core ^ side) + i % height
+
+    rows_of, rows_across = row_numbers(0), row_numbers(1)
+    factors = [row_factor(rows_of, rows_across, where[6 + s]) for s in range(slices)]
+    width = blocks * COLBLK
+    first = block * COLBLK - 2 * slices * HALFCOL
+    lane = first + lax.broadcasted_iota(jnp.int32, (1, width), 1)
+    inside = (lane >= 0) & (lane < columns)
+    for s in range(slices):
+        slot = place ^ s
+        for part, source in enumerate((own, other)):
+            x = source[slot].astype(jnp.float32)
+            square = x * x
+            c = jnp.where(inside, evaluate(COS_SERIES, square), 0.0)
+            d = jnp.where(inside, evaluate(SIN_SERIES, square) * x, 0.0)
+            skip = s * HALFCOL
+            used = width - 2 * skip
+            cosine[s, part * half : (part + 1) * half, :used] = c[:, skip : skip + used]
+            sine[s, part * half : (part + 1) * half, :used] = d[:, skip : skip + used]
+
+    turn = 2.0 * math.pi / columns
+    col_phase = turn * (lax.rem(across * lane, columns)).astype(jnp.float32)
+    row_phase = 2.0 * math.pi / rows * (lax.rem(along * row_numbers(0)[:, :1], rows)).astype(jnp.float32)
+    row_cos, row_sin = jnp.cos(row_phase), jnp.sin(row_phase)
+    col_cos, col_sin = jnp.cos(col_phase), jnp.sin(col_phase)
+
+    def to_windows(j, count, high, low):
+        for part, (x, y) in enumerate(((high[0], low[0]), (high[1], low[1]))):
+            if j < count:
+                windows[2 * part, j * rows : (j + 1) * rows, :COLBLK] = x
+                windows[2 * part + 1, j * rows : (j + 1) * rows, :COLBLK] = y
+            if j > 0:
+                windows[2 * part, (j - 1) * rows : j * rows, COLBLK:] = x
+                windows[2 * part + 1, (j - 1) * rows : j * rows, COLBLK:] = y
+
+    def mix_cols(count, weights):
+        n = count * rows
+        total = dot(windows[0, :n], weights[0]) + dot(windows[2, :n], weights[2])
+        total += dot(windows[1, :n], weights[0]) + dot(windows[3, :n], weights[2])
+        total += dot(windows[0, :n], weights[1]) + dot(windows[2, :n], weights[3])
+        field[:n] = total
+
+    def mix_row_block(factor_high, factor_low, x):
+        high, low = split(x)
+        return dot(factor_high, high) + (dot(factor_high, low) + dot(factor_low, high))
+
+    for s in range(slices):
+        high, low = split(complex_form(*factors[s]))
+        n = blocks - s
+        for j in range(n):
+            cols = slice(j * COLBLK, (j + 1) * COLBLK)
+            c, d = cosine[s, :, cols], sine[s, :, cols]
+            if s == 0:
+                cc, cs = col_cos[:, cols], col_sin[:, cols]
+                a = row_cos * cc - row_sin * cs
+                b = row_cos * cs + row_sin * cc
+            else:
+                a = field[j * rows : (j + 1) * rows, :COLBLK]
+                b = field[j * rows : (j + 1) * rows, COLBLK:]
+            y = jnp.concatenate([c * a - d * b, c * b + d * a], axis=0)
+            start = 2 * slices * HALFCOL - s * HALFCOL
+            begin = j * COLBLK
+            if begin < start + COLBLK and begin + COLBLK > start:
+                lo, hi = max(start, begin), min(start + COLBLK, begin + COLBLK)
+                kept[s, :, lo - start : hi - start] = y[:, lo - begin : hi - begin]
+            v = mix_row_block(high, low, y)
+            v_high, v_low = split(v)
+            to_windows(j, n - 1, (v_high[:rows], v_high[rows:]), (v_low[:rows], v_low[rows:]))
+        mix_cols(n - 1, forward_cols)
+
+    n = blocks - slices
+    for j in range(n):
+        a = field[j * rows : (j + 1) * rows, :COLBLK]
+        b = field[j * rows : (j + 1) * rows, COLBLK:]
+        seen = jnp.concatenate(
+            [measured[k, side, :, j * COLBLK : (j + 1) * COLBLK] for side in range(2) for k in range(planes)], axis=0
+        ).astype(jnp.float32)
+        begin = slices * HALFCOL + j * COLBLK
+        error = 2.0 * (a * a + b * b - seen)
+        error = jnp.where(inside[:, begin : begin + COLBLK], error, 0.0)
+        a_high, a_low = split(error * a)
+        b_high, b_low = split(error * b)
+        to_windows(j, n - 1, (a_high, b_high), (a_low, b_low))
+
+    for s in reversed(range(slices)):
+        n -= 1
+        mix_cols(n, adjoint_cols)
+        real_part, imag_part = factors[s]
+        high, low = split(complex_form(real_part.T, -imag_part.T))
+        for j in range(n):
+            a = field[j * rows : (j + 1) * rows, :COLBLK]
+            b = field[j * rows : (j + 1) * rows, COLBLK:]
+            v = mix_row_block(high, low, jnp.concatenate([a, b], axis=0))
+            a, b = v[:rows], v[rows:]
+            begin = s * HALFCOL - j * COLBLK
+            if -COLBLK < begin < COLBLK:
+                lo, hi = max(begin, 0), min(begin + COLBLK, COLBLK)
+                y = kept[s, :, lo - begin : hi - begin]
+                part = PHASE_SCALE * (y[:rows] * b[:, lo:hi] - y[rows:] * a[:, lo:hi])
+                out[place ^ s, :, lo - begin : hi - begin] = part
+            if s > 0:
+                shift = (2 * slices * HALFCOL - s * HALFCOL) - s * HALFCOL + j * COLBLK
+                c = cosine[s, :, shift : shift + COLBLK]
+                d = sine[s, :, shift : shift + COLBLK]
+                a_high, a_low = split(c * a + d * b)
+                b_high, b_low = split(c * b - d * a)
+                to_windows(j, n - 1, (a_high, b_high), (a_low, b_low))
+
+
+def swap(x, axis, step):
+    size = lax.axis_size(axis)
+    return lax.ppermute(x, axis, [(i, i ^ step) for i in range(size)])
+
+
+def window_body(index_volume, angles, offsets, measured):
+    slices = lax.axis_size("depth")
+    planes = lax.axis_size("row") // 2
+    place = lax.axis_index("depth")
+    core = lax.axis_index("row") % 2
+    plane = lax.axis_index("row") // 2
+    height, columns = index_volume.shape[1:]
+    rows = 2 * planes * height
+    span = slices * COLBLK
+    cone = 2 * slices * HALFCOL
+    blocks = 1 + 2 * cone // COLBLK
+
+    padded = jnp.pad(index_volume[0], ((0, 0), (cone, cone)))
+    pieces = [lax.dynamic_slice_in_dim(padded, span * (plane ^ k), span + 2 * cone, 1) for k in range(planes)]
+    pieces = [pieces[0]] + [swap(pieces[k], "row", 2 * k) for k in range(1, planes)]
+    own_slice = jnp.stack(pieces)
+    parts = [lax.dynamic_slice_in_dim(own_slice, COLBLK * (place ^ j), blocks * COLBLK, 2) for j in range(slices)]
+    parts = [parts[0]] + [swap(parts[j], "depth", j) for j in range(1, slices)]
+    own = jnp.stack(parts).reshape(slices, planes * height, blocks * COLBLK)
+    other = swap(own, "row", 1)
+
+    all_offsets = jnp.stack([offsets[0]] + [swap(offsets, "depth", j)[0] for j in range(1, slices)])
+    all_offsets = jnp.stack([all_offsets[place ^ s] for s in range(slices)])
+
+    mine = lax.dynamic_index_in_dim(measured, core, 0, False)
+    theirs = swap(lax.dynamic_index_in_dim(measured, 1 - core, 0, False), "row", 1)
+    both = jnp.pad(jnp.stack([mine, theirs]), ((0, 0), (0, 0), (cone // 2, cone // 2)))
+    seen = [lax.dynamic_slice_in_dim(both, span * (plane ^ k), span + cone, 2) for k in range(planes)]
+    seen = jnp.stack([seen[0]] + [swap(seen[k], "row", 2 * k) for k in range(1, planes)])
+    seen = lax.dynamic_slice_in_dim(seen, COLBLK * place, COLBLK + cone, 3)
+
+    angle = angles[core]
+    across = angle - TILTS // 2
+    along = jnp.mod(3 * angle, TILTS) - TILTS // 2
+    where = jnp.concatenate(
+        [jnp.stack([across, along, plane * slices + place, plane, core, place]), all_offsets]
+    ).astype(jnp.int32)
+
+    width = blocks * COLBLK
+    sizes = (slices, planes, height, blocks, columns)
+    result = pl.pallas_call(
+        functools.partial(sweep, sizes),
+        out_shape=jax.ShapeDtypeStruct((slices, rows, COLBLK), jnp.float32),
+        in_specs=[pl.BlockSpec(memory_space=pltpu.SMEM)] + [pl.BlockSpec(memory_space=pltpu.VMEM)] * 5,
+        out_specs=pl.BlockSpec(memory_space=pltpu.VMEM),
+        scratch_shapes=[
+            pltpu.VMEM((slices, rows, width), jnp.float32),
+            pltpu.VMEM((slices, rows, width), jnp.float32),
+            pltpu.VMEM(((blocks - 1) * rows, 2 * COLBLK), jnp.float32),
+            pltpu.VMEM((4, (blocks - 1) * rows, 2 * COLBLK), jnp.bfloat16),
+            pltpu.VMEM((slices, 2 * rows, COLBLK), jnp.float32),
+        ],
+        compiler_params=pltpu.CompilerParams(vmem_limit_bytes=48 * 1024 * 1024),
+    )(where, own, other, seen, jnp.asarray(column_weights(False)), jnp.asarray(column_weights(True)))
+
+    half = planes * height
+    summed = result[:, :half] + swap(result[:, half:], "row", 1)
+    parts = jnp.stack([summed[0]] + [swap(summed[j], "depth", j) for j in range(1, slices)])
+    parts = parts.reshape(slices, planes, height, COLBLK)
+    parts = jnp.stack([parts[place ^ j] for j in range(slices)])
+    parts = parts.transpose(1, 2, 0, 3).reshape(planes, height, span)
+    parts = jnp.stack([parts[0]] + [swap(parts[k], "row", 2 * k) for k in range(1, planes)])
+    parts = jnp.stack([parts[plane ^ k] for k in range(planes)])
+    return parts.transpose(1, 0, 2).reshape(1, height, columns)
+
+
+def suits(mesh, index_volume, measured):
+    depth, row = mesh.shape["depth"], mesh.shape["row"]
+    slices, rows, columns = index_volume.shape
+    return (
+        slices == depth
+        and depth & (depth - 1) == 0
+        and row & (row - 1) == 0
+        and row > 1
+        and measured.shape[0] == 2
+        and rows == COLBLK
+        and rows // row % 16 == 0
+        and columns == COLBLK * depth * (row // 2)
+    )
+
+
 def solution(mesh):
     in_specs = (P("depth", "row", None), P(), P("depth"), P(None, "row", None))
     out_specs = P("depth", "row", None)
-    return jax.shard_map(body, mesh=mesh, in_specs=in_specs, out_specs=out_specs, check_vma=False)
+
+    def run(index_volume, angles, offsets, measured):
+        chosen = window_body if suits(mesh, index_volume, measured) else body
+        mapped = jax.shard_map(chosen, mesh=mesh, in_specs=in_specs, out_specs=out_specs, check_vma=False)
+        return mapped(index_volume, angles, offsets, measured)
+
+    return run

time: 233 us -> 69.3 us (0.30)
  the two profiles are of different devices: /device:TPU:1 before, /device:TPU:0 now
where the time goes in v1:
time: 69.3 us; the launch traced here: 69 us
  starting transfers between devices  26.9 us (39%)
  Pallas kernels  17.3 us (25%)
  waiting for transfers between devices  13.2 us (19%)
  local copies, waits for them, and re-layouts  6.69 us (10%)
  other arithmetic  2.57 us (4%)
  between operations  2.41 us (3%)
    ppermute x21, starting transfers between devices, swap(): return lax.ppermute(x, axis, [(i, i ^ step) for i in range(size)])  26.9 us
    pallas_call x1, Pallas kernels, window_body(): pl.pallas_call(functools.partial(sweep, sizes), out_shape=jax.ShapeDtypeS...  17.3 us
    ppermute x21, waiting for transfers between devices, swap(): return lax.ppermute(x, axis, [(i, i ^ step) for i in range(size)])  13.2 us
    concatenate x1, local copies, waits for them, and re-layouts, window_body(): jnp.concatenate([jnp.stack([across, along, plane * slices + place, plane,...  2.52 us
    another operation x1, other arithmetic, window_body(): jnp.stack([offsets[0]] + [swap(offsets, 'depth', j)[0] for j in range(1,...  1.88 us
    unnamed x13, local copies, waits for them, and re-layouts  1.52 us
  transfers between devices with their start and end apart: 21, of which 9 were waited for; matrix products, arithmetic and copies ran while one was open for 9% of the time, Pallas kernels for 0%

profile of v1, /device:TPU:0, one launch (start us, length us, event | category | flops | bytes accessed | tf_op | source)
XLA Modules:
  0.0 69.0 jit_solution(14675552777722912275)
XLA Ops:
  0.0 0.8 %copy-done.3 = bf16[1,16,2048]{2,1,0:T(8,128)(2,1)S(1)} copy-done((bf16[1,16,2048]{2,1,0:T(8,128)(2,1)S(1)}, bf16[1,16,2048]{2,1,0:T(8,128)(2,1)}, u32[]{:S(2)}) %copy-start.3) | copy-done | bytes 65560
  1.0 3.1 %collective-permute-start.3 = (bf16[16,1536]{1,0:T(8,128)(2,1)S(1)}, bf16[16,1536]{1,0:T(8,128)(2,1)S(1)}, u32[]{:S(2)}, u32[]{:S(2)}) collective-permute-start(bf16[16,1536]{1,0:T(8,128)(2,1)S(1)} %get-tuple-element.32), channel_id=1, source_target_pairs={{0,2},{1,3},{2,0},{3,1},{4,6},{5,7},{6,4},{7,5},{8,10},{9,11},{10,... | collective-permute-start | bytes 147464 | tf_op jit(solution)/shard_map/ppermute | solution.py:435
  4.1 2.6 %collective-permute-start.4 = (bf16[16,1536]{1,0:T(8,128)(2,1)S(1)}, bf16[16,1536]{1,0:T(8,128)(2,1)S(1)}, u32[]{:S(2)}, u32[]{:S(2)}) collective-permute-start(bf16[16,1536]{1,0:T(8,128)(2,1)S(1)} %get-tuple-element.33), channel_id=1, source_target_pairs={{0,4},{1,5},{2,6},{3,7},{4,0},{5,1},{6,2},{7,3},{8,12},{9,13},{10,... | collective-permute-start | bytes 147464 | tf_op jit(solution)/shard_map/ppermute | solution.py:435
  6.7 1.7 %collective-permute-start.1 = (s32[1]{0:T(128)}, s32[1]{0:T(128)}, u32[]{:S(2)}, u32[]{:S(2)}) collective-permute-start(s32[1]{0:T(128)} %param.8), channel_id=1, source_target_pairs={{0,16},{8,24},{16,0},{24,8},{1,17},{9,25},{17,1},{25,9},{2,18},{10... | collective-permute-start | bytes 20 | tf_op jit(solution)/shard_map/ppermute | solution.py:435
  8.4 1.5 %collective-permute-start = (s32[1]{0:T(128)}, s32[1]{0:T(128)}, u32[]{:S(2)}, u32[]{:S(2)}) collective-permute-start(s32[1]{0:T(128)} %param.8), channel_id=1, source_target_pairs={{0,8},{8,0},{16,24},{24,16},{1,9},{9,1},{17,25},{25,17},{2,10},{10... | collective-permute-start | bytes 20 | tf_op jit(solution)/shard_map/ppermute | solution.py:435
  13.5 1.7 %collective-permute-start.8 = (bf16[4,16,1152]{2,1,0:T(8,128)(2,1)S(1)}, bf16[4,16,1152]{2,1,0:T(8,128)(2,1)S(1)}, u32[]{:S(2)}, u32[]{:S(2)}) collective-permute-start(bf16[4,16,1152]{2,1,0:T(8,128)(2,1)S(1)} %get-tuple-element.6), channel_id=1, source_target_pairs={{0,24},{8,16},{16,8},{24,0},{1,25},{9,17},{17,9},{25,1},{2,26},{10... | collective-permute-start | bytes 442376 | tf_op jit(solution)/shard_map/ppermute | solution.py:435
  15.7 1.4 %collective-permute-start.6 = (bf16[4,16,1152]{2,1,0:T(8,128)(2,1)S(1)}, bf16[4,16,1152]{2,1,0:T(8,128)(2,1)S(1)}, u32[]{:S(2)}, u32[]{:S(2)}) collective-permute-start(bf16[4,16,1152]{2,1,0:T(8,128)(2,1)S(1)} %get-tuple-element.8), channel_id=1, source_target_pairs={{0,8},{8,0},{16,24},{24,16},{1,9},{9,1},{17,25},{25,17},{2,10},{10... | collective-permute-start | bytes 442376 | tf_op jit(solution)/shard_map/ppermute | solution.py:435
  17.1 3.3 %collective-permute-done.8 = bf16[4,16,1152]{2,1,0:T(8,128)(2,1)S(1)} collective-permute-done((bf16[4,16,1152]{2,1,0:T(8,128)(2,1)S(1)}, bf16[4,16,1152]{2,1,0:T(8,128)(2,1)S(1)}, u32[]{:S(2)}, u32[]{:S(2)}) %collective-permute-start.8) | collective-permute-done | bytes 147488 | tf_op jit(solution)/shard_map/ppermute | solution.py:435
  20.4 1.4 %collective-permute-start.2 = (s32[1]{0:T(128)}, s32[1]{0:T(128)}, u32[]{:S(2)}, u32[]{:S(2)}) collective-permute-start(s32[1]{0:T(128)} %param.8), channel_id=1, source_target_pairs={{0,24},{8,16},{16,8},{24,0},{1,25},{9,17},{17,9},{25,1},{2,26},{10... | collective-permute-start | bytes 20 | tf_op jit(solution)/shard_map/ppermute | solution.py:435
  23.2 3.5 %collective-permute-start.13 = (bf16[2,16,1024]{2,1,0:T(8,128)(2,1)S(1)}, bf16[2,16,1024]{2,1,0:T(8,128)(2,1)S(1)}, u32[]{:S(2)}, u32[]{:S(2)}) collective-permute-start(bf16[2,16,1024]{2,1,0:T(8,128)(2,1)S(1)} %get-tuple-element.9), channel_id=1, source_target_pairs={{0,6},{1,7},{2,4},{3,5},{4,2},{5,3},{6,0},{7,1},{8,14},{9,15},{10,... | collective-permute-start | bytes 196616 | tf_op jit(solution)/shard_map/ppermute | solution.py:435
  26.7 1.0 %collective-permute-start.11 = (bf16[2,16,1024]{2,1,0:T(8,128)(2,1)S(1)}, bf16[2,16,1024]{2,1,0:T(8,128)(2,1)S(1)}, u32[]{:S(2)}, u32[]{:S(2)}) collective-permute-start(bf16[2,16,1024]{2,1,0:T(8,128)(2,1)S(1)} %get-tuple-element.11), channel_id=1, source_target_pairs={{0,2},{1,3},{2,0},{3,1},{4,6},{5,7},{6,4},{7,5},{8,10},{9,11},{10,... | collective-permute-start | bytes 196616 | tf_op jit(solution)/shard_map/ppermute | solution.py:435
  27.7 1.9 %pad_add_fusion = s32[4]{0:T(128)S(1)} fusion(s32[1]{0:T(128)} %collective-permute-done.2, s32[1]{0:T(128)} %collective-permute-done.1, s32[1]{0:T(128)} %collective-permute-done, s32[1]{0:T(128)S(6)} %copy.20), kind=kLoop, calls=%fused_computation.49 | loop fusion | flops 12 | bytes 32 | tf_op jit(solution)/shard_map/stack | solution.py:459
  29.5 0.6 fusion.10
  30.2 2.5 %concatenate.5.where = s32[10]{0:T(128)S(1)} concatenate(s32[1]{0:T(128)S(6)} %sub.13, s32[1]{0:T(128)} %bitcast.1, s32[1]{0:T(128)} %bitcast.2, s32[1]{0:T(128)} %bitcast.3, s32[1]{0:T(128)} %bitcast.4, s32[1]{0:T(128)} %bitcast.5, s32[1]{0:T(128)} %get-tuple-element.38, s32[1]{0:T(128)} %get-tuple-element.37, s32[1]{0:T(128)} %get-tuple-element.36, s32[1]{0:T(128)} %get-tuple-element.35), dimensions={0} | concatenate | bytes 80 | tf_op jit(solution)/shard_map/concatenate | solution.py:472
  32.8 17.3 %shard_map.64 = f32[4,128,128]{2,1,0:T(8,128)S(1)} custom-call(s32[10]{0:T(128)S(1)} %concatenate.5.where, bf16[4,64,1152]{2,1,0:T(8,128)(2,1)S(1)} %pad_maximum_fusion.own, bf16[4,64,1152]{2,1,0:T(8,128)(2,1)S(1)} %collective-permute-done.9.other, bf16[4,2,16,640]{3,2,1,0:T(8,128)(2,1)S(1)} %fusion.6.measured, bf16[4,256,256]{2,1,0:T(8,128)(2,1)S(1)} %copy-done.1, ...), custom_call_target="tpu_custom_call" | custom-call | tf_op jit(solution)/shard_map/pallas_call | solution.py:478
  50.2 1.3 %collective-permute-done.14 = f32[4,64,128]{2,1,0:T(8,128)S(1)} collective-permute-done((f32[4,64,128]{2,1,0:T(8,128)S(1)}, f32[4,64,128]{2,1,0:T(8,128)S(1)}, u32[]{:S(2)}, u32[]{:S(2)}) %collective-permute-start.14) | collective-permute-done | bytes 131104 | tf_op jit(solution)/shard_map/ppermute | solution.py:435
  51.5 1.5 %collective-permute-start.17 = (f32[64,128]{1,0:T(8,128)S(1)}, f32[64,128]{1,0:T(8,128)S(1)}, u32[]{:S(2)}, u32[]{:S(2)}) collective-permute-start(f32[64,128]{1,0:T(8,128)S(1)} %get-tuple-element.26), channel_id=1, source_target_pairs={{0,24},{8,16},{16,8},{24,0},{1,25},{9,17},{17,9},{25,1},{2,26},{10... | collective-permute-start | bytes 98312 | tf_op jit(solution)/shard_map/ppermute | solution.py:435
  53.6 1.5 %collective-permute-start.15 = (f32[64,128]{1,0:T(8,128)S(1)}, f32[64,128]{1,0:T(8,128)S(1)}, u32[]{:S(2)}, u32[]{:S(2)}) collective-permute-start(f32[64,128]{1,0:T(8,128)S(1)} %get-tuple-element.28), channel_id=1, source_target_pairs={{0,8},{8,0},{16,24},{24,16},{1,9},{9,1},{17,25},{25,17},{2,10},{10... | collective-permute-start | bytes 98312 | tf_op jit(solution)/shard_map/ppermute | solution.py:435
  55.1 1.3 %collective-permute-done.17 = f32[64,128]{1,0:T(8,128)S(1)} collective-permute-done((f32[64,128]{1,0:T(8,128)S(1)}, f32[64,128]{1,0:T(8,128)S(1)}, u32[]{:S(2)}, u32[]{:S(2)}) %collective-permute-start.17) | collective-permute-done | bytes 32800 | tf_op jit(solution)/shard_map/ppermute | solution.py:435
  58.0 1.3 %collective-permute-start.18 = (f32[16,512]{1,0:T(8,128)S(1)}, f32[16,512]{1,0:T(8,128)S(1)}, u32[]{:S(2)}, u32[]{:S(2)}) collective-permute-start(f32[16,512]{1,0:T(8,128)S(1)} %bitcast.81), channel_id=1, source_target_pairs={{0,2},{1,3},{2,0},{3,1},{4,6},{5,7},{6,4},{7,5},{8,10},{9,11},{10,... | collective-permute-start | bytes 98312 | tf_op jit(solution)/shard_map/ppermute | solution.py:435
  59.3 2.8 %collective-permute-start.19 = (f32[16,512]{1,0:T(8,128)S(1)}, f32[16,512]{1,0:T(8,128)S(1)}, u32[]{:S(2)}, u32[]{:S(2)}) collective-permute-start(f32[16,512]{1,0:T(8,128)S(1)} %bitcast.80), channel_id=1, source_target_pairs={{0,4},{1,5},{2,6},{3,7},{4,0},{5,1},{6,2},{7,3},{8,12},{9,13},{10,... | collective-permute-start | bytes 98312 | tf_op jit(solution)/shard_map/ppermute | solution.py:435
  62.5 2.0 %collective-permute-done.19 = f32[16,512]{1,0:T(8,128)S(1)} collective-permute-done((f32[16,512]{1,0:T(8,128)S(1)}, f32[16,512]{1,0:T(8,128)S(1)}, u32[]{:S(2)}, u32[]{:S(2)}) %collective-permute-start.19) | collective-permute-done | bytes 32800 | tf_op jit(solution)/shard_map/ppermute | solution.py:435
  64.5 3.4 %collective-permute-done.20 = f32[16,512]{1,0:T(8,128)S(1)} collective-permute-done((f32[16,512]{1,0:T(8,128)S(1)}, f32[16,512]{1,0:T(8,128)S(1)}, u32[]{:S(2)}, u32[]{:S(2)}) %collective-permute-start.20) | collective-permute-done | bytes 32800 | tf_op jit(solution)/shard_map/ppermute | solution.py:435
  68.3 0.7 %reshape.33 = f32[1,16,2048]{2,1,0:T(8,128)} reshape(f32[16,4,512]{2,1,0:T(4,128)S(1)} %maximum_bitcast_fusion.1) | data formatting | bytes 262144 | tf_op jit(solution)/shard_map/reshape | solution.py:501
  (58 shorter events, 6.5 us)
Async XLA Ops:
  1.0 12.4 %collective-permute-start.3 = (bf16[16,1536]{1,0:T(8,128)(2,1)S(1)}, bf16[16,1536]{1,0:T(8,128)(2,1)S(1)}, u32[]{:S(2)}, u32[]{:S(2)}) collective-permute-start(bf16[16,1536]{1,0:T(8,128)(2,1)S(1)} %get-tuple-element.32), channel_id=1, source_target_pairs={{0,2},{1,3},{2,0},{3,1},{4,6},{5,7},{6,4},{7,5},{8,10},{9,11},{10,... | collective-permute-start | bytes 147464 | tf_op jit(solution)/shard_map/ppermute | solution.py:435
  4.1 9.3 %collective-permute-start.4 = (bf16[16,1536]{1,0:T(8,128)(2,1)S(1)}, bf16[16,1536]{1,0:T(8,128)(2,1)S(1)}, u32[]{:S(2)}, u32[]{:S(2)}) collective-permute-start(bf16[16,1536]{1,0:T(8,128)(2,1)S(1)} %get-tuple-element.33), channel_id=1, source_target_pairs={{0,4},{1,5},{2,6},{3,7},{4,0},{5,1},{6,2},{7,3},{8,12},{9,13},{10,... | collective-permute-start | bytes 147464 | tf_op jit(solution)/shard_map/ppermute | solution.py:435
  6.7 6.7 %collective-permute-start.5 = (bf16[16,1536]{1,0:T(8,128)(2,1)S(1)}, bf16[16,1536]{1,0:T(8,128)(2,1)S(1)}, u32[]{:S(2)}, u32[]{:S(2)}) collective-permute-start(bf16[16,1536]{1,0:T(8,128)(2,1)S(1)} %get-tuple-element.34), channel_id=1, source_target_pairs={{0,6},{1,7},{2,4},{3,5},{4,2},{5,3},{6,0},{7,1},{8,14},{9,15},{10,... | collective-permute-start | bytes 147464 | tf_op jit(solution)/shard_map/ppermute | solution.py:435
  6.7 20.0 %collective-permute-start.1 = (s32[1]{0:T(128)}, s32[1]{0:T(128)}, u32[]{:S(2)}, u32[]{:S(2)}) collective-permute-start(s32[1]{0:T(128)} %param.8), channel_id=1, source_target_pairs={{0,16},{8,24},{16,0},{24,8},{1,17},{9,25},{17,1},{25,9},{2,18},{10... | collective-permute-start | bytes 20 | tf_op jit(solution)/shard_map/ppermute | solution.py:435
  8.4 18.3 %collective-permute-start = (s32[1]{0:T(128)}, s32[1]{0:T(128)}, u32[]{:S(2)}, u32[]{:S(2)}) collective-permute-start(s32[1]{0:T(128)} %param.8), channel_id=1, source_target_pairs={{0,8},{8,0},{16,24},{24,16},{1,9},{9,1},{17,25},{25,17},{2,10},{10... | collective-permute-start | bytes 20 | tf_op jit(solution)/shard_map/ppermute | solution.py:435
  13.4 3.6 %copy-start.2 = (bf16[2,16,2048]{2,1,0:T(8,128)(2,1)S(1)}, bf16[2,16,2048]{2,1,0:T(8,128)(2,1)}, u32[]{:S(2)}) copy-start(bf16[2,16,2048]{2,1,0:T(8,128)(2,1)} %param.9) | copy-start | bytes 393220
  13.5 6.9 %collective-permute-start.8 = (bf16[4,16,1152]{2,1,0:T(8,128)(2,1)S(1)}, bf16[4,16,1152]{2,1,0:T(8,128)(2,1)S(1)}, u32[]{:S(2)}, u32[]{:S(2)}) collective-permute-start(bf16[4,16,1152]{2,1,0:T(8,128)(2,1)S(1)} %get-tuple-element.6), channel_id=1, source_target_pairs={{0,24},{8,16},{16,8},{24,0},{1,25},{9,17},{17,9},{25,1},{2,26},{10... | collective-permute-start | bytes 442376 | tf_op jit(solution)/shard_map/ppermute | solution.py:435
  15.2 6.7 %collective-permute-start.7 = (bf16[4,16,1152]{2,1,0:T(8,128)(2,1)S(1)}, bf16[4,16,1152]{2,1,0:T(8,128)(2,1)S(1)}, u32[]{:S(2)}, u32[]{:S(2)}) collective-permute-start(bf16[4,16,1152]{2,1,0:T(8,128)(2,1)S(1)} %get-tuple-element.7), channel_id=1, source_target_pairs={{0,16},{8,24},{16,0},{24,8},{1,17},{9,25},{17,1},{25,9},{2,18},{10... | collective-permute-start | bytes 442376 | tf_op jit(solution)/shard_map/ppermute | solution.py:435
  15.7 6.2 %collective-permute-start.6 = (bf16[4,16,1152]{2,1,0:T(8,128)(2,1)S(1)}, bf16[4,16,1152]{2,1,0:T(8,128)(2,1)S(1)}, u32[]{:S(2)}, u32[]{:S(2)}) collective-permute-start(bf16[4,16,1152]{2,1,0:T(8,128)(2,1)S(1)} %get-tuple-element.8), channel_id=1, source_target_pairs={{0,8},{8,0},{16,24},{24,16},{1,9},{9,1},{17,25},{25,17},{2,10},{10... | collective-permute-start | bytes 442376 | tf_op jit(solution)/shard_map/ppermute | solution.py:435
  20.4 7.3 %collective-permute-start.2 = (s32[1]{0:T(128)}, s32[1]{0:T(128)}, u32[]{:S(2)}, u32[]{:S(2)}) collective-permute-start(s32[1]{0:T(128)} %param.8), channel_id=1, source_target_pairs={{0,24},{8,16},{16,8},{24,0},{1,25},{9,17},{17,9},{25,1},{2,26},{10... | collective-permute-start | bytes 20 | tf_op jit(solution)/shard_map/ppermute | solution.py:435
  21.9 1.3 %collective-permute-start.10 = (bf16[16,2048]{1,0:T(8,128)(2,1)S(1)}, bf16[16,2048]{1,0:T(8,128)(2,1)S(1)}, u32[]{:S(2)}, u32[]{:S(2)}) collective-permute-start(bf16[16,2048]{1,0:T(8,128)(2,1)S(1)} %get-tuple-element.30), channel_id=1, source_target_pairs={{0,1},{1,0},{2,3},{3,2},{4,5},{5,4},{6,7},{7,6},{8,9},{9,8},{10,11... | collective-permute-start | bytes 196616 | tf_op jit(solution)/shard_map/ppermute | solution.py:435
  22.0 10.8 %collective-permute-start.9 = (bf16[4,64,1152]{2,1,0:T(8,128)(2,1)S(1)}, bf16[4,64,1152]{2,1,0:T(8,128)(2,1)S(1)}, u32[]{:S(2)}, u32[]{:S(2)}) collective-permute-start(bf16[4,64,1152]{2,1,0:T(8,128)(2,1)S(1)} %pad_maximum_fusion.own), channel_id=1, source_target_pairs={{0,1},{1,0},{2,3},{3,2},{4,5},{5,4},{6,7},{7,6},{8,9},{9,8},{10,11... | collective-permute-start | bytes 1769480 | tf_op jit(solution)/shard_map/ppermute | solution.py:435
  23.1 9.7 %copy-start.1 = (bf16[4,256,256]{2,1,0:T(8,128)(2,1)S(1)}, bf16[4,256,256]{2,1,0:T(8,128)(2,1)}, u32[]{:S(2)}) copy-start(bf16[4,256,256]{2,1,0:T(8,128)(2,1)} %constant.81.clone.forward_cols) | copy-start | bytes 1572868
  23.1 9.7 %copy-start = (bf16[4,256,256]{2,1,0:T(8,128)(2,1)S(1)}, bf16[4,256,256]{2,1,0:T(8,128)(2,1)}, u32[]{:S(2)}) copy-start(bf16[4,256,256]{2,1,0:T(8,128)(2,1)} %constant.82.clone.adjoint_cols) | copy-start | bytes 1572868
  23.2 9.5 %collective-permute-start.13 = (bf16[2,16,1024]{2,1,0:T(8,128)(2,1)S(1)}, bf16[2,16,1024]{2,1,0:T(8,128)(2,1)S(1)}, u32[]{:S(2)}, u32[]{:S(2)}) collective-permute-start(bf16[2,16,1024]{2,1,0:T(8,128)(2,1)S(1)} %get-tuple-element.9), channel_id=1, source_target_pairs={{0,6},{1,7},{2,4},{3,5},{4,2},{5,3},{6,0},{7,1},{8,14},{9,15},{10,... | collective-permute-start | bytes 196616 | tf_op jit(solution)/shard_map/ppermute | solution.py:435
  26.7 6.0 %collective-permute-start.12 = (bf16[2,16,1024]{2,1,0:T(8,128)(2,1)S(1)}, bf16[2,16,1024]{2,1,0:T(8,128)(2,1)S(1)}, u32[]{:S(2)}, u32[]{:S(2)}) collective-permute-start(bf16[2,16,1024]{2,1,0:T(8,128)(2,1)S(1)} %get-tuple-element.10), channel_id=1, source_target_pairs={{0,4},{1,5},{2,6},{3,7},{4,0},{5,1},{6,2},{7,3},{8,12},{9,13},{10,... | collective-permute-start | bytes 196616 | tf_op jit(solution)/shard_map/ppermute | solution.py:435
  26.7 6.0 %collective-permute-start.11 = (bf16[2,16,1024]{2,1,0:T(8,128)(2,1)S(1)}, bf16[2,16,1024]{2,1,0:T(8,128)(2,1)S(1)}, u32[]{:S(2)}, u32[]{:S(2)}) collective-permute-start(bf16[2,16,1024]{2,1,0:T(8,128)(2,1)S(1)} %get-tuple-element.11), channel_id=1, source_target_pairs={{0,2},{1,3},{2,0},{3,1},{4,6},{5,7},{6,4},{7,5},{8,10},{9,11},{10,... | collective-permute-start | bytes 196616 | tf_op jit(solution)/shard_map/ppermute | solution.py:435
  50.1 1.4 %collective-permute-start.14 = (f32[4,64,128]{2,1,0:T(8,128)S(1)}, f32[4,64,128]{2,1,0:T(8,128)S(1)}, u32[]{:S(2)}, u32[]{:S(2)}) collective-permute-start(f32[4,64,128]{2,1,0:T(8,128)S(1)} %slice.48), channel_id=1, source_target_pairs={{0,1},{1,0},{2,3},{3,2},{4,5},{5,4},{6,7},{7,6},{8,9},{9,8},{10,11... | collective-permute-start | bytes 393224 | tf_op jit(solution)/shard_map/ppermute | solution.py:435
  51.5 4.9 %collective-permute-start.17 = (f32[64,128]{1,0:T(8,128)S(1)}, f32[64,128]{1,0:T(8,128)S(1)}, u32[]{:S(2)}, u32[]{:S(2)}) collective-permute-start(f32[64,128]{1,0:T(8,128)S(1)} %get-tuple-element.26), channel_id=1, source_target_pairs={{0,24},{8,16},{16,8},{24,0},{1,25},{9,17},{17,9},{25,1},{2,26},{10... | collective-permute-start | bytes 98312 | tf_op jit(solution)/shard_map/ppermute | solution.py:435
  53.1 3.9 %collective-permute-start.16 = (f32[64,128]{1,0:T(8,128)S(1)}, f32[64,128]{1,0:T(8,128)S(1)}, u32[]{:S(2)}, u32[]{:S(2)}) collective-permute-start(f32[64,128]{1,0:T(8,128)S(1)} %get-tuple-element.27), channel_id=1, source_target_pairs={{0,16},{8,24},{16,0},{24,8},{1,17},{9,25},{17,1},{25,9},{2,18},{10... | collective-permute-start | bytes 98312 | tf_op jit(solution)/shard_map/ppermute | solution.py:435
  53.6 3.9 %collective-permute-start.15 = (f32[64,128]{1,0:T(8,128)S(1)}, f32[64,128]{1,0:T(8,128)S(1)}, u32[]{:S(2)}, u32[]{:S(2)}) collective-permute-start(f32[64,128]{1,0:T(8,128)S(1)} %get-tuple-element.28), channel_id=1, source_target_pairs={{0,8},{8,0},{16,24},{24,16},{1,9},{9,1},{17,25},{25,17},{2,10},{10... | collective-permute-start | bytes 98312 | tf_op jit(solution)/shard_map/ppermute | solution.py:435
  58.0 4.5 %collective-permute-start.18 = (f32[16,512]{1,0:T(8,128)S(1)}, f32[16,512]{1,0:T(8,128)S(1)}, u32[]{:S(2)}, u32[]{:S(2)}) collective-permute-start(f32[16,512]{1,0:T(8,128)S(1)} %bitcast.81), channel_id=1, source_target_pairs={{0,2},{1,3},{2,0},{3,1},{4,6},{5,7},{6,4},{7,5},{8,10},{9,11},{10,... | collective-permute-start | bytes 98312 | tf_op jit(solution)/shard_map/ppermute | solution.py:435
  59.3 5.2 %collective-permute-start.19 = (f32[16,512]{1,0:T(8,128)S(1)}, f32[16,512]{1,0:T(8,128)S(1)}, u32[]{:S(2)}, u32[]{:S(2)}) collective-permute-start(f32[16,512]{1,0:T(8,128)S(1)} %bitcast.80), channel_id=1, source_target_pairs={{0,4},{1,5},{2,6},{3,7},{4,0},{5,1},{6,2},{7,3},{8,12},{9,13},{10,... | collective-permute-start | bytes 98312 | tf_op jit(solution)/shard_map/ppermute | solution.py:435
  62.1 5.7 %collective-permute-start.20 = (f32[16,512]{1,0:T(8,128)S(1)}, f32[16,512]{1,0:T(8,128)S(1)}, u32[]{:S(2)}, u32[]{:S(2)}) collective-permute-start(f32[16,512]{1,0:T(8,128)S(1)} %bitcast.79), channel_id=1, source_target_pairs={{0,6},{1,7},{2,4},{3,5},{4,2},{5,3},{6,0},{7,1},{8,14},{9,15},{10,... | collective-permute-start | bytes 98312 | tf_op jit(solution)/shard_map/ppermute | solution.py:435
  (2 other events, 1.5 us)

commit v2 on v0

--- a/solution.py
+++ b/solution.py
@@ -1,8 +1,12 @@
+import functools
 import math
 
 import jax
 import jax.numpy as jnp
+import numpy as np
 from jax import lax
+from jax.experimental import pallas as pl
+from jax.experimental.pallas import tpu as pltpu
 from jax.sharding import PartitionSpec as P
 
 TILTS = 16
@@ -233,7 +237,333 @@
     return gradient
 
 
+def taps_of(radius, chirp_rate):
+    distance = np.arange(-radius, radius + 1, dtype=np.float64)
+    phase_arg = chirp_rate / radius * distance * distance
+    weight = 1.0 / math.sqrt(2 * radius + 1)
+    return (np.cos(phase_arg) * weight, np.sin(phase_arg) * weight)
+
+
+def split_constant(matrix):
+    high = matrix.astype(jnp.bfloat16)
+    low = (matrix - high.astype(np.float64)).astype(jnp.bfloat16)
+    return (high, low)
+
+
+def column_weights(conjugate):
+    taps = taps_of(HALFCOL, CHIRP_COL)
+    source = np.arange(COLBLK + 2 * HALFCOL)[:, None]
+    target = np.arange(COLBLK)[None, :]
+    place = source - target
+    inside = (place >= 0) & (place <= 2 * HALFCOL)
+    real_part, imag_part = [np.where(inside, t[np.clip(place, 0, 2 * HALFCOL)], 0.0) for t in taps]
+    if conjugate:
+        imag_part = -imag_part
+    from_real = np.concatenate([real_part, imag_part], axis=1)
+    from_imag = np.concatenate([-imag_part, real_part], axis=1)
+    high, low = split_constant(np.concatenate([from_real, from_imag], axis=0))
+    return np.concatenate([high, high, low], axis=0)
+
+
+def series(kind):
+    nodes = np.cos((np.arange(40) + 0.5) * np.pi / 40) * 8.0 + 8.0
+    x = np.sqrt(nodes)
+    values = np.cos(PHASE_SCALE * x) if kind == "cos" else np.sin(PHASE_SCALE * x) / x
+    fitted = np.polynomial.chebyshev.Chebyshev.fit(nodes, values, 6, domain=[0.0, 16.0])
+    return [float(v) for v in fitted.convert(kind=np.polynomial.Polynomial).coef]
+
+
+COS_SERIES = series("cos")
+SIN_SERIES = series("sin")
+
+
+def evaluate(coefficients, x):
+    total = x * coefficients[-1] + coefficients[-2]
+    for value in coefficients[-3::-1]:
+        total = total * x + value
+    return total
+
+
+def split(x):
+    high = x.astype(jnp.bfloat16)
+    return (high, (x - high.astype(jnp.float32)).astype(jnp.bfloat16))
+
+
+def dot(a, b):
+    return jnp.dot(a, b, preferred_element_type=jnp.float32)
+
+
+def row_factor(rows_of, rows_across, offset):
+    n = rows_of.shape[0]
+    distance = jnp.abs(rows_across - rows_of - offset)
+    cosines, sines = taps_of(HALF, CHIRP_ROW)
+    real_part = jnp.zeros((n, n), jnp.float32)
+    imag_part = jnp.zeros((n, n), jnp.float32)
+    for k in range(HALF + 1):
+        hit = distance == k
+        real_part = jnp.where(hit, float(cosines[HALF + k]), real_part)
+        imag_part = jnp.where(hit, float(sines[HALF + k]), imag_part)
+    return (real_part, imag_part)
+
+
+def complex_form(real_part, imag_part):
+    upper = jnp.concatenate([real_part, -imag_part], axis=1)
+    lower = jnp.concatenate([imag_part, real_part], axis=1)
+    return jnp.concatenate([upper, lower], axis=0)
+
+
+def sweep(sizes, angles, tiles, own, other, measured, forward_cols, adjoint_cols, mine, theirs, cosine, sine, field, kept):
+    slices, planes, height, blocks, columns = sizes
+    half = planes * height
+    rows = 2 * half
+    place = lax.axis_index("depth")
+    core = lax.axis_index("row") % 2
+    plane = lax.axis_index("row") // 2
+    block = plane * slices + place
+    angle = angles[core]
+    across = angle - TILTS // 2
+    along = lax.rem(3 * angle, TILTS) - TILTS // 2
+
+    def row_numbers(axis):
+        i = lax.broadcasted_iota(jnp.int32, (rows, rows), axis)
+        side = i // half
+        step = (i - side * half) // height
+        return 2 * height * (plane ^ step) + height * (core ^ side) + i % height
+
+    rows_of, rows_across = row_numbers(0), row_numbers(1)
+    walk_off = [tiles[place ^ s, :1].astype(jnp.int32) for s in range(slices)]
+    factors = [row_factor(rows_of, rows_across, offset) for offset in walk_off]
+    width = blocks * COLBLK
+    first = block * COLBLK - 2 * slices * HALFCOL
+    lane = first + lax.broadcasted_iota(jnp.int32, (1, width), 1)
+    inside = (lane >= 0) & (lane < columns)
+
+    turn = 2.0 * math.pi / columns
+    col_phase = turn * (lax.rem(across * lane, columns)).astype(jnp.float32)
+    row_phase = 2.0 * math.pi / rows * (lax.rem(along * row_numbers(0)[:, :1], rows)).astype(jnp.float32)
+    row_cos, row_sin = jnp.cos(row_phase), jnp.sin(row_phase)
+    col_cos, col_sin = jnp.cos(col_phase), jnp.sin(col_phase)
+
+    def read(level, j):
+        return (field[level, j, :, :COLBLK], field[level, j, :, COLBLK:])
+
+    def operand(a, b):
+        a_high, a_low = split(a)
+        b_high, b_low = split(b)
+        return (a_high, b_high, a_low, b_low)
+
+    def mix_cols(level, j, left, right, weights):
+        wide = jnp.concatenate([part for pair in zip(left, right) for part in pair], axis=1)
+        total = dot(wide, weights[: 8 * COLBLK]) + dot(wide[:, : 4 * COLBLK], weights[8 * COLBLK :])
+        field[level, j] = total
+
+    def mix_rows(factor, blocks_in):
+        y = jnp.concatenate([jnp.concatenate([a, b], axis=0) for a, b in blocks_in], axis=1)
+        y_high, y_low = split(y)
+        v = dot(factor[0], y_high) + (dot(factor[0], y_low) + dot(factor[1], y_high))
+        cut = [slice(i * COLBLK, (i + 1) * COLBLK) for i in range(len(blocks_in))]
+        return [(v[:rows, c], v[rows:, c]) for c in cut]
+
+    def pairs(n):
+        return [range(j, min(j + 2, n)) for j in range(0, n, 2)]
+
+    def forward(s):
+        factor = split(complex_form(*factors[s]))
+        slot = place ^ s
+        last = None
+        for group in pairs(blocks - s):
+            turned = []
+            for j in group:
+                begin = s * HALFCOL + j * COLBLK
+                x = jnp.concatenate([r[slot, :, begin : begin + COLBLK] for r in (own, other)], axis=0)
+                x = x.astype(jnp.float32)
+                square = x * x
+                seen = inside[:, begin : begin + COLBLK]
+                c = jnp.where(seen, evaluate(COS_SERIES, square), 0.0)
+                d = jnp.where(seen, evaluate(SIN_SERIES, square) * x, 0.0)
+                if s > 0:
+                    cosine[s, :, j * COLBLK : (j + 1) * COLBLK] = c
+                    sine[s, :, j * COLBLK : (j + 1) * COLBLK] = d
+                if s == 0:
+                    cc, cs = col_cos[:, begin : begin + COLBLK], col_sin[:, begin : begin + COLBLK]
+                    a = row_cos * cc - row_sin * cs
+                    b = row_cos * cs + row_sin * cc
+                else:
+                    a, b = read(s - 1, j)
+                a, b = c * a - d * b, c * b + d * a
+                start = (2 * slices - s) * HALFCOL - j * COLBLK
+                lo, hi = max(start, 0), min(start + COLBLK, COLBLK)
+                if lo < hi:
+                    kept[s, :rows, lo - start : hi - start] = a[:, lo:hi]
+                    kept[s, rows:, lo - start : hi - start] = b[:, lo:hi]
+                turned.append((a, b))
+            for j, v in zip(group, mix_rows(factor, turned)):
+                parts = operand(*v)
+                if j > 0:
+                    mix_cols(s, j - 1, last, parts, forward_cols)
+                last = parts
+            yield
+
+    def residual():
+        last = None
+        for group in pairs(blocks - slices):
+            for j in group:
+                a, b = read(slices - 1, j)
+                cols = slice(j * COLBLK, (j + 1) * COLBLK)
+                seen = [measured[k, side, :, cols] for side in range(2) for k in range(planes)]
+                seen = jnp.concatenate(seen, axis=0).astype(jnp.float32)
+                begin = slices * HALFCOL + j * COLBLK
+                error = 2.0 * (a * a + b * b - seen)
+                error = jnp.where(inside[:, begin : begin + COLBLK], error, 0.0)
+                parts = operand(error * a, error * b)
+                if j > 0:
+                    mix_cols(slices, j - 1, last, parts, adjoint_cols)
+                last = parts
+            yield
+
+    def backward(s):
+        real_part, imag_part = factors[s]
+        factor = split(complex_form(real_part.T, -imag_part.T))
+        level = 2 * slices - 1 - s
+        last = None
+        for group in pairs(s + 1):
+            for j, (a, b) in zip(group, mix_rows(factor, [read(level, j) for j in group])):
+                start = s * HALFCOL - j * COLBLK
+                lo, hi = max(start, 0), min(start + COLBLK, COLBLK)
+                if lo < hi:
+                    y = kept[s, :, lo - start : hi - start]
+                    part = PHASE_SCALE * (y[:rows] * b[:, lo:hi] - y[rows:] * a[:, lo:hi])
+                    mine[place ^ s, :, lo - start : hi - start] = part[:half]
+                    theirs[place ^ s, :, lo - start : hi - start] = part[half:]
+                if s > 0:
+                    begin = 2 * (slices - s) * HALFCOL + j * COLBLK
+                    c = cosine[s, :, begin : begin + COLBLK]
+                    d = sine[s, :, begin : begin + COLBLK]
+                    parts = operand(c * a + d * b, c * b - d * a)
+                    if j > 0:
+                        mix_cols(level + 1, j - 1, last, parts, adjoint_cols)
+                    last = parts
+            yield
+
+    stages = [forward(s) for s in range(slices)] + [residual()] + [backward(s) for s in reversed(range(slices))]
+    counts = [blocks - s for s in range(slices)] + [blocks - slices] + [s + 1 for s in reversed(range(slices))]
+    order = [(2 * k + t, k) for k, n in enumerate(counts) for t in range(len(pairs(n)))]
+    for _, k in sorted(order):
+        next(stages[k])
+
+
+def arrange(sizes, *refs):
+    slices, planes = sizes[:2]
+    place = lax.axis_index("depth")
+    plane = lax.axis_index("row") // 2
+    out = refs[-1]
+    for k in range(planes):
+        for j in range(slices):
+            block = (plane ^ k) * slices + (place ^ j)
+            out[0, :, pl.ds(pl.multiple_of(block * COLBLK, COLBLK), COLBLK)] = refs[k][j]
+
+
+def swap(x, axis, step):
+    size = lax.axis_size(axis)
+    return lax.ppermute(x, axis, [(i, i ^ step) for i in range(size)])
+
+
+def window_body(index_volume, angles, offsets, measured):
+    slices = lax.axis_size("depth")
+    planes = lax.axis_size("row") // 2
+    place = lax.axis_index("depth")
+    core = lax.axis_index("row") % 2
+    plane = lax.axis_index("row") // 2
+    height, columns = index_volume.shape[1:]
+    rows = 2 * planes * height
+    half = planes * height
+    span = slices * COLBLK
+    cone = 2 * slices * HALFCOL
+    blocks = 1 + 2 * cone // COLBLK
+    width = blocks * COLBLK
+
+    padded = jnp.pad(index_volume[0], ((0, 0), (cone, cone)))
+    far = [None] + [
+        swap(lax.dynamic_slice_in_dim(padded, span * (plane ^ k), span + 2 * cone, 1), "row", 2 * k)
+        for k in range(1, planes)
+    ]
+    offset_tile = jnp.broadcast_to(offsets[0].astype(jnp.bfloat16), (height, COLBLK))
+    near = []
+    for j in range(slices):
+        part = lax.dynamic_slice_in_dim(padded, span * plane + COLBLK * (place ^ j), width, 1)
+        near.append(jnp.concatenate([part, offset_tile], axis=1))
+        if j > 0:
+            near[j] = swap(near[j], "depth", j)
+    far = jnp.stack(far[1:])
+    rest = []
+    for j in range(slices):
+        part = lax.dynamic_slice_in_dim(far, COLBLK * (place ^ j), width, 2)
+        rest.append(part if j == 0 else swap(part, "depth", j))
+    own = [jnp.concatenate([n[None, :, :width], r]) for n, r in zip(near, rest)]
+    own_first = own[0].reshape(1, half, width)
+    own_later = jnp.stack(own[1:]).reshape(slices - 1, half, width)
+    other = jnp.concatenate([swap(own_first, "row", 1), swap(own_later, "row", 1)])
+    own = jnp.concatenate([own_first, own_later])
+    tiles = jnp.stack([n[:, width:] for n in near])
+
+    mine = lax.dynamic_index_in_dim(measured, core, 0, False)
+    theirs = swap(lax.dynamic_index_in_dim(measured, 1 - core, 0, False), "row", 1)
+    both = jnp.pad(jnp.stack([mine, theirs]), ((0, 0), (0, 0), (cone // 2, cone // 2)))
+    both, _ = lax.optimization_barrier((both, far))
+    seen = [
+        lax.dynamic_slice_in_dim(both, span * (plane ^ k) + COLBLK * place, COLBLK + cone, 2) for k in range(planes)
+    ]
+    seen = jnp.stack([seen[0]] + [swap(seen[k], "row", 2 * k) for k in range(1, planes)])
+
+    sizes = (slices, planes, height, blocks, columns)
+    mine, theirs = pl.pallas_call(
+        functools.partial(sweep, sizes),
+        out_shape=[jax.ShapeDtypeStruct((slices, half, COLBLK), jnp.float32)] * 2,
+        in_specs=[pl.BlockSpec(memory_space=pltpu.SMEM)] + [pl.BlockSpec(memory_space=pltpu.VMEM)] * 6,
+        out_specs=[pl.BlockSpec(memory_space=pltpu.VMEM)] * 2,
+        scratch_shapes=[
+            pltpu.VMEM((slices, rows, width), jnp.float32),
+            pltpu.VMEM((slices, rows, width), jnp.float32),
+            pltpu.VMEM((2 * slices, blocks - 1, rows, 2 * COLBLK), jnp.float32),
+            pltpu.VMEM((slices, 2 * rows, COLBLK), jnp.float32),
+        ],
+        compiler_params=pltpu.CompilerParams(vmem_limit_bytes=40 * 1024 * 1024),
+    )(angles, tiles, own, other, seen, jnp.asarray(column_weights(False)), jnp.asarray(column_weights(True)))
+
+    summed = mine + swap(theirs, "row", 1)
+    parts = [summed[0]] + [swap(summed[j], "depth", j) for j in range(1, slices)]
+    parts = jnp.stack(parts).reshape(slices, planes, height, COLBLK)
+    parts = [parts[:, k] if k == 0 else swap(parts[:, k], "row", 2 * k) for k in range(planes)]
+    return pl.pallas_call(
+        functools.partial(arrange, sizes),
+        out_shape=jax.ShapeDtypeStruct((1, height, columns), jnp.float32),
+        in_specs=[pl.BlockSpec(memory_space=pltpu.VMEM)] * planes,
+        out_specs=pl.BlockSpec(memory_space=pltpu.VMEM),
+    )(*parts)
+
+
+def suits(mesh, index_volume, measured):
+    depth, row = mesh.shape["depth"], mesh.shape["row"]
+    slices, rows, columns = index_volume.shape
+    return (
+        slices == depth
+        and depth & (depth - 1) == 0
+        and row & (row - 1) == 0
+        and row > 1
+        and measured.shape[0] == 2
+        and rows == COLBLK
+        and rows // row % 16 == 0
+        and columns == COLBLK * depth * (row // 2)
+    )
+
+
 def solution(mesh):
     in_specs = (P("depth", "row", None), P(), P("depth"), P(None, "row", None))
     out_specs = P("depth", "row", None)
-    return jax.shard_map(body, mesh=mesh, in_specs=in_specs, out_specs=out_specs, check_vma=False)
+
+    def run(index_volume, angles, offsets, measured):
+        chosen = window_body if suits(mesh, index_volume, measured) else body
+        mapped = jax.shard_map(chosen, mesh=mesh, in_specs=in_specs, out_specs=out_specs, check_vma=False)
+        return mapped(index_volume, angles, offsets, measured)
+
+    return run

time: 233 us -> 58.8 us (0.25)
  the two profiles are of different devices: /device:TPU:1 before, /device:TPU:0 now
where the time goes in v2:
time: 58.8 us; the launch traced here: 58.6 us
  starting transfers between devices  25.7 us (44%)
  waiting for transfers between devices  14.9 us (25%)
  Pallas kernels  13.5 us (23%)
  local copies, waits for them, and re-layouts  2.93 us (5%)
  between operations  1.06 us (2%)
    ppermute x22, starting transfers between devices, swap(): return lax.ppermute(x, axis, [(i, i ^ step) for i in range(size)])  25.7 us
    ppermute x22, waiting for transfers between devices, swap(): return lax.ppermute(x, axis, [(i, i ^ step) for i in range(size)])  14.9 us
    pallas_call x1, Pallas kernels, window_body(): pl.pallas_call(functools.partial(sweep, sizes), out_shape=[jax.ShapeDtype...  12.1 us
    unnamed x16, local copies, waits for them, and re-layouts  1.93 us
    pallas_call x1, Pallas kernels, window_body(): pl.pallas_call(functools.partial(arrange, sizes), out_shape=jax.ShapeDtyp...  1.48 us
  transfers between devices with their start and end apart: 22, of which 12 were waited for; matrix products, arithmetic and copies ran while one was open for 1% of the time, Pallas kernels for 0%

profile of v2, /device:TPU:0, one launch (start us, length us, event | category | flops | bytes accessed | tf_op | source)
XLA Modules:
  0.0 58.6 jit_solution(3960321010127122811)
XLA Ops:
  1.0 4.0 %collective-permute-start.2 = (bf16[16,1280]{1,0:T(8,128)(2,1)S(1)}, bf16[16,1280]{1,0:T(8,128)(2,1)S(1)}, u32[]{:S(2)}, u32[]{:S(2)}) collective-permute-start(bf16[16,1280]{1,0:T(8,128)(2,1)S(1)} %concatenate.32), channel_id=1, source_target_pairs={{0,24},{8,16},{16,8},{24,0},{1,25},{9,17},{17,9},{25,1},{2,26},{10... | collective-permute-start | bytes 122888 | tf_op jit(solution)/shard_map/ppermute | solution.py:468
  5.7 4.1 %collective-permute-start.5 = (bf16[16,1536]{1,0:T(8,128)(2,1)S(1)}, bf16[16,1536]{1,0:T(8,128)(2,1)S(1)}, u32[]{:S(2)}, u32[]{:S(2)}) collective-permute-start(bf16[16,1536]{1,0:T(8,128)(2,1)S(1)} %get-tuple-element.35), channel_id=1, source_target_pairs={{0,6},{1,7},{2,4},{3,5},{4,2},{5,3},{6,0},{7,1},{8,14},{9,15},{10,... | collective-permute-start | bytes 147464 | tf_op jit(solution)/shard_map/ppermute | solution.py:468
  9.9 0.7 %collective-permute-start.3 = (bf16[16,1536]{1,0:T(8,128)(2,1)S(1)}, bf16[16,1536]{1,0:T(8,128)(2,1)S(1)}, u32[]{:S(2)}, u32[]{:S(2)}) collective-permute-start(bf16[16,1536]{1,0:T(8,128)(2,1)S(1)} %get-tuple-element.33), channel_id=1, source_target_pairs={{0,2},{1,3},{2,0},{3,1},{4,6},{5,7},{6,4},{7,5},{8,10},{9,11},{10,... | collective-permute-start | bytes 147464 | tf_op jit(solution)/shard_map/ppermute | solution.py:468
  10.8 1.3 %collective-permute-done.5 = bf16[16,1536]{1,0:T(8,128)(2,1)S(1)} collective-permute-done((bf16[16,1536]{1,0:T(8,128)(2,1)S(1)}, bf16[16,1536]{1,0:T(8,128)(2,1)S(1)}, u32[]{:S(2)}, u32[]{:S(2)}) %collective-permute-start.5) | collective-permute-done | bytes 49184 | tf_op jit(solution)/shard_map/ppermute | solution.py:468
  12.2 2.6 %collective-permute-done.4 = bf16[16,1536]{1,0:T(8,128)(2,1)S(1)} collective-permute-done((bf16[16,1536]{1,0:T(8,128)(2,1)S(1)}, bf16[16,1536]{1,0:T(8,128)(2,1)S(1)}, u32[]{:S(2)}, u32[]{:S(2)}) %collective-permute-start.4) | collective-permute-done | bytes 49184 | tf_op jit(solution)/shard_map/ppermute | solution.py:468
  14.9 2.5 %collective-permute-start.8 = (bf16[3,16,1152]{2,1,0:T(8,128)(2,1)S(1)}, bf16[3,16,1152]{2,1,0:T(8,128)(2,1)S(1)}, u32[]{:S(2)}, u32[]{:S(2)}) collective-permute-start(bf16[3,16,1152]{2,1,0:T(8,128)(2,1)S(1)} %get-tuple-element.16), channel_id=1, source_target_pairs={{0,24},{8,16},{16,8},{24,0},{1,25},{9,17},{17,9},{25,1},{2,26},{10... | collective-permute-start | bytes 331784 | tf_op jit(solution)/shard_map/ppermute | solution.py:468
  18.5 1.7 %collective-permute-start.14 = (bf16[2,16,640]{2,1,0:T(8,128)(2,1)S(1)}, bf16[2,16,640]{2,1,0:T(8,128)(2,1)S(1)}, u32[]{:S(2)}, u32[]{:S(2)}) collective-permute-start(bf16[2,16,640]{2,1,0:T(8,128)(2,1)S(1)} %get-tuple-element.12), channel_id=1, source_target_pairs={{0,6},{1,7},{2,4},{3,5},{4,2},{5,3},{6,0},{7,1},{8,14},{9,15},{10,... | collective-permute-start | bytes 122888 | tf_op jit(solution)/shard_map/ppermute | solution.py:468
  20.2 0.6 %collective-permute-start.13 = (bf16[2,16,640]{2,1,0:T(8,128)(2,1)S(1)}, bf16[2,16,640]{2,1,0:T(8,128)(2,1)S(1)}, u32[]{:S(2)}, u32[]{:S(2)}) collective-permute-start(bf16[2,16,640]{2,1,0:T(8,128)(2,1)S(1)} %get-tuple-element.13), channel_id=1, source_target_pairs={{0,4},{1,5},{2,6},{3,7},{4,0},{5,1},{6,2},{7,3},{8,12},{9,13},{10,... | collective-permute-start | bytes 122888 | tf_op jit(solution)/shard_map/ppermute | solution.py:468
  21.2 1.8 %collective-permute-start.12 = (bf16[2,16,640]{2,1,0:T(8,128)(2,1)S(1)}, bf16[2,16,640]{2,1,0:T(8,128)(2,1)S(1)}, u32[]{:S(2)}, u32[]{:S(2)}) collective-permute-start(bf16[2,16,640]{2,1,0:T(8,128)(2,1)S(1)} %get-tuple-element.14), channel_id=1, source_target_pairs={{0,2},{1,3},{2,0},{3,1},{4,6},{5,7},{6,4},{7,5},{8,10},{9,11},{10,... | collective-permute-start | bytes 122888 | tf_op jit(solution)/shard_map/ppermute | solution.py:468
  24.3 0.8 %collective-permute-done.13 = bf16[2,16,640]{2,1,0:T(8,128)(2,1)S(1)} collective-permute-done((bf16[2,16,640]{2,1,0:T(8,128)(2,1)S(1)}, bf16[2,16,640]{2,1,0:T(8,128)(2,1)S(1)}, u32[]{:S(2)}, u32[]{:S(2)}) %collective-permute-start.13) | collective-permute-done | bytes 40992 | tf_op jit(solution)/shard_map/ppermute | solution.py:468
  25.8 0.9 %copy-done.1 = bf16[1536,256]{1,0:T(8,128)(2,1)S(1)} copy-done((bf16[1536,256]{1,0:T(8,128)(2,1)S(1)}, bf16[1536,256]{1,0:T(8,128)(2,1)}, u32[]{:S(2)}) %copy-start.1) | copy-done | bytes 786456
  27.0 12.1 %shard_map.64 = (f32[4,64,128]{2,1,0:T(8,128)S(1)}, f32[4,64,128]{2,1,0:T(8,128)S(1)}) custom-call(s32[2]{0:T(128)S(1)} %copy-done.2, bf16[4,16,128]{2,1,0:T(8,128)(2,1)S(1)} %pad_maximum_fusion.10.tiles, bf16[4,64,1152]{2,1,0:T(8,128)(2,1)S(1)} %pad_maximum_fusion.own, bf16[4,64,1152]{2,1,0:T(8,128)(2,1)S(1)} %pad_maximum_fusion.1.other, ...), custom_call_target="tpu_custom_call" | custom-call | tf_op jit(solution)/shard_map/pallas_call | solution.py:519
  39.1 1.3 %collective-permute-done.15 = f32[4,64,128]{2,1,0:T(8,128)S(1)} collective-permute-done((f32[4,64,128]{2,1,0:T(8,128)S(1)}, f32[4,64,128]{2,1,0:T(8,128)S(1)}, u32[]{:S(2)}, u32[]{:S(2)}) %collective-permute-start.15) | collective-permute-done | bytes 131104 | tf_op jit(solution)/shard_map/ppermute | solution.py:468
  40.5 2.3 %collective-permute-start.18 = (f32[64,128]{1,0:T(8,128)S(1)}, f32[64,128]{1,0:T(8,128)S(1)}, u32[]{:S(2)}, u32[]{:S(2)}) collective-permute-start(f32[64,128]{1,0:T(8,128)S(1)} %get-tuple-element.24), channel_id=1, source_target_pairs={{0,24},{8,16},{16,8},{24,0},{1,25},{9,17},{17,9},{25,1},{2,26},{10... | collective-permute-start | bytes 98312 | tf_op jit(solution)/shard_map/ppermute | solution.py:468
  43.3 0.7 %collective-permute-start.16 = (f32[64,128]{1,0:T(8,128)S(1)}, f32[64,128]{1,0:T(8,128)S(1)}, u32[]{:S(2)}, u32[]{:S(2)}) collective-permute-start(f32[64,128]{1,0:T(8,128)S(1)} %get-tuple-element.26), channel_id=1, source_target_pairs={{0,8},{8,0},{16,24},{24,16},{1,9},{9,1},{17,25},{25,17},{2,10},{10... | collective-permute-start | bytes 98312 | tf_op jit(solution)/shard_map/ppermute | solution.py:468
  44.1 1.3 %collective-permute-done.18 = f32[64,128]{1,0:T(8,128)S(1)} collective-permute-done((f32[64,128]{1,0:T(8,128)S(1)}, f32[64,128]{1,0:T(8,128)S(1)}, u32[]{:S(2)}, u32[]{:S(2)}) %collective-permute-start.18) | collective-permute-done | bytes 32800 | tf_op jit(solution)/shard_map/ppermute | solution.py:468
  45.4 1.3 %collective-permute-done.17 = f32[64,128]{1,0:T(8,128)S(1)} collective-permute-done((f32[64,128]{1,0:T(8,128)S(1)}, f32[64,128]{1,0:T(8,128)S(1)}, u32[]{:S(2)}, u32[]{:S(2)}) %collective-permute-start.17) | collective-permute-done | bytes 32800 | tf_op jit(solution)/shard_map/ppermute | solution.py:468
  47.3 0.6 %slice_bitcast_fusion.3 = (f32[4,16,128]{2,1,0:T(8,128)S(1)}, f32[4,16,128]{2,1,0:T(8,128)S(1)}, f32[4,16,128]{2,1,0:T(8,128)S(1)}, f32[4,16,128]{2,1,0:T(8,128)}) fusion(f32[4,4,16,128]{3,2,0,1:T(8,128)S(1)} %pad_maximum_fusion.9), kind=kLoop, calls=%fused_computation.29 | loop fusion | bytes 262144 | tf_op jit(solution)/shard_map/squeeze | solution.py:536
  47.9 1.6 %collective-permute-start.19 = (f32[4,16,128]{2,1,0:T(8,128)S(1)}, f32[4,16,128]{2,1,0:T(8,128)S(1)}, u32[]{:S(2)}, u32[]{:S(2)}) collective-permute-start(f32[4,16,128]{2,1,0:T(8,128)S(1)} %get-tuple-element.21), channel_id=1, source_target_pairs={{0,2},{1,3},{2,0},{3,1},{4,6},{5,7},{6,4},{7,5},{8,10},{9,11},{10,... | collective-permute-start | bytes 98312 | tf_op jit(solution)/shard_map/ppermute | solution.py:468
  49.5 1.3 %collective-permute-start.20 = (f32[4,16,128]{2,1,0:T(8,128)S(1)}, f32[4,16,128]{2,1,0:T(8,128)S(1)}, u32[]{:S(2)}, u32[]{:S(2)}) collective-permute-start(f32[4,16,128]{2,1,0:T(8,128)S(1)} %get-tuple-element.20), channel_id=1, source_target_pairs={{0,4},{1,5},{2,6},{3,7},{4,0},{5,1},{6,2},{7,3},{8,12},{9,13},{10,... | collective-permute-start | bytes 98312 | tf_op jit(solution)/shard_map/ppermute | solution.py:468
  50.8 1.5 %collective-permute-start.21 = (f32[4,16,128]{2,1,0:T(8,128)S(1)}, f32[4,16,128]{2,1,0:T(8,128)S(1)}, u32[]{:S(2)}, u32[]{:S(2)}) collective-permute-start(f32[4,16,128]{2,1,0:T(8,128)S(1)} %get-tuple-element.19), channel_id=1, source_target_pairs={{0,6},{1,7},{2,4},{3,5},{4,2},{5,3},{6,0},{7,1},{8,14},{9,15},{10,... | collective-permute-start | bytes 98312 | tf_op jit(solution)/shard_map/ppermute | solution.py:468
  52.3 2.2 %collective-permute-done.20.refs_2_ = f32[4,16,128]{2,1,0:T(8,128)S(1)} collective-permute-done((f32[4,16,128]{2,1,0:T(8,128)S(1)}, f32[4,16,128]{2,1,0:T(8,128)S(1)}, u32[]{:S(2)}, u32[]{:S(2)}) %collective-permute-start.20) | collective-permute-done | bytes 32800 | tf_op jit(solution)/shard_map/ppermute | solution.py:468
  54.5 2.0 %collective-permute-done.21.refs_3_ = f32[4,16,128]{2,1,0:T(8,128)S(1)} collective-permute-done((f32[4,16,128]{2,1,0:T(8,128)S(1)}, f32[4,16,128]{2,1,0:T(8,128)S(1)}, u32[]{:S(2)}, u32[]{:S(2)}) %collective-permute-start.21) | collective-permute-done | bytes 32800 | tf_op jit(solution)/shard_map/ppermute | solution.py:468
  57.1 1.5 %shard_map.65 = f32[1,16,2048]{2,1,0:T(8,128)} custom-call(f32[4,16,128]{2,1,0:T(8,128)} %get-tuple-element.22.refs_0_, f32[4,16,128]{2,1,0:T(8,128)} %copy-done.5, f32[4,16,128]{2,1,0:T(8,128)} %copy-done.6, f32[4,16,128]{2,1,0:T(8,128)} %copy-done.7), custom_call_target="tpu_custom_call" | custom-call | tf_op jit(solution)/shard_map/pallas_call | solution.py:537
  (68 shorter events, 6.7 us)
Async XLA Ops:
  1.0 8.9 %collective-permute-start.2 = (bf16[16,1280]{1,0:T(8,128)(2,1)S(1)}, bf16[16,1280]{1,0:T(8,128)(2,1)S(1)}, u32[]{:S(2)}, u32[]{:S(2)}) collective-permute-start(bf16[16,1280]{1,0:T(8,128)(2,1)S(1)} %concatenate.32), channel_id=1, source_target_pairs={{0,24},{8,16},{16,8},{24,0},{1,25},{9,17},{17,9},{25,1},{2,26},{10... | collective-permute-start | bytes 122888 | tf_op jit(solution)/shard_map/ppermute | solution.py:468
  5.0 5.7 %collective-permute-start.1 = (bf16[16,1280]{1,0:T(8,128)(2,1)S(1)}, bf16[16,1280]{1,0:T(8,128)(2,1)S(1)}, u32[]{:S(2)}, u32[]{:S(2)}) collective-permute-start(bf16[16,1280]{1,0:T(8,128)(2,1)S(1)} %concatenate.31), channel_id=1, source_target_pairs={{0,16},{8,24},{16,0},{24,8},{1,17},{9,25},{17,1},{25,9},{2,18},{10... | collective-permute-start | bytes 122888 | tf_op jit(solution)/shard_map/ppermute | solution.py:468
  5.5 5.3 %collective-permute-start = (bf16[16,1280]{1,0:T(8,128)(2,1)S(1)}, bf16[16,1280]{1,0:T(8,128)(2,1)S(1)}, u32[]{:S(2)}, u32[]{:S(2)}) collective-permute-start(bf16[16,1280]{1,0:T(8,128)(2,1)S(1)} %concatenate.30), channel_id=1, source_target_pairs={{0,8},{8,0},{16,24},{24,16},{1,9},{9,1},{17,25},{25,17},{2,10},{10... | collective-permute-start | bytes 122888 | tf_op jit(solution)/shard_map/ppermute | solution.py:468
  5.6 4.2 %copy-start.4 = (bf16[2,16,2048]{2,1,0:T(8,128)(2,1)S(1)}, bf16[2,16,2048]{2,1,0:T(8,128)(2,1)}, u32[]{:S(2)}) copy-start(bf16[2,16,2048]{2,1,0:T(8,128)(2,1)} %param.9) | copy-start | bytes 393220
  5.7 6.4 %collective-permute-start.5 = (bf16[16,1536]{1,0:T(8,128)(2,1)S(1)}, bf16[16,1536]{1,0:T(8,128)(2,1)S(1)}, u32[]{:S(2)}, u32[]{:S(2)}) collective-permute-start(bf16[16,1536]{1,0:T(8,128)(2,1)S(1)} %get-tuple-element.35), channel_id=1, source_target_pairs={{0,6},{1,7},{2,4},{3,5},{4,2},{5,3},{6,0},{7,1},{8,14},{9,15},{10,... | collective-permute-start | bytes 147464 | tf_op jit(solution)/shard_map/ppermute | solution.py:468
  9.8 5.0 %collective-permute-start.4 = (bf16[16,1536]{1,0:T(8,128)(2,1)S(1)}, bf16[16,1536]{1,0:T(8,128)(2,1)S(1)}, u32[]{:S(2)}, u32[]{:S(2)}) collective-permute-start(bf16[16,1536]{1,0:T(8,128)(2,1)S(1)} %get-tuple-element.34), channel_id=1, source_target_pairs={{0,4},{1,5},{2,6},{3,7},{4,0},{5,1},{6,2},{7,3},{8,12},{9,13},{10,... | collective-permute-start | bytes 147464 | tf_op jit(solution)/shard_map/ppermute | solution.py:468
  9.9 4.9 %collective-permute-start.3 = (bf16[16,1536]{1,0:T(8,128)(2,1)S(1)}, bf16[16,1536]{1,0:T(8,128)(2,1)S(1)}, u32[]{:S(2)}, u32[]{:S(2)}) collective-permute-start(bf16[16,1536]{1,0:T(8,128)(2,1)S(1)} %get-tuple-element.33), channel_id=1, source_target_pairs={{0,2},{1,3},{2,0},{3,1},{4,6},{5,7},{6,4},{7,5},{8,10},{9,11},{10,... | collective-permute-start | bytes 147464 | tf_op jit(solution)/shard_map/ppermute | solution.py:468
  10.6 7.8 %collective-permute-start.11 = (bf16[16,2048]{1,0:T(8,128)(2,1)S(1)}, bf16[16,2048]{1,0:T(8,128)(2,1)S(1)}, u32[]{:S(2)}, u32[]{:S(2)}) collective-permute-start(bf16[16,2048]{1,0:T(8,128)(2,1)S(1)} %get-tuple-element.28), channel_id=1, source_target_pairs={{0,1},{1,0},{2,3},{3,2},{4,5},{5,4},{6,7},{7,6},{8,9},{9,8},{10,11... | collective-permute-start | bytes 196616 | tf_op jit(solution)/shard_map/ppermute | solution.py:468
  14.9 6.3 %collective-permute-start.8 = (bf16[3,16,1152]{2,1,0:T(8,128)(2,1)S(1)}, bf16[3,16,1152]{2,1,0:T(8,128)(2,1)S(1)}, u32[]{:S(2)}, u32[]{:S(2)}) collective-permute-start(bf16[3,16,1152]{2,1,0:T(8,128)(2,1)S(1)} %get-tuple-element.16), channel_id=1, source_target_pairs={{0,24},{8,16},{16,8},{24,0},{1,25},{9,17},{17,9},{25,1},{2,26},{10... | collective-permute-start | bytes 331784 | tf_op jit(solution)/shard_map/ppermute | solution.py:468
  17.4 5.6 %collective-permute-start.7 = (bf16[3,16,1152]{2,1,0:T(8,128)(2,1)S(1)}, bf16[3,16,1152]{2,1,0:T(8,128)(2,1)S(1)}, u32[]{:S(2)}, u32[]{:S(2)}) collective-permute-start(bf16[3,16,1152]{2,1,0:T(8,128)(2,1)S(1)} %get-tuple-element.17), channel_id=1, source_target_pairs={{0,16},{8,24},{16,0},{24,8},{1,17},{9,25},{17,1},{25,9},{2,18},{10... | collective-permute-start | bytes 331784 | tf_op jit(solution)/shard_map/ppermute | solution.py:468
  17.9 5.1 %collective-permute-start.6 = (bf16[3,16,1152]{2,1,0:T(8,128)(2,1)S(1)}, bf16[3,16,1152]{2,1,0:T(8,128)(2,1)S(1)}, u32[]{:S(2)}, u32[]{:S(2)}) collective-permute-start(bf16[3,16,1152]{2,1,0:T(8,128)(2,1)S(1)} %get-tuple-element.18), channel_id=1, source_target_pairs={{0,8},{8,0},{16,24},{24,16},{1,9},{9,1},{17,25},{25,17},{2,10},{10... | collective-permute-start | bytes 331784 | tf_op jit(solution)/shard_map/ppermute | solution.py:468
  18.5 5.9 %collective-permute-start.14 = (bf16[2,16,640]{2,1,0:T(8,128)(2,1)S(1)}, bf16[2,16,640]{2,1,0:T(8,128)(2,1)S(1)}, u32[]{:S(2)}, u32[]{:S(2)}) collective-permute-start(bf16[2,16,640]{2,1,0:T(8,128)(2,1)S(1)} %get-tuple-element.12), channel_id=1, source_target_pairs={{0,6},{1,7},{2,4},{3,5},{4,2},{5,3},{6,0},{7,1},{8,14},{9,15},{10,... | collective-permute-start | bytes 122888 | tf_op jit(solution)/shard_map/ppermute | solution.py:468
  20.2 4.9 %collective-permute-start.13 = (bf16[2,16,640]{2,1,0:T(8,128)(2,1)S(1)}, bf16[2,16,640]{2,1,0:T(8,128)(2,1)S(1)}, u32[]{:S(2)}, u32[]{:S(2)}) collective-permute-start(bf16[2,16,640]{2,1,0:T(8,128)(2,1)S(1)} %get-tuple-element.13), channel_id=1, source_target_pairs={{0,4},{1,5},{2,6},{3,7},{4,0},{5,1},{6,2},{7,3},{8,12},{9,13},{10,... | collective-permute-start | bytes 122888 | tf_op jit(solution)/shard_map/ppermute | solution.py:468
  21.2 4.4 %collective-permute-start.12 = (bf16[2,16,640]{2,1,0:T(8,128)(2,1)S(1)}, bf16[2,16,640]{2,1,0:T(8,128)(2,1)S(1)}, u32[]{:S(2)}, u32[]{:S(2)}) collective-permute-start(bf16[2,16,640]{2,1,0:T(8,128)(2,1)S(1)} %get-tuple-element.14), channel_id=1, source_target_pairs={{0,2},{1,3},{2,0},{3,1},{4,6},{5,7},{6,4},{7,5},{8,10},{9,11},{10,... | collective-permute-start | bytes 122888 | tf_op jit(solution)/shard_map/ppermute | solution.py:468
  23.1 2.6 %collective-permute-start.10 = (bf16[3,64,1152]{2,1,0:T(8,128)(2,1)S(1)}, bf16[3,64,1152]{2,1,0:T(8,128)(2,1)S(1)}, u32[]{:S(2)}, u32[]{:S(2)}) collective-permute-start(bf16[3,64,1152]{2,1,0:T(8,128)(2,1)S(1)} %pad_maximum_fusion.2), channel_id=1, source_target_pairs={{0,1},{1,0},{2,3},{3,2},{4,5},{5,4},{6,7},{7,6},{8,9},{9,8},{10,11... | collective-permute-start | bytes 1327112 | tf_op jit(solution)/shard_map/ppermute | solution.py:468
  23.2 2.5 %collective-permute-start.9 = (bf16[1,64,1152]{2,1,0:T(8,128)(2,1)S(1)}, bf16[1,64,1152]{2,1,0:T(8,128)(2,1)S(1)}, u32[]{:S(2)}, u32[]{:S(2)}) collective-permute-start(bf16[1,64,1152]{2,1,0:T(8,128)(2,1)S(1)} %bitcast.55), channel_id=1, source_target_pairs={{0,1},{1,0},{2,3},{3,2},{4,5},{5,4},{6,7},{7,6},{8,9},{9,8},{10,11... | collective-permute-start | bytes 442376 | tf_op jit(solution)/shard_map/ppermute | solution.py:468
  39.1 1.4 %collective-permute-start.15 = (f32[4,64,128]{2,1,0:T(8,128)S(1)}, f32[4,64,128]{2,1,0:T(8,128)S(1)}, u32[]{:S(2)}, u32[]{:S(2)}) collective-permute-start(f32[4,64,128]{2,1,0:T(8,128)S(1)} %get-tuple-element.10), channel_id=1, source_target_pairs={{0,1},{1,0},{2,3},{3,2},{4,5},{5,4},{6,7},{7,6},{8,9},{9,8},{10,11... | collective-permute-start | bytes 393224 | tf_op jit(solution)/shard_map/ppermute | solution.py:468
  40.5 4.9 %collective-permute-start.18 = (f32[64,128]{1,0:T(8,128)S(1)}, f32[64,128]{1,0:T(8,128)S(1)}, u32[]{:S(2)}, u32[]{:S(2)}) collective-permute-start(f32[64,128]{1,0:T(8,128)S(1)} %get-tuple-element.24), channel_id=1, source_target_pairs={{0,24},{8,16},{16,8},{24,0},{1,25},{9,17},{17,9},{25,1},{2,26},{10... | collective-permute-start | bytes 98312 | tf_op jit(solution)/shard_map/ppermute | solution.py:468
  42.8 3.9 %collective-permute-start.17 = (f32[64,128]{1,0:T(8,128)S(1)}, f32[64,128]{1,0:T(8,128)S(1)}, u32[]{:S(2)}, u32[]{:S(2)}) collective-permute-start(f32[64,128]{1,0:T(8,128)S(1)} %get-tuple-element.25), channel_id=1, source_target_pairs={{0,16},{8,24},{16,0},{24,8},{1,17},{9,25},{17,1},{25,9},{2,18},{10... | collective-permute-start | bytes 98312 | tf_op jit(solution)/shard_map/ppermute | solution.py:468
  43.3 3.9 %collective-permute-start.16 = (f32[64,128]{1,0:T(8,128)S(1)}, f32[64,128]{1,0:T(8,128)S(1)}, u32[]{:S(2)}, u32[]{:S(2)}) collective-permute-start(f32[64,128]{1,0:T(8,128)S(1)} %get-tuple-element.26), channel_id=1, source_target_pairs={{0,8},{8,0},{16,24},{24,16},{1,9},{9,1},{17,25},{25,17},{2,10},{10... | collective-permute-start | bytes 98312 | tf_op jit(solution)/shard_map/ppermute | solution.py:468
  47.9 4.4 %collective-permute-start.19 = (f32[4,16,128]{2,1,0:T(8,128)S(1)}, f32[4,16,128]{2,1,0:T(8,128)S(1)}, u32[]{:S(2)}, u32[]{:S(2)}) collective-permute-start(f32[4,16,128]{2,1,0:T(8,128)S(1)} %get-tuple-element.21), channel_id=1, source_target_pairs={{0,2},{1,3},{2,0},{3,1},{4,6},{5,7},{6,4},{7,5},{8,10},{9,11},{10,... | collective-permute-start | bytes 98312 | tf_op jit(solution)/shard_map/ppermute | solution.py:468
  49.5 5.0 %collective-permute-start.20 = (f32[4,16,128]{2,1,0:T(8,128)S(1)}, f32[4,16,128]{2,1,0:T(8,128)S(1)}, u32[]{:S(2)}, u32[]{:S(2)}) collective-permute-start(f32[4,16,128]{2,1,0:T(8,128)S(1)} %get-tuple-element.20), channel_id=1, source_target_pairs={{0,4},{1,5},{2,6},{3,7},{4,0},{5,1},{6,2},{7,3},{8,12},{9,13},{10,... | collective-permute-start | bytes 98312 | tf_op jit(solution)/shard_map/ppermute | solution.py:468
  50.8 5.7 %collective-permute-start.21 = (f32[4,16,128]{2,1,0:T(8,128)S(1)}, f32[4,16,128]{2,1,0:T(8,128)S(1)}, u32[]{:S(2)}, u32[]{:S(2)}) collective-permute-start(f32[4,16,128]{2,1,0:T(8,128)S(1)} %get-tuple-element.19), channel_id=1, source_target_pairs={{0,6},{1,7},{2,4},{3,5},{4,2},{5,3},{6,0},{7,1},{8,14},{9,15},{10,... | collective-permute-start | bytes 98312 | tf_op jit(solution)/shard_map/ppermute | solution.py:468
  52.3 4.2 %copy-start.5 = (f32[4,16,128]{2,1,0:T(8,128)}, f32[4,16,128]{2,1,0:T(8,128)S(1)}, u32[]{:S(2)}) copy-start(f32[4,16,128]{2,1,0:T(8,128)S(1)} %collective-permute-done.19.refs_1_) | copy-start | bytes 98308
  (6 other events, 7.2 us)

commit v3 on v2

--- a/solution.py
+++ b/solution.py
@@ -244,25 +244,27 @@
     return (np.cos(phase_arg) * weight, np.sin(phase_arg) * weight)
 
 
-def split_constant(matrix):
-    high = matrix.astype(jnp.bfloat16)
-    low = (matrix - high.astype(np.float64)).astype(jnp.bfloat16)
-    return (high, low)
-
-
-def column_weights(conjugate):
+def column_parts():
     taps = taps_of(HALFCOL, CHIRP_COL)
     source = np.arange(COLBLK + 2 * HALFCOL)[:, None]
     target = np.arange(COLBLK)[None, :]
     place = source - target
     inside = (place >= 0) & (place <= 2 * HALFCOL)
-    real_part, imag_part = [np.where(inside, t[np.clip(place, 0, 2 * HALFCOL)], 0.0) for t in taps]
-    if conjugate:
-        imag_part = -imag_part
-    from_real = np.concatenate([real_part, imag_part], axis=1)
-    from_imag = np.concatenate([-imag_part, real_part], axis=1)
-    high, low = split_constant(np.concatenate([from_real, from_imag], axis=0))
-    return np.concatenate([high, high, low], axis=0)
+    parts = [np.where(inside, t[np.clip(place, 0, 2 * HALFCOL)], 0.0) for t in taps]
+    high = [part.astype(jnp.bfloat16) for part in parts]
+    low = [(part - h.astype(np.float64)).astype(jnp.bfloat16) for part, h in zip(parts, high)]
+    return [[jnp.asarray(part) for part in pair] for pair in (high, low)]
+
+
+def column_weights(high, low):
+    results = []
+    for sign in (1, -1):
+        rows = []
+        for real_part, imag_part in (high, low):
+            rows.append(jnp.concatenate([real_part, sign * imag_part], axis=1))
+            rows.append(jnp.concatenate([-sign * imag_part, real_part], axis=1))
+        results.append(jnp.concatenate(rows))
+    return results
 
 
 def series(kind):
@@ -312,17 +314,15 @@
     return jnp.concatenate([upper, lower], axis=0)
 
 
-def sweep(sizes, angles, tiles, own, other, measured, forward_cols, adjoint_cols, mine, theirs, cosine, sine, field, kept):
-    slices, planes, height, blocks, columns = sizes
+def sweep(sizes, tilts, tiles, own, other, measured, forward_cols, adjoint_cols, mine, theirs, cosine, sine, field, kept):
+    slices, planes, height, blocks, broad, columns = sizes
     half = planes * height
     rows = 2 * half
     place = lax.axis_index("depth")
     core = lax.axis_index("row") % 2
     plane = lax.axis_index("row") // 2
-    block = plane * slices + place
-    angle = angles[core]
-    across = angle - TILTS // 2
-    along = lax.rem(3 * angle, TILTS) - TILTS // 2
+    block = plane % 2 * slices + place
+    across, along = [jnp.where(core == 0, tilts[i : i + 1, :1], tilts[i : i + 1, 1:]) for i in range(2)]
 
     def row_numbers(axis):
         i = lax.broadcasted_iota(jnp.int32, (rows, rows), axis)
@@ -334,7 +334,7 @@
     walk_off = [tiles[place ^ s, :1].astype(jnp.int32) for s in range(slices)]
     factors = [row_factor(rows_of, rows_across, offset) for offset in walk_off]
     width = blocks * COLBLK
-    first = block * COLBLK - 2 * slices * HALFCOL
+    first = block * broad - 2 * slices * HALFCOL
     lane = first + lax.broadcasted_iota(jnp.int32, (1, width), 1)
     inside = (lane >= 0) & (lane < columns)
 
@@ -354,7 +354,8 @@
 
     def mix_cols(level, j, left, right, weights):
         wide = jnp.concatenate([part for pair in zip(left, right) for part in pair], axis=1)
-        total = dot(wide, weights[: 8 * COLBLK]) + dot(wide[:, : 4 * COLBLK], weights[8 * COLBLK :])
+        high, low = wide[:, : 4 * COLBLK], wide[:, 4 * COLBLK :]
+        total = dot(high, weights[: 4 * COLBLK]) + (dot(low, weights[: 4 * COLBLK]) + dot(high, weights[4 * COLBLK :]))
         field[level, j] = total
 
     def mix_rows(factor, blocks_in):
@@ -392,7 +393,7 @@
                     a, b = read(s - 1, j)
                 a, b = c * a - d * b, c * b + d * a
                 start = (2 * slices - s) * HALFCOL - j * COLBLK
-                lo, hi = max(start, 0), min(start + COLBLK, COLBLK)
+                lo, hi = max(start, 0), min(start + broad, COLBLK)
                 if lo < hi:
                     kept[s, :rows, lo - start : hi - start] = a[:, lo:hi]
                     kept[s, rows:, lo - start : hi - start] = b[:, lo:hi]
@@ -426,15 +427,15 @@
         factor = split(complex_form(real_part.T, -imag_part.T))
         level = 2 * slices - 1 - s
         last = None
-        for group in pairs(s + 1):
+        for group in pairs(s + broad // COLBLK):
             for j, (a, b) in zip(group, mix_rows(factor, [read(level, j) for j in group])):
                 start = s * HALFCOL - j * COLBLK
-                lo, hi = max(start, 0), min(start + COLBLK, COLBLK)
+                lo, hi = max(start, 0), min(start + broad, COLBLK)
                 if lo < hi:
                     y = kept[s, :, lo - start : hi - start]
                     part = PHASE_SCALE * (y[:rows] * b[:, lo:hi] - y[rows:] * a[:, lo:hi])
-                    mine[place ^ s, :, lo - start : hi - start] = part[:half]
-                    theirs[place ^ s, :, lo - start : hi - start] = part[half:]
+                    mine[place ^ s, :, lo - start : hi - start] = part[: 2 * height]
+                    theirs[place ^ s, :, lo - start : hi - start] = part[half : half + 2 * height]
                 if s > 0:
                     begin = 2 * (slices - s) * HALFCOL + j * COLBLK
                     c = cosine[s, :, begin : begin + COLBLK]
@@ -446,21 +447,21 @@
             yield
 
     stages = [forward(s) for s in range(slices)] + [residual()] + [backward(s) for s in reversed(range(slices))]
-    counts = [blocks - s for s in range(slices)] + [blocks - slices] + [s + 1 for s in reversed(range(slices))]
+    counts = [blocks - s for s in range(slices)] + [blocks - slices] + [s + broad // COLBLK for s in reversed(range(slices))]
     order = [(2 * k + t, k) for k, n in enumerate(counts) for t in range(len(pairs(n)))]
     for _, k in sorted(order):
         next(stages[k])
 
 
 def arrange(sizes, *refs):
-    slices, planes = sizes[:2]
+    slices, broad = sizes[0], sizes[4]
     place = lax.axis_index("depth")
-    plane = lax.axis_index("row") // 2
+    group = lax.axis_index("row") // 2 % 2
     out = refs[-1]
-    for k in range(planes):
-        for j in range(slices):
-            block = (plane ^ k) * slices + (place ^ j)
-            out[0, :, pl.ds(pl.multiple_of(block * COLBLK, COLBLK), COLBLK)] = refs[k][j]
+    for j in range(slices):
+        for i in range(2):
+            block = (group ^ i) * slices + (place ^ j)
+            out[0, :, pl.ds(pl.multiple_of(block * broad, broad), broad)] = refs[j][i]
 
 
 def swap(x, axis, step):
@@ -474,71 +475,73 @@
     place = lax.axis_index("depth")
     core = lax.axis_index("row") % 2
     plane = lax.axis_index("row") // 2
+    group = plane % 2
     height, columns = index_volume.shape[1:]
     rows = 2 * planes * height
     half = planes * height
-    span = slices * COLBLK
+    span = columns // 2
+    broad = span // slices
     cone = 2 * slices * HALFCOL
-    blocks = 1 + 2 * cone // COLBLK
+    blocks = (broad + 2 * cone) // COLBLK
     width = blocks * COLBLK
-
-    padded = jnp.pad(index_volume[0], ((0, 0), (cone, cone)))
-    far = [None] + [
-        swap(lax.dynamic_slice_in_dim(padded, span * (plane ^ k), span + 2 * cone, 1), "row", 2 * k)
-        for k in range(1, planes)
-    ]
-    offset_tile = jnp.broadcast_to(offsets[0].astype(jnp.bfloat16), (height, COLBLK))
-    near = []
-    for j in range(slices):
-        part = lax.dynamic_slice_in_dim(padded, span * plane + COLBLK * (place ^ j), width, 1)
-        near.append(jnp.concatenate([part, offset_tile], axis=1))
-        if j > 0:
-            near[j] = swap(near[j], "depth", j)
-    far = jnp.stack(far[1:])
-    rest = []
-    for j in range(slices):
-        part = lax.dynamic_slice_in_dim(far, COLBLK * (place ^ j), width, 2)
-        rest.append(part if j == 0 else swap(part, "depth", j))
-    own = [jnp.concatenate([n[None, :, :width], r]) for n, r in zip(near, rest)]
-    own_first = own[0].reshape(1, half, width)
-    own_later = jnp.stack(own[1:]).reshape(slices - 1, half, width)
-    other = jnp.concatenate([swap(own_first, "row", 1), swap(own_later, "row", 1)])
-    own = jnp.concatenate([own_first, own_later])
-    tiles = jnp.stack([n[:, width:] for n in near])
 
     mine = lax.dynamic_index_in_dim(measured, core, 0, False)
     theirs = swap(lax.dynamic_index_in_dim(measured, 1 - core, 0, False), "row", 1)
     both = jnp.pad(jnp.stack([mine, theirs]), ((0, 0), (0, 0), (cone // 2, cone // 2)))
-    both, _ = lax.optimization_barrier((both, far))
-    seen = [
-        lax.dynamic_slice_in_dim(both, span * (plane ^ k) + COLBLK * place, COLBLK + cone, 2) for k in range(planes)
+    first_two = [lax.dynamic_slice_in_dim(both, span * (group ^ i) + broad * place, broad + cone, 2) for i in range(2)]
+    weights, first_two = lax.optimization_barrier((column_parts(), first_two))
+
+    far = [
+        lax.dynamic_slice_in_dim(index_volume[0], (span - cone) * (group ^ k % 2), span + cone, 1)
+        for k in range(planes)
     ]
-    seen = jnp.stack([seen[0]] + [swap(seen[k], "row", 2 * k) for k in range(1, planes)])
-
-    sizes = (slices, planes, height, blocks, columns)
+    far = [far[k] if k == 0 else swap(far[k], "row", 2 * k) for k in range(planes)]
+    tilts = jnp.stack([angles - TILTS // 2, jnp.mod(3 * angles, TILTS) - TILTS // 2])
+    weights, tilts, first_two, far = lax.optimization_barrier(
+        (column_weights(*weights), tilts, first_two, far)
+    )
+    far = jnp.pad(jnp.stack(far), ((0, 0), (0, 0), (cone, cone)))
+    offset_tile = jnp.broadcast_to(offsets[0].astype(jnp.bfloat16), (planes, height, COLBLK))
+    parts = [lax.dynamic_slice_in_dim(far, cone * group + broad * (place ^ j), width, 2) for j in range(slices)]
+    own = [jnp.concatenate([part, offset_tile], axis=2) for part in parts]
+    last_sent = own[1]
+    own = [own[j] if j == 0 else swap(own[j], "depth", j) for j in range(slices)]
+    tiles = jnp.stack([x[0, :, width:] for x in own])
+    own_first = own[0][:, :, :width].reshape(1, half, width)
+    own_later = jnp.stack([x[:, :, :width] for x in own[1:]]).reshape(slices - 1, half, width)
+    other_first = swap(own_first, "row", 1)
+    other = jnp.concatenate([other_first, swap(own_later, "row", 1)])
+    own = jnp.concatenate([own_first, own_later])
+
+    first_two = jnp.stack([first_two[0], swap(first_two[1], "row", 2)])
+    first_two, _ = lax.optimization_barrier((first_two, last_sent))
+    seen = [first_two] + [swap(first_two, "row", 2 * k) for k in range(2, planes, 2)]
+    seen = jnp.concatenate(seen)
+
+    sizes = (slices, planes, height, blocks, broad, columns)
     mine, theirs = pl.pallas_call(
         functools.partial(sweep, sizes),
-        out_shape=[jax.ShapeDtypeStruct((slices, half, COLBLK), jnp.float32)] * 2,
-        in_specs=[pl.BlockSpec(memory_space=pltpu.SMEM)] + [pl.BlockSpec(memory_space=pltpu.VMEM)] * 6,
+        out_shape=[jax.ShapeDtypeStruct((slices, 2 * height, broad), jnp.float32)] * 2,
+        in_specs=[pl.BlockSpec(memory_space=pltpu.VMEM)] * 7,
         out_specs=[pl.BlockSpec(memory_space=pltpu.VMEM)] * 2,
         scratch_shapes=[
             pltpu.VMEM((slices, rows, width), jnp.float32),
             pltpu.VMEM((slices, rows, width), jnp.float32),
             pltpu.VMEM((2 * slices, blocks - 1, rows, 2 * COLBLK), jnp.float32),
-            pltpu.VMEM((slices, 2 * rows, COLBLK), jnp.float32),
+            pltpu.VMEM((slices, 2 * rows, broad), jnp.float32),
         ],
         compiler_params=pltpu.CompilerParams(vmem_limit_bytes=40 * 1024 * 1024),
-    )(angles, tiles, own, other, seen, jnp.asarray(column_weights(False)), jnp.asarray(column_weights(True)))
+    )(tilts, tiles, own, other, seen, *weights)
 
     summed = mine + swap(theirs, "row", 1)
-    parts = [summed[0]] + [swap(summed[j], "depth", j) for j in range(1, slices)]
-    parts = jnp.stack(parts).reshape(slices, planes, height, COLBLK)
-    parts = [parts[:, k] if k == 0 else swap(parts[:, k], "row", 2 * k) for k in range(planes)]
+    parts = jnp.stack([summed[:, :height], swap(summed[:, height:], "row", 2)], axis=1)
+    parts = [parts[j] if j == 0 else swap(parts[j], "depth", j) for j in range(slices)]
     return pl.pallas_call(
         functools.partial(arrange, sizes),
         out_shape=jax.ShapeDtypeStruct((1, height, columns), jnp.float32),
-        in_specs=[pl.BlockSpec(memory_space=pltpu.VMEM)] * planes,
+        in_specs=[pl.BlockSpec(memory_space=pltpu.VMEM)] * slices,
         out_specs=pl.BlockSpec(memory_space=pltpu.VMEM),
+        compiler_params=pltpu.CompilerParams(vmem_limit_bytes=4 * 1024 * 1024),
     )(*parts)
 
 
@@ -549,11 +552,12 @@
         slices == depth
         and depth & (depth - 1) == 0
         and row & (row - 1) == 0
-        and row > 1
+        and row > 2
         and measured.shape[0] == 2
         and rows == COLBLK
         and rows // row % 16 == 0
-        and columns == COLBLK * depth * (row // 2)
+        and columns % (2 * depth * COLBLK) == 0
+        and columns >= 4 * depth * HALFCOL
     )
 
 

time: 58.8 us -> 51.9 us (0.88)
  starting transfers between devices: 25.7 us -> 17.9 us
    ppermute x22 -> x16, starting transfers between devices: 25.7 us -> 17.9 us  [swap(): return lax.ppermute(x, axis, [(i, i ^ step) for i in range(size)])]
    unnamed x16 -> x14, local copies, waits for them, and re-layouts: 1.93 us -> 3.18 us
    pallas_call x1, Pallas kernels: 12.1 us -> 13.2 us  [window_body(): pl.pallas_call(functools.partial(sweep, sizes), out_shape=[jax.ShapeDtype...]
    pallas_call x1, Pallas kernels: 1.48 us -> 0.67 us  [window_body(): pl.pallas_call(functools.partial(arrange, sizes), out_shape=jax.ShapeDtyp...]
    squeeze x1 -> x0, local copies, waits for them, and re-layouts: 0.62 us -> none  [window_body(): parts[:, k]]
    ppermute x22 -> x16, waiting for transfers between devices: 14.9 us -> 15.1 us  [swap(): return lax.ppermute(x, axis, [(i, i ^ step) for i in range(size)])]
  transfers between devices with their start and end apart: 22 -> 16, of which waited for: 12 -> 12; matrix products, arithmetic and copies ran while one was open for 1% -> 1% of each run, Pallas kernels for 0% -> 0%
where the time goes in v3:
time: 51.9 us; the launch traced here: 51.6 us
  starting transfers between devices  17.9 us (34%)
  waiting for transfers between devices  15.1 us (29%)
  Pallas kernels  13.9 us (27%)
  local copies, waits for them, and re-layouts  3.37 us (6%)
  between operations  0.92 us (2%)
    ppermute x16, starting transfers between devices, swap(): return lax.ppermute(x, axis, [(i, i ^ step) for i in range(size)])  17.9 us
    ppermute x16, waiting for transfers between devices, swap(): return lax.ppermute(x, axis, [(i, i ^ step) for i in range(size)])  15.1 us
    pallas_call x1, Pallas kernels, window_body(): pl.pallas_call(functools.partial(sweep, sizes), out_shape=[jax.ShapeDtype...  13.2 us
    unnamed x14, local copies, waits for them, and re-layouts  3.18 us
  transfers between devices with their start and end apart: 16, of which 12 were waited for; matrix products, arithmetic and copies ran while one was open for 1% of the time, Pallas kernels for 0%

profile of v3, /device:TPU:0, one launch (start us, length us, event | category | flops | bytes accessed | tf_op | source)
XLA Modules:
  0.0 51.6 jit_solution(15526878116001891234)
XLA Ops:
  0.0 0.8 %copy-done.2 = bf16[1,16,2048]{2,1,0:T(8,128)(2,1)S(1)} copy-done((bf16[1,16,2048]{2,1,0:T(8,128)(2,1)S(1)}, bf16[1,16,2048]{2,1,0:T(8,128)(2,1)}, u32[]{:S(2)}) %copy-start.2) | copy-done | bytes 65560
  0.8 5.1 %collective-permute-start.3 = (bf16[16,1536]{1,0:T(8,128)(2,1)S(1)}, bf16[16,1536]{1,0:T(8,128)(2,1)S(1)}, u32[]{:S(2)}, u32[]{:S(2)}) collective-permute-start(bf16[16,1536]{1,0:T(8,128)(2,1)S(1)} %get-tuple-element.57), channel_id=1, source_target_pairs={{0,6},{1,7},{2,4},{3,5},{4,2},{5,3},{6,0},{7,1},{8,14},{9,15},{10,... | collective-permute-start | bytes 147464 | tf_op jit(solution)/shard_map/ppermute | solution.py:469
  6.0 0.6 %collective-permute-start.2 = (bf16[16,1536]{1,0:T(8,128)(2,1)S(1)}, bf16[16,1536]{1,0:T(8,128)(2,1)S(1)}, u32[]{:S(2)}, u32[]{:S(2)}) collective-permute-start(bf16[16,1536]{1,0:T(8,128)(2,1)S(1)} %get-tuple-element.30), channel_id=1, source_target_pairs={{0,4},{1,5},{2,6},{3,7},{4,0},{5,1},{6,2},{7,3},{8,12},{9,13},{10,... | collective-permute-start | bytes 147464 | tf_op jit(solution)/shard_map/ppermute | solution.py:469
  7.4 0.6 %copy-done.6 = s32[2]{0:T(128)S(1)} copy-done((s32[2]{0:T(128)S(1)}, s32[2]{0:T(128)}, u32[]{:S(2)}) %copy-start.6) | copy-done | bytes 32
  8.1 0.8 %copy-done = bf16[256,128]{1,0:T(8,128)(2,1)S(1)} copy-done((bf16[256,128]{1,0:T(8,128)(2,1)S(1)}, bf16[256,128]{1,0:T(8,128)(2,1)}, u32[]{:S(2)}) %copy-start) | copy-done | bytes 65560
  9.0 0.8 %copy-done.4 = bf16[256,128]{1,0:T(8,128)(2,1)S(1)} copy-done((bf16[256,128]{1,0:T(8,128)(2,1)S(1)}, bf16[256,128]{1,0:T(8,128)(2,1)}, u32[]{:S(2)}) %copy-start.4) | copy-done | bytes 65560
  10.1 1.2 %collective-permute-done.2 = bf16[16,1536]{1,0:T(8,128)(2,1)S(1)} collective-permute-done((bf16[16,1536]{1,0:T(8,128)(2,1)S(1)}, bf16[16,1536]{1,0:T(8,128)(2,1)S(1)}, u32[]{:S(2)}, u32[]{:S(2)}) %collective-permute-start.2) | collective-permute-done | bytes 49184 | tf_op jit(solution)/shard_map/ppermute | solution.py:469
  11.4 1.6 %collective-permute-start.5 = (bf16[4,16,1408]{2,1,0:T(8,128)(2,1)S(1)}, bf16[4,16,1408]{2,1,0:T(8,128)(2,1)S(1)}, u32[]{:S(2)}, u32[]{:S(2)}) collective-permute-start(bf16[4,16,1408]{2,1,0:T(8,128)(2,1)S(1)} %concatenate.61), channel_id=1, source_target_pairs={{0,16},{8,24},{16,0},{24,8},{1,17},{9,25},{17,1},{25,9},{2,18},{10... | collective-permute-start | bytes 540680 | tf_op jit(solution)/shard_map/ppermute | solution.py:469
  13.0 1.4 %collective-permute-start.6 = (bf16[4,16,1408]{2,1,0:T(8,128)(2,1)S(1)}, bf16[4,16,1408]{2,1,0:T(8,128)(2,1)S(1)}, u32[]{:S(2)}, u32[]{:S(2)}) collective-permute-start(bf16[4,16,1408]{2,1,0:T(8,128)(2,1)S(1)} %concatenate.62), channel_id=1, source_target_pairs={{0,24},{8,16},{16,8},{24,0},{1,25},{9,17},{17,9},{25,1},{2,26},{10... | collective-permute-start | bytes 540680 | tf_op jit(solution)/shard_map/ppermute | solution.py:469
  14.4 0.6 %collective-permute-start.4 = (bf16[4,16,1408]{2,1,0:T(8,128)(2,1)S(1)}, bf16[4,16,1408]{2,1,0:T(8,128)(2,1)S(1)}, u32[]{:S(2)}, u32[]{:S(2)}) collective-permute-start(bf16[4,16,1408]{2,1,0:T(8,128)(2,1)S(1)} %concatenate.60), channel_id=1, source_target_pairs={{0,8},{8,0},{16,24},{24,16},{1,9},{9,1},{17,25},{25,17},{2,10},{10... | collective-permute-start | bytes 540680 | tf_op jit(solution)/shard_map/ppermute | solution.py:469
  15.0 1.7 %collective-permute-start.9 = (bf16[2,16,768]{2,1,0:T(8,128)(2,1)S(1)}, bf16[2,16,768]{2,1,0:T(8,128)(2,1)S(1)}, u32[]{:S(2)}, u32[]{:S(2)}) collective-permute-start(bf16[2,16,768]{2,1,0:T(8,128)(2,1)S(1)} %get-tuple-element.35), channel_id=1, source_target_pairs={{0,2},{1,3},{2,0},{3,1},{4,6},{5,7},{6,4},{7,5},{8,10},{9,11},{10,... | collective-permute-start | bytes 147464 | tf_op jit(solution)/shard_map/ppermute | solution.py:469
  16.8 2.3 %collective-permute-done.9 = bf16[2,16,768]{2,1,0:T(8,128)(2,1)S(1)} collective-permute-done((bf16[2,16,768]{2,1,0:T(8,128)(2,1)S(1)}, bf16[2,16,768]{2,1,0:T(8,128)(2,1)S(1)}, u32[]{:S(2)}, u32[]{:S(2)}) %collective-permute-start.9) | collective-permute-done | bytes 49184 | tf_op jit(solution)/shard_map/ppermute | solution.py:469
  19.1 1.3 %collective-permute-start.10 = (bf16[2,2,16,768]{3,2,1,0:T(8,128)(2,1)S(1)}, bf16[2,2,16,768]{3,2,1,0:T(8,128)(2,1)S(1)}, u32[]{:S(2)}, u32[]{:S(2)}) collective-permute-start(bf16[2,2,16,768]{3,2,1,0:T(8,128)(2,1)S(1)} %pad_maximum_fusion.12), channel_id=1, source_target_pairs={{0,4},{1,5},{2,6},{3,7},{4,0},{5,1},{6,2},{7,3},{8,12},{9,13},{10,... | collective-permute-start | bytes 294920 | tf_op jit(solution)/shard_map/ppermute | solution.py:469
  20.5 0.8 %collective-permute-done.6 = bf16[4,16,1408]{2,1,0:T(8,128)(2,1)S(1)} collective-permute-done((bf16[4,16,1408]{2,1,0:T(8,128)(2,1)S(1)}, bf16[4,16,1408]{2,1,0:T(8,128)(2,1)S(1)}, u32[]{:S(2)}, u32[]{:S(2)}) %collective-permute-start.6) | collective-permute-done | bytes 180256 | tf_op jit(solution)/shard_map/ppermute | solution.py:469
  21.3 0.8 %collective-permute-done.4 = bf16[4,16,1408]{2,1,0:T(8,128)(2,1)S(1)} collective-permute-done((bf16[4,16,1408]{2,1,0:T(8,128)(2,1)S(1)}, bf16[4,16,1408]{2,1,0:T(8,128)(2,1)S(1)}, u32[]{:S(2)}, u32[]{:S(2)}) %collective-permute-start.4) | collective-permute-done | bytes 180256 | tf_op jit(solution)/shard_map/ppermute | solution.py:469
  22.3 2.4 %collective-permute-done.10 = bf16[2,2,16,768]{3,2,1,0:T(8,128)(2,1)S(1)} collective-permute-done((bf16[2,2,16,768]{3,2,1,0:T(8,128)(2,1)S(1)}, bf16[2,2,16,768]{3,2,1,0:T(8,128)(2,1)S(1)}, u32[]{:S(2)}, u32[]{:S(2)}) %collective-permute-start.10) | collective-permute-done | bytes 98336 | tf_op jit(solution)/shard_map/ppermute | solution.py:469
  25.0 13.2 %shard_map.82 = (f32[4,32,256]{2,1,0:T(8,128)S(1)}, f32[4,32,256]{2,1,0:T(8,128)S(1)}) custom-call(s32[2,2]{1,0:T(2,128)S(1)} %pad_add_fusion.tilts, bf16[4,16,128]{2,1,0:T(8,128)(2,1)S(1)} %pad_maximum_fusion.14.tiles, bf16[4,64,1280]{2,1,0:T(8,128)(2,1)S(1)} %pad_maximum_fusion.8.own, bf16[4,64,1280]{2,1,0:T(8,128)(2,1)S(1)} %pad_maximum_fusion.9.other, ...), custom_call_target="tpu_custom_call" | custom-call | tf_op jit(solution)/shard_map/pallas_call | solution.py:522
  38.3 1.3 %collective-permute-done.11 = f32[4,32,256]{2,1,0:T(8,128)S(1)} collective-permute-done((f32[4,32,256]{2,1,0:T(8,128)S(1)}, f32[4,32,256]{2,1,0:T(8,128)S(1)}, u32[]{:S(2)}, u32[]{:S(2)}) %collective-permute-start.11) | collective-permute-done | bytes 131104 | tf_op jit(solution)/shard_map/ppermute | solution.py:469
  39.7 1.8 %collective-permute-start.12 = (f32[4,16,256]{2,1,0:T(8,128)S(1)}, f32[4,16,256]{2,1,0:T(8,128)S(1)}, u32[]{:S(2)}, u32[]{:S(2)}) collective-permute-start(f32[4,16,256]{2,1,0:T(8,128)S(1)} %get-tuple-element.53), channel_id=1, source_target_pairs={{0,2},{1,3},{2,0},{3,1},{4,6},{5,7},{6,4},{7,5},{8,10},{9,11},{10,... | collective-permute-start | bytes 196616 | tf_op jit(solution)/shard_map/ppermute | solution.py:469
  41.5 2.5 %collective-permute-done.12 = f32[4,16,256]{2,1,0:T(8,128)S(1)} collective-permute-done((f32[4,16,256]{2,1,0:T(8,128)S(1)}, f32[4,16,256]{2,1,0:T(8,128)S(1)}, u32[]{:S(2)}, u32[]{:S(2)}) %collective-permute-start.12) | collective-permute-done | bytes 65568 | tf_op jit(solution)/shard_map/ppermute | solution.py:469
  44.0 2.5 %collective-permute-start.15 = (f32[2,16,256]{2,1,0:T(8,128)S(1)}, f32[2,16,256]{2,1,0:T(8,128)S(1)}, u32[]{:S(2)}, u32[]{:S(2)}) collective-permute-start(f32[2,16,256]{2,1,0:T(8,128)S(1)} %get-tuple-element.49), channel_id=1, source_target_pairs={{0,24},{8,16},{16,8},{24,0},{1,25},{9,17},{17,9},{25,1},{2,26},{10... | collective-permute-start | bytes 98312 | tf_op jit(solution)/shard_map/ppermute | solution.py:469
  47.6 1.3 %collective-permute-done.15.refs_3_ = f32[2,16,256]{2,1,0:T(8,128)S(1)} collective-permute-done((f32[2,16,256]{2,1,0:T(8,128)S(1)}, f32[2,16,256]{2,1,0:T(8,128)S(1)}, u32[]{:S(2)}, u32[]{:S(2)}) %collective-permute-start.15) | collective-permute-done | bytes 32800 | tf_op jit(solution)/shard_map/ppermute | solution.py:469
  48.9 1.6 %collective-permute-done.13.refs_1_ = f32[2,16,256]{2,1,0:T(8,128)S(1)} collective-permute-done((f32[2,16,256]{2,1,0:T(8,128)S(1)}, f32[2,16,256]{2,1,0:T(8,128)S(1)}, u32[]{:S(2)}, u32[]{:S(2)}) %collective-permute-start.13) | collective-permute-done | bytes 32800 | tf_op jit(solution)/shard_map/ppermute | solution.py:469
  51.0 0.7 %shard_map.83 = f32[1,16,2048]{2,1,0:T(8,128)} custom-call(f32[2,16,256]{2,1,0:T(8,128)S(1)} %get-tuple-element.50.refs_0_, f32[2,16,256]{2,1,0:T(8,128)S(1)} %collective-permute-done.13.refs_1_, f32[2,16,256]{2,1,0:T(8,128)S(1)} %collective-permute-done.14.refs_2_, f32[2,16,256]{2,1,0:T(8,128)S(1)} %collective-permute-done.15.refs_3_), custom_call_target="tpu_custom_call" | custom-call | tf_op jit(solution)/shard_map/pallas_call | solution.py:539
  (53 shorter events, 2.8 us)
Async XLA Ops:
  0.0 0.8 %copy-start.2 = (bf16[1,16,2048]{2,1,0:T(8,128)(2,1)S(1)}, bf16[1,16,2048]{2,1,0:T(8,128)(2,1)}, u32[]{:S(2)}) copy-start(bf16[1,16,2048]{2,1,0:T(8,128)(2,1)} %param.8) | copy-start | bytes 196612
  0.0 6.6 %copy-start.3 = (bf16[2,16,2048]{2,1,0:T(8,128)(2,1)S(1)}, bf16[2,16,2048]{2,1,0:T(8,128)(2,1)}, u32[]{:S(2)}) copy-start(bf16[2,16,2048]{2,1,0:T(8,128)(2,1)} %param.11) | copy-start | bytes 393220
  0.8 9.1 %collective-permute-start.3 = (bf16[16,1536]{1,0:T(8,128)(2,1)S(1)}, bf16[16,1536]{1,0:T(8,128)(2,1)S(1)}, u32[]{:S(2)}, u32[]{:S(2)}) collective-permute-start(bf16[16,1536]{1,0:T(8,128)(2,1)S(1)} %get-tuple-element.57), channel_id=1, source_target_pairs={{0,6},{1,7},{2,4},{3,5},{4,2},{5,3},{6,0},{7,1},{8,14},{9,15},{10,... | collective-permute-start | bytes 147464 | tf_op jit(solution)/shard_map/ppermute | solution.py:469
  6.0 4.1 %collective-permute-start.1 = (bf16[16,1536]{1,0:T(8,128)(2,1)S(1)}, bf16[16,1536]{1,0:T(8,128)(2,1)S(1)}, u32[]{:S(2)}, u32[]{:S(2)}) collective-permute-start(bf16[16,1536]{1,0:T(8,128)(2,1)S(1)} %get-tuple-element.57), channel_id=1, source_target_pairs={{0,2},{1,3},{2,0},{3,1},{4,6},{5,7},{6,4},{7,5},{8,10},{9,11},{10,... | collective-permute-start | bytes 147464 | tf_op jit(solution)/shard_map/ppermute | solution.py:469
  6.0 5.3 %collective-permute-start.2 = (bf16[16,1536]{1,0:T(8,128)(2,1)S(1)}, bf16[16,1536]{1,0:T(8,128)(2,1)S(1)}, u32[]{:S(2)}, u32[]{:S(2)}) collective-permute-start(bf16[16,1536]{1,0:T(8,128)(2,1)S(1)} %get-tuple-element.30), channel_id=1, source_target_pairs={{0,4},{1,5},{2,6},{3,7},{4,0},{5,1},{6,2},{7,3},{8,12},{9,13},{10,... | collective-permute-start | bytes 147464 | tf_op jit(solution)/shard_map/ppermute | solution.py:469
  6.6 1.4 %collective-permute-start = (bf16[16,2048]{1,0:T(8,128)(2,1)S(1)}, bf16[16,2048]{1,0:T(8,128)(2,1)S(1)}, u32[]{:S(2)}, u32[]{:S(2)}) collective-permute-start(bf16[16,2048]{1,0:T(8,128)(2,1)S(1)} %get-tuple-element.56), channel_id=1, source_target_pairs={{0,1},{1,0},{2,3},{3,2},{4,5},{5,4},{6,7},{7,6},{8,9},{9,8},{10,11... | collective-permute-start | bytes 196616 | tf_op jit(solution)/shard_map/ppermute | solution.py:469
  7.4 0.7 %copy-start.6 = (s32[2]{0:T(128)S(1)}, s32[2]{0:T(128)}, u32[]{:S(2)}) copy-start(s32[2]{0:T(128)} %param.9) | copy-start | bytes 28
  8.1 0.8 %copy-start = (bf16[256,128]{1,0:T(8,128)(2,1)S(1)}, bf16[256,128]{1,0:T(8,128)(2,1)}, u32[]{:S(2)}) copy-start(bf16[256,128]{1,0:T(8,128)(2,1)} %constant.93.clone) | copy-start | bytes 196612
  8.1 0.9 %copy-start.1 = (bf16[256,128]{1,0:T(8,128)(2,1)S(1)}, bf16[256,128]{1,0:T(8,128)(2,1)}, u32[]{:S(2)}) copy-start(bf16[256,128]{1,0:T(8,128)(2,1)} %constant.91.clone) | copy-start | bytes 196612
  9.0 0.8 %copy-start.4 = (bf16[256,128]{1,0:T(8,128)(2,1)S(1)}, bf16[256,128]{1,0:T(8,128)(2,1)}, u32[]{:S(2)}) copy-start(bf16[256,128]{1,0:T(8,128)(2,1)} %constant.92.clone) | copy-start | bytes 196612
  9.0 0.9 %copy-start.5 = (bf16[256,128]{1,0:T(8,128)(2,1)S(1)}, bf16[256,128]{1,0:T(8,128)(2,1)}, u32[]{:S(2)}) copy-start(bf16[256,128]{1,0:T(8,128)(2,1)} %constant.90.clone) | copy-start | bytes 196612
  11.4 9.1 %collective-permute-start.5 = (bf16[4,16,1408]{2,1,0:T(8,128)(2,1)S(1)}, bf16[4,16,1408]{2,1,0:T(8,128)(2,1)S(1)}, u32[]{:S(2)}, u32[]{:S(2)}) collective-permute-start(bf16[4,16,1408]{2,1,0:T(8,128)(2,1)S(1)} %concatenate.61), channel_id=1, source_target_pairs={{0,16},{8,24},{16,0},{24,8},{1,17},{9,25},{17,1},{25,9},{2,18},{10... | collective-permute-start | bytes 540680 | tf_op jit(solution)/shard_map/ppermute | solution.py:469
  13.0 8.4 %collective-permute-start.6 = (bf16[4,16,1408]{2,1,0:T(8,128)(2,1)S(1)}, bf16[4,16,1408]{2,1,0:T(8,128)(2,1)S(1)}, u32[]{:S(2)}, u32[]{:S(2)}) collective-permute-start(bf16[4,16,1408]{2,1,0:T(8,128)(2,1)S(1)} %concatenate.62), channel_id=1, source_target_pairs={{0,24},{8,16},{16,8},{24,0},{1,25},{9,17},{17,9},{25,1},{2,26},{10... | collective-permute-start | bytes 540680 | tf_op jit(solution)/shard_map/ppermute | solution.py:469
  14.4 7.8 %collective-permute-start.4 = (bf16[4,16,1408]{2,1,0:T(8,128)(2,1)S(1)}, bf16[4,16,1408]{2,1,0:T(8,128)(2,1)S(1)}, u32[]{:S(2)}, u32[]{:S(2)}) collective-permute-start(bf16[4,16,1408]{2,1,0:T(8,128)(2,1)S(1)} %concatenate.60), channel_id=1, source_target_pairs={{0,8},{8,0},{16,24},{24,16},{1,9},{9,1},{17,25},{25,17},{2,10},{10... | collective-permute-start | bytes 540680 | tf_op jit(solution)/shard_map/ppermute | solution.py:469
  15.0 4.1 %collective-permute-start.9 = (bf16[2,16,768]{2,1,0:T(8,128)(2,1)S(1)}, bf16[2,16,768]{2,1,0:T(8,128)(2,1)S(1)}, u32[]{:S(2)}, u32[]{:S(2)}) collective-permute-start(bf16[2,16,768]{2,1,0:T(8,128)(2,1)S(1)} %get-tuple-element.35), channel_id=1, source_target_pairs={{0,2},{1,3},{2,0},{3,1},{4,6},{5,7},{6,4},{7,5},{8,10},{9,11},{10,... | collective-permute-start | bytes 147464 | tf_op jit(solution)/shard_map/ppermute | solution.py:469
  16.8 8.2 %collective-permute-start.7 = (bf16[1,64,1280]{2,1,0:T(8,128)(2,1)S(1)}, bf16[1,64,1280]{2,1,0:T(8,128)(2,1)S(1)}, u32[]{:S(2)}, u32[]{:S(2)}) collective-permute-start(bf16[1,64,1280]{2,1,0:T(8,128)(2,1)S(1)} %bitcast.41), channel_id=1, source_target_pairs={{0,1},{1,0},{2,3},{3,2},{4,5},{5,4},{6,7},{7,6},{8,9},{9,8},{10,11... | collective-permute-start | bytes 491528 | tf_op jit(solution)/shard_map/ppermute | solution.py:469
  19.1 5.6 %collective-permute-start.10 = (bf16[2,2,16,768]{3,2,1,0:T(8,128)(2,1)S(1)}, bf16[2,2,16,768]{3,2,1,0:T(8,128)(2,1)S(1)}, u32[]{:S(2)}, u32[]{:S(2)}) collective-permute-start(bf16[2,2,16,768]{3,2,1,0:T(8,128)(2,1)S(1)} %pad_maximum_fusion.12), channel_id=1, source_target_pairs={{0,4},{1,5},{2,6},{3,7},{4,0},{5,1},{6,2},{7,3},{8,12},{9,13},{10,... | collective-permute-start | bytes 294920 | tf_op jit(solution)/shard_map/ppermute | solution.py:469
  22.2 2.7 %collective-permute-start.8 = (bf16[3,64,1280]{2,1,0:T(8,128)(2,1)S(1)}, bf16[3,64,1280]{2,1,0:T(8,128)(2,1)S(1)}, u32[]{:S(2)}, u32[]{:S(2)}) collective-permute-start(bf16[3,64,1280]{2,1,0:T(8,128)(2,1)S(1)} %pad_maximum_fusion.10), channel_id=1, source_target_pairs={{0,1},{1,0},{2,3},{3,2},{4,5},{5,4},{6,7},{7,6},{8,9},{9,8},{10,11... | collective-permute-start | bytes 1474568 | tf_op jit(solution)/shard_map/ppermute | solution.py:469
  38.2 1.4 %collective-permute-start.11 = (f32[4,32,256]{2,1,0:T(8,128)S(1)}, f32[4,32,256]{2,1,0:T(8,128)S(1)}, u32[]{:S(2)}, u32[]{:S(2)}) collective-permute-start(f32[4,32,256]{2,1,0:T(8,128)S(1)} %get-tuple-element.40), channel_id=1, source_target_pairs={{0,1},{1,0},{2,3},{3,2},{4,5},{5,4},{6,7},{7,6},{8,9},{9,8},{10,11... | collective-permute-start | bytes 393224 | tf_op jit(solution)/shard_map/ppermute | solution.py:469
  39.7 4.3 %collective-permute-start.12 = (f32[4,16,256]{2,1,0:T(8,128)S(1)}, f32[4,16,256]{2,1,0:T(8,128)S(1)}, u32[]{:S(2)}, u32[]{:S(2)}) collective-permute-start(f32[4,16,256]{2,1,0:T(8,128)S(1)} %get-tuple-element.53), channel_id=1, source_target_pairs={{0,2},{1,3},{2,0},{3,1},{4,6},{5,7},{6,4},{7,5},{8,10},{9,11},{10,... | collective-permute-start | bytes 196616 | tf_op jit(solution)/shard_map/ppermute | solution.py:469
  44.0 4.9 %collective-permute-start.15 = (f32[2,16,256]{2,1,0:T(8,128)S(1)}, f32[2,16,256]{2,1,0:T(8,128)S(1)}, u32[]{:S(2)}, u32[]{:S(2)}) collective-permute-start(f32[2,16,256]{2,1,0:T(8,128)S(1)} %get-tuple-element.49), channel_id=1, source_target_pairs={{0,24},{8,16},{16,8},{24,0},{1,25},{9,17},{17,9},{25,1},{2,26},{10... | collective-permute-start | bytes 98312 | tf_op jit(solution)/shard_map/ppermute | solution.py:469
  46.5 3.9 %collective-permute-start.13 = (f32[2,16,256]{2,1,0:T(8,128)S(1)}, f32[2,16,256]{2,1,0:T(8,128)S(1)}, u32[]{:S(2)}, u32[]{:S(2)}) collective-permute-start(f32[2,16,256]{2,1,0:T(8,128)S(1)} %get-tuple-element.51), channel_id=1, source_target_pairs={{0,8},{8,0},{16,24},{24,16},{1,9},{9,1},{17,25},{25,17},{2,10},{10... | collective-permute-start | bytes 98312 | tf_op jit(solution)/shard_map/ppermute | solution.py:469
  47.1 3.9 %collective-permute-start.14 = (f32[2,16,256]{2,1,0:T(8,128)S(1)}, f32[2,16,256]{2,1,0:T(8,128)S(1)}, u32[]{:S(2)}, u32[]{:S(2)}) collective-permute-start(f32[2,16,256]{2,1,0:T(8,128)S(1)} %get-tuple-element.52), channel_id=1, source_target_pairs={{0,16},{8,24},{16,0},{24,8},{1,17},{9,25},{17,1},{25,9},{2,18},{10... | collective-permute-start | bytes 98312 | tf_op jit(solution)/shard_map/ppermute | solution.py:469

commit v4 on v3

--- a/solution.py
+++ b/solution.py
@@ -267,16 +267,16 @@
     return results
 
 
-def series(kind):
+def series(kind, degree):
     nodes = np.cos((np.arange(40) + 0.5) * np.pi / 40) * 8.0 + 8.0
     x = np.sqrt(nodes)
     values = np.cos(PHASE_SCALE * x) if kind == "cos" else np.sin(PHASE_SCALE * x) / x
-    fitted = np.polynomial.chebyshev.Chebyshev.fit(nodes, values, 6, domain=[0.0, 16.0])
+    fitted = np.polynomial.chebyshev.Chebyshev.fit(nodes, values, degree, domain=[0.0, 16.0])
     return [float(v) for v in fitted.convert(kind=np.polynomial.Polynomial).coef]
 
 
-COS_SERIES = series("cos")
-SIN_SERIES = series("sin")
+COS_SERIES = series("cos", 5)
+SIN_SERIES = series("sin", 5)
 
 
 def evaluate(coefficients, x):
@@ -338,11 +338,17 @@
     lane = first + lax.broadcasted_iota(jnp.int32, (1, width), 1)
     inside = (lane >= 0) & (lane < columns)
 
-    turn = 2.0 * math.pi / columns
-    col_phase = turn * (lax.rem(across * lane, columns)).astype(jnp.float32)
-    row_phase = 2.0 * math.pi / rows * (lax.rem(along * row_numbers(0)[:, :1], rows)).astype(jnp.float32)
-    row_cos, row_sin = jnp.cos(row_phase), jnp.sin(row_phase)
-    col_cos, col_sin = jnp.cos(col_phase), jnp.sin(col_phase)
+    def wave(count, period):
+        count = lax.rem(count, period)
+        count = jnp.where(2 * count >= period, count - period, count)
+        count = jnp.where(2 * count < -period, count + period, count)
+        x = 2.0 * math.pi / period * count.astype(jnp.float32)
+        c = evaluate(COS_SERIES, x * x)
+        d = evaluate(SIN_SERIES, x * x) * x
+        return (1.0 - 2.0 * d * d, 2.0 * c * d)
+
+    row_cos, row_sin = wave(along * row_numbers(0)[:, :1], rows)
+    col_cos, col_sin = wave(across * lane, columns)
 
     def read(level, j):
         return (field[level, j, :, :COLBLK], field[level, j, :, COLBLK:])
@@ -495,7 +501,11 @@
         lax.dynamic_slice_in_dim(index_volume[0], (span - cone) * (group ^ k % 2), span + cone, 1)
         for k in range(planes)
     ]
-    far = [far[k] if k == 0 else swap(far[k], "row", 2 * k) for k in range(planes)]
+    far = [
+        far[k] if k == 0 else swap(far[k], "row", 2 * k) if k < planes - 1 else swap(index_volume[0], "row", 2 * k)
+        for k in range(planes)
+    ]
+    far[-1] = lax.dynamic_slice_in_dim(far[-1], (span - cone) * group, span + cone, 1)
     tilts = jnp.stack([angles - TILTS // 2, jnp.mod(3 * angles, TILTS) - TILTS // 2])
     weights, tilts, first_two, far = lax.optimization_barrier(
         (column_weights(*weights), tilts, first_two, far)

time: 51.9 us -> 50.5 us (0.973)
  waiting for transfers between devices: 15.1 us -> 13.7 us
  starting transfers between devices: 17.9 us -> 19.2 us
  local copies, waits for them, and re-layouts: 3.37 us -> 2.52 us
  Pallas kernels: 13.9 us -> 13.3 us
    ppermute x16, waiting for transfers between devices: 15.1 us -> 13.7 us  [swap(): return lax.ppermute(x, axis, [(i, i ^ step) for i in range(size)])]
    ppermute x16, starting transfers between devices: 17.9 us -> 19.2 us  [swap(): return lax.ppermute(x, axis, [(i, i ^ step) for i in range(size)])]
    unnamed x14, local copies, waits for them, and re-layouts: 3.18 us -> 2.31 us
    pallas_call x1, Pallas kernels: 13.2 us -> 12.7 us  [window_body(): pl.pallas_call(functools.partial(sweep, sizes), out_shape=[jax.ShapeDtype...]
  transfers between devices with their start and end apart: 16 -> 16, of which waited for: 12 -> 10; matrix products, arithmetic and copies ran while one was open for 1% -> 1% of each run, Pallas kernels for 0% -> 0%
where the time goes in v4:
time: 50.5 us; the launch traced here: 50.3 us
  starting transfers between devices  19.2 us (38%)
  waiting for transfers between devices  13.7 us (27%)
  Pallas kernels  13.3 us (26%)
  local copies, waits for them, and re-layouts  2.52 us (5%)
  between operations  0.96 us (2%)
    ppermute x16, starting transfers between devices, swap(): return lax.ppermute(x, axis, [(i, i ^ step) for i in range(size)])  19.2 us
    ppermute x16, waiting for transfers between devices, swap(): return lax.ppermute(x, axis, [(i, i ^ step) for i in range(size)])  13.7 us
    pallas_call x1, Pallas kernels, window_body(): pl.pallas_call(functools.partial(sweep, sizes), out_shape=[jax.ShapeDtype...  12.7 us
    unnamed x14, local copies, waits for them, and re-layouts  2.31 us
  transfers between devices with their start and end apart: 16, of which 10 were waited for; matrix products, arithmetic and copies ran while one was open for 1% of the time, Pallas kernels for 0%

profile of v4, /device:TPU:0, one launch (start us, length us, event | category | flops | bytes accessed | tf_op | source)
XLA Modules:
  0.0 50.3 jit_solution(14108468150625690724)
XLA Ops:
  0.0 5.0 %collective-permute-start.3 = (bf16[16,2048]{1,0:T(8,128)(2,1)}, bf16[16,2048]{1,0:T(8,128)(2,1)S(1)}, u32[]{:S(2)}, u32[]{:S(2)}) collective-permute-start(bf16[16,2048]{1,0:T(8,128)(2,1)} %bitcast.47), channel_id=1, source_target_pairs={{0,6},{1,7},{2,4},{3,5},{4,2},{5,3},{6,0},{7,1},{8,14},{9,15},{10,... | collective-permute-start | bytes 196616 | tf_op jit(solution)/shard_map/ppermute | solution.py:475
  5.1 1.4 %collective-permute-start.2 = (bf16[16,1536]{1,0:T(8,128)(2,1)S(1)}, bf16[16,1536]{1,0:T(8,128)(2,1)S(1)}, u32[]{:S(2)}, u32[]{:S(2)}) collective-permute-start(bf16[16,1536]{1,0:T(8,128)(2,1)S(1)} %get-tuple-element.30), channel_id=1, source_target_pairs={{0,4},{1,5},{2,6},{3,7},{4,0},{5,1},{6,2},{7,3},{8,12},{9,13},{10,... | collective-permute-start | bytes 147464 | tf_op jit(solution)/shard_map/ppermute | solution.py:475
  7.3 0.6 %copy-done.6 = s32[2]{0:T(128)S(1)} copy-done((s32[2]{0:T(128)S(1)}, s32[2]{0:T(128)}, u32[]{:S(2)}) %copy-start.6) | copy-done | bytes 32
  8.1 0.8 %copy-done = bf16[256,128]{1,0:T(8,128)(2,1)S(1)} copy-done((bf16[256,128]{1,0:T(8,128)(2,1)S(1)}, bf16[256,128]{1,0:T(8,128)(2,1)}, u32[]{:S(2)}) %copy-start) | copy-done | bytes 65560
  9.0 0.8 %copy-done.5 = bf16[256,128]{1,0:T(8,128)(2,1)S(1)} copy-done((bf16[256,128]{1,0:T(8,128)(2,1)S(1)}, bf16[256,128]{1,0:T(8,128)(2,1)}, u32[]{:S(2)}) %copy-start.5) | copy-done | bytes 65560
  9.9 0.6 %collective-permute-done.2 = bf16[16,1536]{1,0:T(8,128)(2,1)S(1)} collective-permute-done((bf16[16,1536]{1,0:T(8,128)(2,1)S(1)}, bf16[16,1536]{1,0:T(8,128)(2,1)S(1)}, u32[]{:S(2)}, u32[]{:S(2)}) %collective-permute-start.2) | collective-permute-done | bytes 49184 | tf_op jit(solution)/shard_map/ppermute | solution.py:475
  10.6 1.6 %collective-permute-start.5 = (bf16[4,16,1408]{2,1,0:T(8,128)(2,1)S(1)}, bf16[4,16,1408]{2,1,0:T(8,128)(2,1)S(1)}, u32[]{:S(2)}, u32[]{:S(2)}) collective-permute-start(bf16[4,16,1408]{2,1,0:T(8,128)(2,1)S(1)} %concatenate.61), channel_id=1, source_target_pairs={{0,16},{8,24},{16,0},{24,8},{1,17},{9,25},{17,1},{25,9},{2,18},{10... | collective-permute-start | bytes 540680 | tf_op jit(solution)/shard_map/ppermute | solution.py:475
  12.1 1.4 %collective-permute-start.6 = (bf16[4,16,1408]{2,1,0:T(8,128)(2,1)S(1)}, bf16[4,16,1408]{2,1,0:T(8,128)(2,1)S(1)}, u32[]{:S(2)}, u32[]{:S(2)}) collective-permute-start(bf16[4,16,1408]{2,1,0:T(8,128)(2,1)S(1)} %concatenate.62), channel_id=1, source_target_pairs={{0,24},{8,16},{16,8},{24,0},{1,25},{9,17},{17,9},{25,1},{2,26},{10... | collective-permute-start | bytes 540680 | tf_op jit(solution)/shard_map/ppermute | solution.py:475
  13.6 0.6 %collective-permute-start.4 = (bf16[4,16,1408]{2,1,0:T(8,128)(2,1)S(1)}, bf16[4,16,1408]{2,1,0:T(8,128)(2,1)S(1)}, u32[]{:S(2)}, u32[]{:S(2)}) collective-permute-start(bf16[4,16,1408]{2,1,0:T(8,128)(2,1)S(1)} %concatenate.60), channel_id=1, source_target_pairs={{0,8},{8,0},{16,24},{24,16},{1,9},{9,1},{17,25},{25,17},{2,10},{10... | collective-permute-start | bytes 540680 | tf_op jit(solution)/shard_map/ppermute | solution.py:475
  14.2 1.7 %collective-permute-start.9 = (bf16[2,16,768]{2,1,0:T(8,128)(2,1)S(1)}, bf16[2,16,768]{2,1,0:T(8,128)(2,1)S(1)}, u32[]{:S(2)}, u32[]{:S(2)}) collective-permute-start(bf16[2,16,768]{2,1,0:T(8,128)(2,1)S(1)} %get-tuple-element.35), channel_id=1, source_target_pairs={{0,2},{1,3},{2,0},{3,1},{4,6},{5,7},{6,4},{7,5},{8,10},{9,11},{10,... | collective-permute-start | bytes 147464 | tf_op jit(solution)/shard_map/ppermute | solution.py:475
  15.9 2.3 %collective-permute-done.9 = bf16[2,16,768]{2,1,0:T(8,128)(2,1)S(1)} collective-permute-done((bf16[2,16,768]{2,1,0:T(8,128)(2,1)S(1)}, bf16[2,16,768]{2,1,0:T(8,128)(2,1)S(1)}, u32[]{:S(2)}, u32[]{:S(2)}) %collective-permute-start.9) | collective-permute-done | bytes 49184 | tf_op jit(solution)/shard_map/ppermute | solution.py:475
  18.3 1.8 %collective-permute-start.10 = (bf16[2,2,16,768]{3,2,1,0:T(8,128)(2,1)S(1)}, bf16[2,2,16,768]{3,2,1,0:T(8,128)(2,1)S(1)}, u32[]{:S(2)}, u32[]{:S(2)}) collective-permute-start(bf16[2,2,16,768]{3,2,1,0:T(8,128)(2,1)S(1)} %pad_maximum_fusion.12), channel_id=1, source_target_pairs={{0,4},{1,5},{2,6},{3,7},{4,0},{5,1},{6,2},{7,3},{8,12},{9,13},{10,... | collective-permute-start | bytes 294920 | tf_op jit(solution)/shard_map/ppermute | solution.py:475
  20.0 0.8 %collective-permute-done.5 = bf16[4,16,1408]{2,1,0:T(8,128)(2,1)S(1)} collective-permute-done((bf16[4,16,1408]{2,1,0:T(8,128)(2,1)S(1)}, bf16[4,16,1408]{2,1,0:T(8,128)(2,1)S(1)}, u32[]{:S(2)}, u32[]{:S(2)}) %collective-permute-start.5) | collective-permute-done | bytes 180256 | tf_op jit(solution)/shard_map/ppermute | solution.py:475
  20.9 1.2 %collective-permute-done.4 = bf16[4,16,1408]{2,1,0:T(8,128)(2,1)S(1)} collective-permute-done((bf16[4,16,1408]{2,1,0:T(8,128)(2,1)S(1)}, bf16[4,16,1408]{2,1,0:T(8,128)(2,1)S(1)}, u32[]{:S(2)}, u32[]{:S(2)}) %collective-permute-start.4) | collective-permute-done | bytes 180256 | tf_op jit(solution)/shard_map/ppermute | solution.py:475
  22.2 1.6 %collective-permute-done.10 = bf16[2,2,16,768]{3,2,1,0:T(8,128)(2,1)S(1)} collective-permute-done((bf16[2,2,16,768]{3,2,1,0:T(8,128)(2,1)S(1)}, bf16[2,2,16,768]{3,2,1,0:T(8,128)(2,1)S(1)}, u32[]{:S(2)}, u32[]{:S(2)}) %collective-permute-start.10) | collective-permute-done | bytes 98336 | tf_op jit(solution)/shard_map/ppermute | solution.py:475
  24.2 12.7 %shard_map.82 = (f32[4,32,256]{2,1,0:T(8,128)S(1)}, f32[4,32,256]{2,1,0:T(8,128)S(1)}) custom-call(s32[2,2]{1,0:T(2,128)S(1)} %pad_add_fusion.tilts, bf16[4,16,128]{2,1,0:T(8,128)(2,1)S(1)} %pad_maximum_fusion.14.tiles, bf16[4,64,1280]{2,1,0:T(8,128)(2,1)S(1)} %pad_maximum_fusion.8.own, bf16[4,64,1280]{2,1,0:T(8,128)(2,1)S(1)} %pad_maximum_fusion.9.other, ...), custom_call_target="tpu_custom_call" | custom-call | tf_op jit(solution)/shard_map/pallas_call | solution.py:532
  37.0 1.2 %collective-permute-done.11 = f32[4,32,256]{2,1,0:T(8,128)S(1)} collective-permute-done((f32[4,32,256]{2,1,0:T(8,128)S(1)}, f32[4,32,256]{2,1,0:T(8,128)S(1)}, u32[]{:S(2)}, u32[]{:S(2)}) %collective-permute-start.11) | collective-permute-done | bytes 131104 | tf_op jit(solution)/shard_map/ppermute | solution.py:475
  38.3 1.8 %collective-permute-start.12 = (f32[4,16,256]{2,1,0:T(8,128)S(1)}, f32[4,16,256]{2,1,0:T(8,128)S(1)}, u32[]{:S(2)}, u32[]{:S(2)}) collective-permute-start(f32[4,16,256]{2,1,0:T(8,128)S(1)} %get-tuple-element.53), channel_id=1, source_target_pairs={{0,2},{1,3},{2,0},{3,1},{4,6},{5,7},{6,4},{7,5},{8,10},{9,11},{10,... | collective-permute-start | bytes 196616 | tf_op jit(solution)/shard_map/ppermute | solution.py:475
  40.1 2.5 %collective-permute-done.12 = f32[4,16,256]{2,1,0:T(8,128)S(1)} collective-permute-done((f32[4,16,256]{2,1,0:T(8,128)S(1)}, f32[4,16,256]{2,1,0:T(8,128)S(1)}, u32[]{:S(2)}, u32[]{:S(2)}) %collective-permute-start.12) | collective-permute-done | bytes 65568 | tf_op jit(solution)/shard_map/ppermute | solution.py:475
  42.6 2.5 %collective-permute-start.15 = (f32[2,16,256]{2,1,0:T(8,128)S(1)}, f32[2,16,256]{2,1,0:T(8,128)S(1)}, u32[]{:S(2)}, u32[]{:S(2)}) collective-permute-start(f32[2,16,256]{2,1,0:T(8,128)S(1)} %get-tuple-element.49), channel_id=1, source_target_pairs={{0,24},{8,16},{16,8},{24,0},{1,25},{9,17},{17,9},{25,1},{2,26},{10... | collective-permute-start | bytes 98312 | tf_op jit(solution)/shard_map/ppermute | solution.py:475
  45.2 0.5 %collective-permute-start.13 = (f32[2,16,256]{2,1,0:T(8,128)S(1)}, f32[2,16,256]{2,1,0:T(8,128)S(1)}, u32[]{:S(2)}, u32[]{:S(2)}) collective-permute-start(f32[2,16,256]{2,1,0:T(8,128)S(1)} %get-tuple-element.51), channel_id=1, source_target_pairs={{0,8},{8,0},{16,24},{24,16},{1,9},{9,1},{17,25},{25,17},{2,10},{10... | collective-permute-start | bytes 98312 | tf_op jit(solution)/shard_map/ppermute | solution.py:475
  46.2 1.3 %collective-permute-done.15.refs_3_ = f32[2,16,256]{2,1,0:T(8,128)S(1)} collective-permute-done((f32[2,16,256]{2,1,0:T(8,128)S(1)}, f32[2,16,256]{2,1,0:T(8,128)S(1)}, u32[]{:S(2)}, u32[]{:S(2)}) %collective-permute-start.15) | collective-permute-done | bytes 32800 | tf_op jit(solution)/shard_map/ppermute | solution.py:475
  47.5 1.5 %collective-permute-done.13.refs_1_ = f32[2,16,256]{2,1,0:T(8,128)S(1)} collective-permute-done((f32[2,16,256]{2,1,0:T(8,128)S(1)}, f32[2,16,256]{2,1,0:T(8,128)S(1)}, u32[]{:S(2)}, u32[]{:S(2)}) %collective-permute-start.13) | collective-permute-done | bytes 32800 | tf_op jit(solution)/shard_map/ppermute | solution.py:475
  49.6 0.7 %shard_map.83 = f32[1,16,2048]{2,1,0:T(8,128)} custom-call(f32[2,16,256]{2,1,0:T(8,128)S(1)} %get-tuple-element.50.refs_0_, f32[2,16,256]{2,1,0:T(8,128)S(1)} %collective-permute-done.13.refs_1_, f32[2,16,256]{2,1,0:T(8,128)S(1)} %collective-permute-done.14.refs_2_, f32[2,16,256]{2,1,0:T(8,128)S(1)} %collective-permute-done.15.refs_3_), custom_call_target="tpu_custom_call" | custom-call | tf_op jit(solution)/shard_map/pallas_call | solution.py:549
  (54 shorter events, 2.2 us)
Async XLA Ops:
  0.0 5.1 %copy-start.2 = (bf16[1,16,2048]{2,1,0:T(8,128)(2,1)S(1)}, bf16[1,16,2048]{2,1,0:T(8,128)(2,1)}, u32[]{:S(2)}) copy-start(bf16[1,16,2048]{2,1,0:T(8,128)(2,1)} %param.8) | copy-start | bytes 196612
  0.0 8.9 %collective-permute-start.3 = (bf16[16,2048]{1,0:T(8,128)(2,1)}, bf16[16,2048]{1,0:T(8,128)(2,1)S(1)}, u32[]{:S(2)}, u32[]{:S(2)}) collective-permute-start(bf16[16,2048]{1,0:T(8,128)(2,1)} %bitcast.47), channel_id=1, source_target_pairs={{0,6},{1,7},{2,4},{3,5},{4,2},{5,3},{6,0},{7,1},{8,14},{9,15},{10,... | collective-permute-start | bytes 196616 | tf_op jit(solution)/shard_map/ppermute | solution.py:475
  5.1 1.5 %copy-start.3 = (bf16[2,16,2048]{2,1,0:T(8,128)(2,1)S(1)}, bf16[2,16,2048]{2,1,0:T(8,128)(2,1)}, u32[]{:S(2)}) copy-start(bf16[2,16,2048]{2,1,0:T(8,128)(2,1)} %param.11) | copy-start | bytes 393220
  5.1 4.8 %collective-permute-start.1 = (bf16[16,1536]{1,0:T(8,128)(2,1)S(1)}, bf16[16,1536]{1,0:T(8,128)(2,1)S(1)}, u32[]{:S(2)}, u32[]{:S(2)}) collective-permute-start(bf16[16,1536]{1,0:T(8,128)(2,1)S(1)} %get-tuple-element.57), channel_id=1, source_target_pairs={{0,2},{1,3},{2,0},{3,1},{4,6},{5,7},{6,4},{7,5},{8,10},{9,11},{10,... | collective-permute-start | bytes 147464 | tf_op jit(solution)/shard_map/ppermute | solution.py:475
  5.1 5.3 %collective-permute-start.2 = (bf16[16,1536]{1,0:T(8,128)(2,1)S(1)}, bf16[16,1536]{1,0:T(8,128)(2,1)S(1)}, u32[]{:S(2)}, u32[]{:S(2)}) collective-permute-start(bf16[16,1536]{1,0:T(8,128)(2,1)S(1)} %get-tuple-element.30), channel_id=1, source_target_pairs={{0,4},{1,5},{2,6},{3,7},{4,0},{5,1},{6,2},{7,3},{8,12},{9,13},{10,... | collective-permute-start | bytes 147464 | tf_op jit(solution)/shard_map/ppermute | solution.py:475
  6.5 1.4 %collective-permute-start = (bf16[16,2048]{1,0:T(8,128)(2,1)S(1)}, bf16[16,2048]{1,0:T(8,128)(2,1)S(1)}, u32[]{:S(2)}, u32[]{:S(2)}) collective-permute-start(bf16[16,2048]{1,0:T(8,128)(2,1)S(1)} %get-tuple-element.56), channel_id=1, source_target_pairs={{0,1},{1,0},{2,3},{3,2},{4,5},{5,4},{6,7},{7,6},{8,9},{9,8},{10,11... | collective-permute-start | bytes 196616 | tf_op jit(solution)/shard_map/ppermute | solution.py:475
  7.3 0.7 %copy-start.6 = (s32[2]{0:T(128)S(1)}, s32[2]{0:T(128)}, u32[]{:S(2)}) copy-start(s32[2]{0:T(128)} %param.9) | copy-start | bytes 28
  8.0 0.8 %copy-start = (bf16[256,128]{1,0:T(8,128)(2,1)S(1)}, bf16[256,128]{1,0:T(8,128)(2,1)}, u32[]{:S(2)}) copy-start(bf16[256,128]{1,0:T(8,128)(2,1)} %constant.93.clone) | copy-start | bytes 196612
  8.0 0.9 %copy-start.1 = (bf16[256,128]{1,0:T(8,128)(2,1)S(1)}, bf16[256,128]{1,0:T(8,128)(2,1)}, u32[]{:S(2)}) copy-start(bf16[256,128]{1,0:T(8,128)(2,1)} %constant.91.clone) | copy-start | bytes 196612
  8.9 0.8 %copy-start.5 = (bf16[256,128]{1,0:T(8,128)(2,1)S(1)}, bf16[256,128]{1,0:T(8,128)(2,1)}, u32[]{:S(2)}) copy-start(bf16[256,128]{1,0:T(8,128)(2,1)} %constant.90.clone) | copy-start | bytes 196612
  8.9 0.9 %copy-start.4 = (bf16[256,128]{1,0:T(8,128)(2,1)S(1)}, bf16[256,128]{1,0:T(8,128)(2,1)}, u32[]{:S(2)}) copy-start(bf16[256,128]{1,0:T(8,128)(2,1)} %constant.92.clone) | copy-start | bytes 196612
  10.6 10.3 %collective-permute-start.5 = (bf16[4,16,1408]{2,1,0:T(8,128)(2,1)S(1)}, bf16[4,16,1408]{2,1,0:T(8,128)(2,1)S(1)}, u32[]{:S(2)}, u32[]{:S(2)}) collective-permute-start(bf16[4,16,1408]{2,1,0:T(8,128)(2,1)S(1)} %concatenate.61), channel_id=1, source_target_pairs={{0,16},{8,24},{16,0},{24,8},{1,17},{9,25},{17,1},{25,9},{2,18},{10... | collective-permute-start | bytes 540680 | tf_op jit(solution)/shard_map/ppermute | solution.py:475
  12.1 8.7 %collective-permute-start.6 = (bf16[4,16,1408]{2,1,0:T(8,128)(2,1)S(1)}, bf16[4,16,1408]{2,1,0:T(8,128)(2,1)S(1)}, u32[]{:S(2)}, u32[]{:S(2)}) collective-permute-start(bf16[4,16,1408]{2,1,0:T(8,128)(2,1)S(1)} %concatenate.62), channel_id=1, source_target_pairs={{0,24},{8,16},{16,8},{24,0},{1,25},{9,17},{17,9},{25,1},{2,26},{10... | collective-permute-start | bytes 540680 | tf_op jit(solution)/shard_map/ppermute | solution.py:475
  13.6 8.5 %collective-permute-start.4 = (bf16[4,16,1408]{2,1,0:T(8,128)(2,1)S(1)}, bf16[4,16,1408]{2,1,0:T(8,128)(2,1)S(1)}, u32[]{:S(2)}, u32[]{:S(2)}) collective-permute-start(bf16[4,16,1408]{2,1,0:T(8,128)(2,1)S(1)} %concatenate.60), channel_id=1, source_target_pairs={{0,8},{8,0},{16,24},{24,16},{1,9},{9,1},{17,25},{25,17},{2,10},{10... | collective-permute-start | bytes 540680 | tf_op jit(solution)/shard_map/ppermute | solution.py:475
  14.2 4.1 %collective-permute-start.9 = (bf16[2,16,768]{2,1,0:T(8,128)(2,1)S(1)}, bf16[2,16,768]{2,1,0:T(8,128)(2,1)S(1)}, u32[]{:S(2)}, u32[]{:S(2)}) collective-permute-start(bf16[2,16,768]{2,1,0:T(8,128)(2,1)S(1)} %get-tuple-element.35), channel_id=1, source_target_pairs={{0,2},{1,3},{2,0},{3,1},{4,6},{5,7},{6,4},{7,5},{8,10},{9,11},{10,... | collective-permute-start | bytes 147464 | tf_op jit(solution)/shard_map/ppermute | solution.py:475
  15.9 8.2 %collective-permute-start.7 = (bf16[1,64,1280]{2,1,0:T(8,128)(2,1)S(1)}, bf16[1,64,1280]{2,1,0:T(8,128)(2,1)S(1)}, u32[]{:S(2)}, u32[]{:S(2)}) collective-permute-start(bf16[1,64,1280]{2,1,0:T(8,128)(2,1)S(1)} %bitcast.42), channel_id=1, source_target_pairs={{0,1},{1,0},{2,3},{3,2},{4,5},{5,4},{6,7},{7,6},{8,9},{9,8},{10,11... | collective-permute-start | bytes 491528 | tf_op jit(solution)/shard_map/ppermute | solution.py:475
  18.3 5.6 %collective-permute-start.10 = (bf16[2,2,16,768]{3,2,1,0:T(8,128)(2,1)S(1)}, bf16[2,2,16,768]{3,2,1,0:T(8,128)(2,1)S(1)}, u32[]{:S(2)}, u32[]{:S(2)}) collective-permute-start(bf16[2,2,16,768]{3,2,1,0:T(8,128)(2,1)S(1)} %pad_maximum_fusion.12), channel_id=1, source_target_pairs={{0,4},{1,5},{2,6},{3,7},{4,0},{5,1},{6,2},{7,3},{8,12},{9,13},{10,... | collective-permute-start | bytes 294920 | tf_op jit(solution)/shard_map/ppermute | solution.py:475
  22.2 1.9 %collective-permute-start.8 = (bf16[3,64,1280]{2,1,0:T(8,128)(2,1)S(1)}, bf16[3,64,1280]{2,1,0:T(8,128)(2,1)S(1)}, u32[]{:S(2)}, u32[]{:S(2)}) collective-permute-start(bf16[3,64,1280]{2,1,0:T(8,128)(2,1)S(1)} %pad_maximum_fusion.10), channel_id=1, source_target_pairs={{0,1},{1,0},{2,3},{3,2},{4,5},{5,4},{6,7},{7,6},{8,9},{9,8},{10,11... | collective-permute-start | bytes 1474568 | tf_op jit(solution)/shard_map/ppermute | solution.py:475
  36.8 1.4 %collective-permute-start.11 = (f32[4,32,256]{2,1,0:T(8,128)S(1)}, f32[4,32,256]{2,1,0:T(8,128)S(1)}, u32[]{:S(2)}, u32[]{:S(2)}) collective-permute-start(f32[4,32,256]{2,1,0:T(8,128)S(1)} %get-tuple-element.40), channel_id=1, source_target_pairs={{0,1},{1,0},{2,3},{3,2},{4,5},{5,4},{6,7},{7,6},{8,9},{9,8},{10,11... | collective-permute-start | bytes 393224 | tf_op jit(solution)/shard_map/ppermute | solution.py:475
  38.3 4.3 %collective-permute-start.12 = (f32[4,16,256]{2,1,0:T(8,128)S(1)}, f32[4,16,256]{2,1,0:T(8,128)S(1)}, u32[]{:S(2)}, u32[]{:S(2)}) collective-permute-start(f32[4,16,256]{2,1,0:T(8,128)S(1)} %get-tuple-element.53), channel_id=1, source_target_pairs={{0,2},{1,3},{2,0},{3,1},{4,6},{5,7},{6,4},{7,5},{8,10},{9,11},{10,... | collective-permute-start | bytes 196616 | tf_op jit(solution)/shard_map/ppermute | solution.py:475
  42.6 4.9 %collective-permute-start.15 = (f32[2,16,256]{2,1,0:T(8,128)S(1)}, f32[2,16,256]{2,1,0:T(8,128)S(1)}, u32[]{:S(2)}, u32[]{:S(2)}) collective-permute-start(f32[2,16,256]{2,1,0:T(8,128)S(1)} %get-tuple-element.49), channel_id=1, source_target_pairs={{0,24},{8,16},{16,8},{24,0},{1,25},{9,17},{17,9},{25,1},{2,26},{10... | collective-permute-start | bytes 98312 | tf_op jit(solution)/shard_map/ppermute | solution.py:475
  45.2 3.9 %collective-permute-start.13 = (f32[2,16,256]{2,1,0:T(8,128)S(1)}, f32[2,16,256]{2,1,0:T(8,128)S(1)}, u32[]{:S(2)}, u32[]{:S(2)}) collective-permute-start(f32[2,16,256]{2,1,0:T(8,128)S(1)} %get-tuple-element.51), channel_id=1, source_target_pairs={{0,8},{8,0},{16,24},{24,16},{1,9},{9,1},{17,25},{25,17},{2,10},{10... | collective-permute-start | bytes 98312 | tf_op jit(solution)/shard_map/ppermute | solution.py:475
  45.7 3.9 %collective-permute-start.14 = (f32[2,16,256]{2,1,0:T(8,128)S(1)}, f32[2,16,256]{2,1,0:T(8,128)S(1)}, u32[]{:S(2)}, u32[]{:S(2)}) collective-permute-start(f32[2,16,256]{2,1,0:T(8,128)S(1)} %get-tuple-element.52), channel_id=1, source_target_pairs={{0,16},{8,24},{16,0},{24,8},{1,17},{9,25},{17,1},{25,9},{2,18},{10... | collective-permute-start | bytes 98312 | tf_op jit(solution)/shard_map/ppermute | solution.py:475

commit v5 on v4

--- a/solution.py
+++ b/solution.py
@@ -347,7 +347,7 @@
         d = evaluate(SIN_SERIES, x * x) * x
         return (1.0 - 2.0 * d * d, 2.0 * c * d)
 
-    row_cos, row_sin = wave(along * row_numbers(0)[:, :1], rows)
+    row_cos, row_sin = wave(along * rows_of, rows)
     col_cos, col_sin = wave(across * lane, columns)
 
     def read(level, j):
@@ -374,16 +374,29 @@
     def pairs(n):
         return [range(j, min(j + 2, n)) for j in range(0, n, 2)]
 
+    low_half = lax.broadcasted_iota(jnp.int32, (rows, COLBLK), 1) < HALFCOL
+
     def forward(s):
         factor = split(complex_form(*factors[s]))
         slot = place ^ s
+
+        def index_block(b):
+            cols = slice(b * COLBLK, (b + 1) * COLBLK)
+            x = jnp.concatenate([r[slot, :, cols] for r in (own, other)], axis=0).astype(jnp.float32)
+            return pltpu.roll(x, HALFCOL, 1) if s % 2 else x
+
+        ahead = index_block(s // 2)
         last = None
         for group in pairs(blocks - s):
             turned = []
             for j in group:
                 begin = s * HALFCOL + j * COLBLK
-                x = jnp.concatenate([r[slot, :, begin : begin + COLBLK] for r in (own, other)], axis=0)
-                x = x.astype(jnp.float32)
+                x = ahead
+                if s % 2:
+                    ahead = index_block(s // 2 + j + 1)
+                    x = jnp.where(low_half, x, ahead)
+                elif j + 1 < blocks - s:
+                    ahead = index_block(s // 2 + j + 1)
                 square = x * x
                 seen = inside[:, begin : begin + COLBLK]
                 c = jnp.where(seen, evaluate(COS_SERIES, square), 0.0)
@@ -399,10 +412,10 @@
                     a, b = read(s - 1, j)
                 a, b = c * a - d * b, c * b + d * a
                 start = (2 * slices - s) * HALFCOL - j * COLBLK
-                lo, hi = max(start, 0), min(start + broad, COLBLK)
-                if lo < hi:
-                    kept[s, :rows, lo - start : hi - start] = a[:, lo:hi]
-                    kept[s, rows:, lo - start : hi - start] = b[:, lo:hi]
+                later = j - (slices - s)
+                if max(start, 0) < min(start + broad, COLBLK):
+                    kept[s, later, :rows] = a
+                    kept[s, later, rows:] = b
                 turned.append((a, b))
             for j, v in zip(group, mix_rows(factor, turned)):
                 parts = operand(*v)
@@ -438,8 +451,7 @@
                 start = s * HALFCOL - j * COLBLK
                 lo, hi = max(start, 0), min(start + broad, COLBLK)
                 if lo < hi:
-                    y = kept[s, :, lo - start : hi - start]
-                    part = PHASE_SCALE * (y[:rows] * b[:, lo:hi] - y[rows:] * a[:, lo:hi])
+                    part = PHASE_SCALE * (kept[s, j, :rows] * b - kept[s, j, rows:] * a)[:, lo:hi]
                     mine[place ^ s, :, lo - start : hi - start] = part[: 2 * height]
                     theirs[place ^ s, :, lo - start : hi - start] = part[half : half + 2 * height]
                 if s > 0:
@@ -538,7 +550,7 @@
             pltpu.VMEM((slices, rows, width), jnp.float32),
             pltpu.VMEM((slices, rows, width), jnp.float32),
             pltpu.VMEM((2 * slices, blocks - 1, rows, 2 * COLBLK), jnp.float32),
-            pltpu.VMEM((slices, 2 * rows, broad), jnp.float32),
+            pltpu.VMEM((slices, slices - 1 + broad // COLBLK, 2 * rows, COLBLK), jnp.float32),
         ],
         compiler_params=pltpu.CompilerParams(vmem_limit_bytes=40 * 1024 * 1024),
     )(tilts, tiles, own, other, seen, *weights)

time: 50.5 us -> 49.7 us (0.984)
  Pallas kernels: 13.3 us -> 12.6 us
    pallas_call x1, Pallas kernels: 12.7 us -> 11.9 us  [window_body(): pl.pallas_call(functools.partial(sweep, sizes), out_shape=[jax.ShapeDtype...]
where the time goes in v5:
time: 49.7 us; the launch traced here: 49.5 us
  starting transfers between devices  19.3 us (39%)
  waiting for transfers between devices  13.7 us (28%)
  Pallas kernels  12.6 us (25%)
  local copies, waits for them, and re-layouts  2.52 us (5%)
  between operations  0.96 us (2%)
    ppermute x16, starting transfers between devices, swap(): return lax.ppermute(x, axis, [(i, i ^ step) for i in range(size)])  19.3 us
    ppermute x16, waiting for transfers between devices, swap(): return lax.ppermute(x, axis, [(i, i ^ step) for i in range(size)])  13.7 us
    pallas_call x1, Pallas kernels, window_body(): pl.pallas_call(functools.partial(sweep, sizes), out_shape=[jax.ShapeDtype...  11.9 us
    unnamed x14, local copies, waits for them, and re-layouts  2.31 us
  transfers between devices with their start and end apart: 16, of which 10 were waited for; matrix products, arithmetic and copies ran while one was open for 1% of the time, Pallas kernels for 0%

profile of v5, /device:TPU:0, one launch (start us, length us, event | category | flops | bytes accessed | tf_op | source)
XLA Modules:
  0.0 49.5 jit_solution(12738834415169006153)
XLA Ops:
  0.0 5.0 %collective-permute-start.3 = (bf16[16,2048]{1,0:T(8,128)(2,1)}, bf16[16,2048]{1,0:T(8,128)(2,1)S(1)}, u32[]{:S(2)}, u32[]{:S(2)}) collective-permute-start(bf16[16,2048]{1,0:T(8,128)(2,1)} %bitcast.47), channel_id=1, source_target_pairs={{0,6},{1,7},{2,4},{3,5},{4,2},{5,3},{6,0},{7,1},{8,14},{9,15},{10,... | collective-permute-start | bytes 196616 | tf_op jit(solution)/shard_map/ppermute | solution.py:487
  5.1 1.4 %collective-permute-start.2 = (bf16[16,1536]{1,0:T(8,128)(2,1)S(1)}, bf16[16,1536]{1,0:T(8,128)(2,1)S(1)}, u32[]{:S(2)}, u32[]{:S(2)}) collective-permute-start(bf16[16,1536]{1,0:T(8,128)(2,1)S(1)} %get-tuple-element.30), channel_id=1, source_target_pairs={{0,4},{1,5},{2,6},{3,7},{4,0},{5,1},{6,2},{7,3},{8,12},{9,13},{10,... | collective-permute-start | bytes 147464 | tf_op jit(solution)/shard_map/ppermute | solution.py:487
  7.3 0.6 %copy-done.6 = s32[2]{0:T(128)S(1)} copy-done((s32[2]{0:T(128)S(1)}, s32[2]{0:T(128)}, u32[]{:S(2)}) %copy-start.6) | copy-done | bytes 32
  8.1 0.8 %copy-done = bf16[256,128]{1,0:T(8,128)(2,1)S(1)} copy-done((bf16[256,128]{1,0:T(8,128)(2,1)S(1)}, bf16[256,128]{1,0:T(8,128)(2,1)}, u32[]{:S(2)}) %copy-start) | copy-done | bytes 65560
  9.0 0.8 %copy-done.5 = bf16[256,128]{1,0:T(8,128)(2,1)S(1)} copy-done((bf16[256,128]{1,0:T(8,128)(2,1)S(1)}, bf16[256,128]{1,0:T(8,128)(2,1)}, u32[]{:S(2)}) %copy-start.5) | copy-done | bytes 65560
  9.9 0.6 %collective-permute-done.2 = bf16[16,1536]{1,0:T(8,128)(2,1)S(1)} collective-permute-done((bf16[16,1536]{1,0:T(8,128)(2,1)S(1)}, bf16[16,1536]{1,0:T(8,128)(2,1)S(1)}, u32[]{:S(2)}, u32[]{:S(2)}) %collective-permute-start.2) | collective-permute-done | bytes 49184 | tf_op jit(solution)/shard_map/ppermute | solution.py:487
  10.6 1.6 %collective-permute-start.5 = (bf16[4,16,1408]{2,1,0:T(8,128)(2,1)S(1)}, bf16[4,16,1408]{2,1,0:T(8,128)(2,1)S(1)}, u32[]{:S(2)}, u32[]{:S(2)}) collective-permute-start(bf16[4,16,1408]{2,1,0:T(8,128)(2,1)S(1)} %concatenate.61), channel_id=1, source_target_pairs={{0,16},{8,24},{16,0},{24,8},{1,17},{9,25},{17,1},{25,9},{2,18},{10... | collective-permute-start | bytes 540680 | tf_op jit(solution)/shard_map/ppermute | solution.py:487
  12.1 1.4 %collective-permute-start.6 = (bf16[4,16,1408]{2,1,0:T(8,128)(2,1)S(1)}, bf16[4,16,1408]{2,1,0:T(8,128)(2,1)S(1)}, u32[]{:S(2)}, u32[]{:S(2)}) collective-permute-start(bf16[4,16,1408]{2,1,0:T(8,128)(2,1)S(1)} %concatenate.62), channel_id=1, source_target_pairs={{0,24},{8,16},{16,8},{24,0},{1,25},{9,17},{17,9},{25,1},{2,26},{10... | collective-permute-start | bytes 540680 | tf_op jit(solution)/shard_map/ppermute | solution.py:487
  13.6 0.6 %collective-permute-start.4 = (bf16[4,16,1408]{2,1,0:T(8,128)(2,1)S(1)}, bf16[4,16,1408]{2,1,0:T(8,128)(2,1)S(1)}, u32[]{:S(2)}, u32[]{:S(2)}) collective-permute-start(bf16[4,16,1408]{2,1,0:T(8,128)(2,1)S(1)} %concatenate.60), channel_id=1, source_target_pairs={{0,8},{8,0},{16,24},{24,16},{1,9},{9,1},{17,25},{25,17},{2,10},{10... | collective-permute-start | bytes 540680 | tf_op jit(solution)/shard_map/ppermute | solution.py:487
  14.2 1.7 %collective-permute-start.9 = (bf16[2,16,768]{2,1,0:T(8,128)(2,1)S(1)}, bf16[2,16,768]{2,1,0:T(8,128)(2,1)S(1)}, u32[]{:S(2)}, u32[]{:S(2)}) collective-permute-start(bf16[2,16,768]{2,1,0:T(8,128)(2,1)S(1)} %get-tuple-element.35), channel_id=1, source_target_pairs={{0,2},{1,3},{2,0},{3,1},{4,6},{5,7},{6,4},{7,5},{8,10},{9,11},{10,... | collective-permute-start | bytes 147464 | tf_op jit(solution)/shard_map/ppermute | solution.py:487
  15.9 2.3 %collective-permute-done.9 = bf16[2,16,768]{2,1,0:T(8,128)(2,1)S(1)} collective-permute-done((bf16[2,16,768]{2,1,0:T(8,128)(2,1)S(1)}, bf16[2,16,768]{2,1,0:T(8,128)(2,1)S(1)}, u32[]{:S(2)}, u32[]{:S(2)}) %collective-permute-start.9) | collective-permute-done | bytes 49184 | tf_op jit(solution)/shard_map/ppermute | solution.py:487
  18.3 1.8 %collective-permute-start.10 = (bf16[2,2,16,768]{3,2,1,0:T(8,128)(2,1)S(1)}, bf16[2,2,16,768]{3,2,1,0:T(8,128)(2,1)S(1)}, u32[]{:S(2)}, u32[]{:S(2)}) collective-permute-start(bf16[2,2,16,768]{3,2,1,0:T(8,128)(2,1)S(1)} %pad_maximum_fusion.12), channel_id=1, source_target_pairs={{0,4},{1,5},{2,6},{3,7},{4,0},{5,1},{6,2},{7,3},{8,12},{9,13},{10,... | collective-permute-start | bytes 294920 | tf_op jit(solution)/shard_map/ppermute | solution.py:487
  20.0 0.8 %collective-permute-done.5 = bf16[4,16,1408]{2,1,0:T(8,128)(2,1)S(1)} collective-permute-done((bf16[4,16,1408]{2,1,0:T(8,128)(2,1)S(1)}, bf16[4,16,1408]{2,1,0:T(8,128)(2,1)S(1)}, u32[]{:S(2)}, u32[]{:S(2)}) %collective-permute-start.5) | collective-permute-done | bytes 180256 | tf_op jit(solution)/shard_map/ppermute | solution.py:487
  20.9 1.2 %collective-permute-done.4 = bf16[4,16,1408]{2,1,0:T(8,128)(2,1)S(1)} collective-permute-done((bf16[4,16,1408]{2,1,0:T(8,128)(2,1)S(1)}, bf16[4,16,1408]{2,1,0:T(8,128)(2,1)S(1)}, u32[]{:S(2)}, u32[]{:S(2)}) %collective-permute-start.4) | collective-permute-done | bytes 180256 | tf_op jit(solution)/shard_map/ppermute | solution.py:487
  22.2 1.6 %collective-permute-done.10 = bf16[2,2,16,768]{3,2,1,0:T(8,128)(2,1)S(1)} collective-permute-done((bf16[2,2,16,768]{3,2,1,0:T(8,128)(2,1)S(1)}, bf16[2,2,16,768]{3,2,1,0:T(8,128)(2,1)S(1)}, u32[]{:S(2)}, u32[]{:S(2)}) %collective-permute-start.10) | collective-permute-done | bytes 98336 | tf_op jit(solution)/shard_map/ppermute | solution.py:487
  24.2 11.9 %shard_map.82 = (f32[4,32,256]{2,1,0:T(8,128)S(1)}, f32[4,32,256]{2,1,0:T(8,128)S(1)}) custom-call(s32[2,2]{1,0:T(2,128)S(1)} %pad_add_fusion.tilts, bf16[4,16,128]{2,1,0:T(8,128)(2,1)S(1)} %pad_maximum_fusion.14.tiles, bf16[4,64,1280]{2,1,0:T(8,128)(2,1)S(1)} %pad_maximum_fusion.8.own, bf16[4,64,1280]{2,1,0:T(8,128)(2,1)S(1)} %pad_maximum_fusion.9.other, ...), custom_call_target="tpu_custom_call" | custom-call | tf_op jit(solution)/shard_map/pallas_call | solution.py:544
  36.2 1.2 %collective-permute-done.11 = f32[4,32,256]{2,1,0:T(8,128)S(1)} collective-permute-done((f32[4,32,256]{2,1,0:T(8,128)S(1)}, f32[4,32,256]{2,1,0:T(8,128)S(1)}, u32[]{:S(2)}, u32[]{:S(2)}) %collective-permute-start.11) | collective-permute-done | bytes 131104 | tf_op jit(solution)/shard_map/ppermute | solution.py:487
  37.5 1.8 %collective-permute-start.12 = (f32[4,16,256]{2,1,0:T(8,128)S(1)}, f32[4,16,256]{2,1,0:T(8,128)S(1)}, u32[]{:S(2)}, u32[]{:S(2)}) collective-permute-start(f32[4,16,256]{2,1,0:T(8,128)S(1)} %get-tuple-element.53), channel_id=1, source_target_pairs={{0,2},{1,3},{2,0},{3,1},{4,6},{5,7},{6,4},{7,5},{8,10},{9,11},{10,... | collective-permute-start | bytes 196616 | tf_op jit(solution)/shard_map/ppermute | solution.py:487
  39.3 2.5 %collective-permute-done.12 = f32[4,16,256]{2,1,0:T(8,128)S(1)} collective-permute-done((f32[4,16,256]{2,1,0:T(8,128)S(1)}, f32[4,16,256]{2,1,0:T(8,128)S(1)}, u32[]{:S(2)}, u32[]{:S(2)}) %collective-permute-start.12) | collective-permute-done | bytes 65568 | tf_op jit(solution)/shard_map/ppermute | solution.py:487
  41.9 2.5 %collective-permute-start.15 = (f32[2,16,256]{2,1,0:T(8,128)S(1)}, f32[2,16,256]{2,1,0:T(8,128)S(1)}, u32[]{:S(2)}, u32[]{:S(2)}) collective-permute-start(f32[2,16,256]{2,1,0:T(8,128)S(1)} %get-tuple-element.49), channel_id=1, source_target_pairs={{0,24},{8,16},{16,8},{24,0},{1,25},{9,17},{17,9},{25,1},{2,26},{10... | collective-permute-start | bytes 98312 | tf_op jit(solution)/shard_map/ppermute | solution.py:487
  44.4 0.5 %collective-permute-start.13 = (f32[2,16,256]{2,1,0:T(8,128)S(1)}, f32[2,16,256]{2,1,0:T(8,128)S(1)}, u32[]{:S(2)}, u32[]{:S(2)}) collective-permute-start(f32[2,16,256]{2,1,0:T(8,128)S(1)} %get-tuple-element.51), channel_id=1, source_target_pairs={{0,8},{8,0},{16,24},{24,16},{1,9},{9,1},{17,25},{25,17},{2,10},{10... | collective-permute-start | bytes 98312 | tf_op jit(solution)/shard_map/ppermute | solution.py:487
  45.4 1.3 %collective-permute-done.15.refs_3_ = f32[2,16,256]{2,1,0:T(8,128)S(1)} collective-permute-done((f32[2,16,256]{2,1,0:T(8,128)S(1)}, f32[2,16,256]{2,1,0:T(8,128)S(1)}, u32[]{:S(2)}, u32[]{:S(2)}) %collective-permute-start.15) | collective-permute-done | bytes 32800 | tf_op jit(solution)/shard_map/ppermute | solution.py:487
  46.8 1.5 %collective-permute-done.13.refs_1_ = f32[2,16,256]{2,1,0:T(8,128)S(1)} collective-permute-done((f32[2,16,256]{2,1,0:T(8,128)S(1)}, f32[2,16,256]{2,1,0:T(8,128)S(1)}, u32[]{:S(2)}, u32[]{:S(2)}) %collective-permute-start.13) | collective-permute-done | bytes 32800 | tf_op jit(solution)/shard_map/ppermute | solution.py:487
  48.8 0.7 %shard_map.83 = f32[1,16,2048]{2,1,0:T(8,128)} custom-call(f32[2,16,256]{2,1,0:T(8,128)S(1)} %get-tuple-element.50.refs_0_, f32[2,16,256]{2,1,0:T(8,128)S(1)} %collective-permute-done.13.refs_1_, f32[2,16,256]{2,1,0:T(8,128)S(1)} %collective-permute-done.14.refs_2_, f32[2,16,256]{2,1,0:T(8,128)S(1)} %collective-permute-done.15.refs_3_), custom_call_target="tpu_custom_call" | custom-call | tf_op jit(solution)/shard_map/pallas_call | solution.py:561
  (54 shorter events, 2.2 us)
Async XLA Ops:
  0.0 5.1 %copy-start.2 = (bf16[1,16,2048]{2,1,0:T(8,128)(2,1)S(1)}, bf16[1,16,2048]{2,1,0:T(8,128)(2,1)}, u32[]{:S(2)}) copy-start(bf16[1,16,2048]{2,1,0:T(8,128)(2,1)} %param.8) | copy-start | bytes 196612
  0.0 8.9 %collective-permute-start.3 = (bf16[16,2048]{1,0:T(8,128)(2,1)}, bf16[16,2048]{1,0:T(8,128)(2,1)S(1)}, u32[]{:S(2)}, u32[]{:S(2)}) collective-permute-start(bf16[16,2048]{1,0:T(8,128)(2,1)} %bitcast.47), channel_id=1, source_target_pairs={{0,6},{1,7},{2,4},{3,5},{4,2},{5,3},{6,0},{7,1},{8,14},{9,15},{10,... | collective-permute-start | bytes 196616 | tf_op jit(solution)/shard_map/ppermute | solution.py:487
  5.1 1.5 %copy-start.3 = (bf16[2,16,2048]{2,1,0:T(8,128)(2,1)S(1)}, bf16[2,16,2048]{2,1,0:T(8,128)(2,1)}, u32[]{:S(2)}) copy-start(bf16[2,16,2048]{2,1,0:T(8,128)(2,1)} %param.11) | copy-start | bytes 393220
  5.1 4.8 %collective-permute-start.1 = (bf16[16,1536]{1,0:T(8,128)(2,1)S(1)}, bf16[16,1536]{1,0:T(8,128)(2,1)S(1)}, u32[]{:S(2)}, u32[]{:S(2)}) collective-permute-start(bf16[16,1536]{1,0:T(8,128)(2,1)S(1)} %get-tuple-element.57), channel_id=1, source_target_pairs={{0,2},{1,3},{2,0},{3,1},{4,6},{5,7},{6,4},{7,5},{8,10},{9,11},{10,... | collective-permute-start | bytes 147464 | tf_op jit(solution)/shard_map/ppermute | solution.py:487
  5.1 5.3 %collective-permute-start.2 = (bf16[16,1536]{1,0:T(8,128)(2,1)S(1)}, bf16[16,1536]{1,0:T(8,128)(2,1)S(1)}, u32[]{:S(2)}, u32[]{:S(2)}) collective-permute-start(bf16[16,1536]{1,0:T(8,128)(2,1)S(1)} %get-tuple-element.30), channel_id=1, source_target_pairs={{0,4},{1,5},{2,6},{3,7},{4,0},{5,1},{6,2},{7,3},{8,12},{9,13},{10,... | collective-permute-start | bytes 147464 | tf_op jit(solution)/shard_map/ppermute | solution.py:487
  6.5 1.4 %collective-permute-start = (bf16[16,2048]{1,0:T(8,128)(2,1)S(1)}, bf16[16,2048]{1,0:T(8,128)(2,1)S(1)}, u32[]{:S(2)}, u32[]{:S(2)}) collective-permute-start(bf16[16,2048]{1,0:T(8,128)(2,1)S(1)} %get-tuple-element.56), channel_id=1, source_target_pairs={{0,1},{1,0},{2,3},{3,2},{4,5},{5,4},{6,7},{7,6},{8,9},{9,8},{10,11... | collective-permute-start | bytes 196616 | tf_op jit(solution)/shard_map/ppermute | solution.py:487
  7.3 0.7 %copy-start.6 = (s32[2]{0:T(128)S(1)}, s32[2]{0:T(128)}, u32[]{:S(2)}) copy-start(s32[2]{0:T(128)} %param.9) | copy-start | bytes 28
  8.0 0.8 %copy-start = (bf16[256,128]{1,0:T(8,128)(2,1)S(1)}, bf16[256,128]{1,0:T(8,128)(2,1)}, u32[]{:S(2)}) copy-start(bf16[256,128]{1,0:T(8,128)(2,1)} %constant.93.clone) | copy-start | bytes 196612
  8.0 0.9 %copy-start.1 = (bf16[256,128]{1,0:T(8,128)(2,1)S(1)}, bf16[256,128]{1,0:T(8,128)(2,1)}, u32[]{:S(2)}) copy-start(bf16[256,128]{1,0:T(8,128)(2,1)} %constant.91.clone) | copy-start | bytes 196612
  8.9 0.8 %copy-start.5 = (bf16[256,128]{1,0:T(8,128)(2,1)S(1)}, bf16[256,128]{1,0:T(8,128)(2,1)}, u32[]{:S(2)}) copy-start(bf16[256,128]{1,0:T(8,128)(2,1)} %constant.90.clone) | copy-start | bytes 196612
  8.9 0.9 %copy-start.4 = (bf16[256,128]{1,0:T(8,128)(2,1)S(1)}, bf16[256,128]{1,0:T(8,128)(2,1)}, u32[]{:S(2)}) copy-start(bf16[256,128]{1,0:T(8,128)(2,1)} %constant.92.clone) | copy-start | bytes 196612
  10.6 10.3 %collective-permute-start.5 = (bf16[4,16,1408]{2,1,0:T(8,128)(2,1)S(1)}, bf16[4,16,1408]{2,1,0:T(8,128)(2,1)S(1)}, u32[]{:S(2)}, u32[]{:S(2)}) collective-permute-start(bf16[4,16,1408]{2,1,0:T(8,128)(2,1)S(1)} %concatenate.61), channel_id=1, source_target_pairs={{0,16},{8,24},{16,0},{24,8},{1,17},{9,25},{17,1},{25,9},{2,18},{10... | collective-permute-start | bytes 540680 | tf_op jit(solution)/shard_map/ppermute | solution.py:487
  12.1 8.7 %collective-permute-start.6 = (bf16[4,16,1408]{2,1,0:T(8,128)(2,1)S(1)}, bf16[4,16,1408]{2,1,0:T(8,128)(2,1)S(1)}, u32[]{:S(2)}, u32[]{:S(2)}) collective-permute-start(bf16[4,16,1408]{2,1,0:T(8,128)(2,1)S(1)} %concatenate.62), channel_id=1, source_target_pairs={{0,24},{8,16},{16,8},{24,0},{1,25},{9,17},{17,9},{25,1},{2,26},{10... | collective-permute-start | bytes 540680 | tf_op jit(solution)/shard_map/ppermute | solution.py:487
  13.6 8.5 %collective-permute-start.4 = (bf16[4,16,1408]{2,1,0:T(8,128)(2,1)S(1)}, bf16[4,16,1408]{2,1,0:T(8,128)(2,1)S(1)}, u32[]{:S(2)}, u32[]{:S(2)}) collective-permute-start(bf16[4,16,1408]{2,1,0:T(8,128)(2,1)S(1)} %concatenate.60), channel_id=1, source_target_pairs={{0,8},{8,0},{16,24},{24,16},{1,9},{9,1},{17,25},{25,17},{2,10},{10... | collective-permute-start | bytes 540680 | tf_op jit(solution)/shard_map/ppermute | solution.py:487
  14.2 4.1 %collective-permute-start.9 = (bf16[2,16,768]{2,1,0:T(8,128)(2,1)S(1)}, bf16[2,16,768]{2,1,0:T(8,128)(2,1)S(1)}, u32[]{:S(2)}, u32[]{:S(2)}) collective-permute-start(bf16[2,16,768]{2,1,0:T(8,128)(2,1)S(1)} %get-tuple-element.35), channel_id=1, source_target_pairs={{0,2},{1,3},{2,0},{3,1},{4,6},{5,7},{6,4},{7,5},{8,10},{9,11},{10,... | collective-permute-start | bytes 147464 | tf_op jit(solution)/shard_map/ppermute | solution.py:487
  15.9 8.2 %collective-permute-start.7 = (bf16[1,64,1280]{2,1,0:T(8,128)(2,1)S(1)}, bf16[1,64,1280]{2,1,0:T(8,128)(2,1)S(1)}, u32[]{:S(2)}, u32[]{:S(2)}) collective-permute-start(bf16[1,64,1280]{2,1,0:T(8,128)(2,1)S(1)} %bitcast.42), channel_id=1, source_target_pairs={{0,1},{1,0},{2,3},{3,2},{4,5},{5,4},{6,7},{7,6},{8,9},{9,8},{10,11... | collective-permute-start | bytes 491528 | tf_op jit(solution)/shard_map/ppermute | solution.py:487
  18.3 5.6 %collective-permute-start.10 = (bf16[2,2,16,768]{3,2,1,0:T(8,128)(2,1)S(1)}, bf16[2,2,16,768]{3,2,1,0:T(8,128)(2,1)S(1)}, u32[]{:S(2)}, u32[]{:S(2)}) collective-permute-start(bf16[2,2,16,768]{3,2,1,0:T(8,128)(2,1)S(1)} %pad_maximum_fusion.12), channel_id=1, source_target_pairs={{0,4},{1,5},{2,6},{3,7},{4,0},{5,1},{6,2},{7,3},{8,12},{9,13},{10,... | collective-permute-start | bytes 294920 | tf_op jit(solution)/shard_map/ppermute | solution.py:487
  22.2 1.9 %collective-permute-start.8 = (bf16[3,64,1280]{2,1,0:T(8,128)(2,1)S(1)}, bf16[3,64,1280]{2,1,0:T(8,128)(2,1)S(1)}, u32[]{:S(2)}, u32[]{:S(2)}) collective-permute-start(bf16[3,64,1280]{2,1,0:T(8,128)(2,1)S(1)} %pad_maximum_fusion.10), channel_id=1, source_target_pairs={{0,1},{1,0},{2,3},{3,2},{4,5},{5,4},{6,7},{7,6},{8,9},{9,8},{10,11... | collective-permute-start | bytes 1474568 | tf_op jit(solution)/shard_map/ppermute | solution.py:487
  36.1 1.4 %collective-permute-start.11 = (f32[4,32,256]{2,1,0:T(8,128)S(1)}, f32[4,32,256]{2,1,0:T(8,128)S(1)}, u32[]{:S(2)}, u32[]{:S(2)}) collective-permute-start(f32[4,32,256]{2,1,0:T(8,128)S(1)} %get-tuple-element.40), channel_id=1, source_target_pairs={{0,1},{1,0},{2,3},{3,2},{4,5},{5,4},{6,7},{7,6},{8,9},{9,8},{10,11... | collective-permute-start | bytes 393224 | tf_op jit(solution)/shard_map/ppermute | solution.py:487
  37.5 4.3 %collective-permute-start.12 = (f32[4,16,256]{2,1,0:T(8,128)S(1)}, f32[4,16,256]{2,1,0:T(8,128)S(1)}, u32[]{:S(2)}, u32[]{:S(2)}) collective-permute-start(f32[4,16,256]{2,1,0:T(8,128)S(1)} %get-tuple-element.53), channel_id=1, source_target_pairs={{0,2},{1,3},{2,0},{3,1},{4,6},{5,7},{6,4},{7,5},{8,10},{9,11},{10,... | collective-permute-start | bytes 196616 | tf_op jit(solution)/shard_map/ppermute | solution.py:487
  41.9 4.9 %collective-permute-start.15 = (f32[2,16,256]{2,1,0:T(8,128)S(1)}, f32[2,16,256]{2,1,0:T(8,128)S(1)}, u32[]{:S(2)}, u32[]{:S(2)}) collective-permute-start(f32[2,16,256]{2,1,0:T(8,128)S(1)} %get-tuple-element.49), channel_id=1, source_target_pairs={{0,24},{8,16},{16,8},{24,0},{1,25},{9,17},{17,9},{25,1},{2,26},{10... | collective-permute-start | bytes 98312 | tf_op jit(solution)/shard_map/ppermute | solution.py:487
  44.4 3.9 %collective-permute-start.13 = (f32[2,16,256]{2,1,0:T(8,128)S(1)}, f32[2,16,256]{2,1,0:T(8,128)S(1)}, u32[]{:S(2)}, u32[]{:S(2)}) collective-permute-start(f32[2,16,256]{2,1,0:T(8,128)S(1)} %get-tuple-element.51), channel_id=1, source_target_pairs={{0,8},{8,0},{16,24},{24,16},{1,9},{9,1},{17,25},{25,17},{2,10},{10... | collective-permute-start | bytes 98312 | tf_op jit(solution)/shard_map/ppermute | solution.py:487
  44.9 3.9 %collective-permute-start.14 = (f32[2,16,256]{2,1,0:T(8,128)S(1)}, f32[2,16,256]{2,1,0:T(8,128)S(1)}, u32[]{:S(2)}, u32[]{:S(2)}) collective-permute-start(f32[2,16,256]{2,1,0:T(8,128)S(1)} %get-tuple-element.52), channel_id=1, source_target_pairs={{0,16},{8,24},{16,0},{24,8},{1,17},{9,25},{17,1},{25,9},{2,18},{10... | collective-permute-start | bytes 98312 | tf_op jit(solution)/shard_map/ppermute | solution.py:487

commit v6 on v5

--- a/solution.py
+++ b/solution.py
@@ -332,7 +332,7 @@
 
     rows_of, rows_across = row_numbers(0), row_numbers(1)
     walk_off = [tiles[place ^ s, :1].astype(jnp.int32) for s in range(slices)]
-    factors = [row_factor(rows_of, rows_across, offset) for offset in walk_off]
+    factors = [[split(part) for part in row_factor(rows_of, rows_across, offset)] for offset in walk_off]
     width = blocks * COLBLK
     first = block * broad - 2 * slices * HALFCOL
     lane = first + lax.broadcasted_iota(jnp.int32, (1, width), 1)
@@ -369,7 +369,8 @@
         y_high, y_low = split(y)
         v = dot(factor[0], y_high) + (dot(factor[0], y_low) + dot(factor[1], y_high))
         cut = [slice(i * COLBLK, (i + 1) * COLBLK) for i in range(len(blocks_in))]
-        return [(v[:rows, c], v[rows:, c]) for c in cut]
+        middle = v.shape[0] // 2
+        return [(v[:middle, c], v[middle:, c]) for c in cut]
 
     def pairs(n):
         return [range(j, min(j + 2, n)) for j in range(0, n, 2)]
@@ -377,7 +378,7 @@
     low_half = lax.broadcasted_iota(jnp.int32, (rows, COLBLK), 1) < HALFCOL
 
     def forward(s):
-        factor = split(complex_form(*factors[s]))
+        factor = [complex_form(real_part, imag_part) for real_part, imag_part in zip(*factors[s])]
         slot = place ^ s
 
         def index_block(b):
@@ -442,8 +443,11 @@
             yield
 
     def backward(s):
-        real_part, imag_part = factors[s]
-        factor = split(complex_form(real_part.T, -imag_part.T))
+        factor = [complex_form(real_part.T, -imag_part.T) for real_part, imag_part in zip(*factors[s])]
+        if s == 0:
+            factor = [
+                jnp.concatenate([x[i * half : i * half + 2 * height] for i in range(4)], axis=0) for x in factor
+            ]
         level = 2 * slices - 1 - s
         last = None
         for group in pairs(s + broad // COLBLK):
@@ -451,9 +455,12 @@
                 start = s * HALFCOL - j * COLBLK
                 lo, hi = max(start, 0), min(start + broad, COLBLK)
                 if lo < hi:
-                    part = PHASE_SCALE * (kept[s, j, :rows] * b - kept[s, j, rows:] * a)[:, lo:hi]
-                    mine[place ^ s, :, lo - start : hi - start] = part[: 2 * height]
-                    theirs[place ^ s, :, lo - start : hi - start] = part[half : half + 2 * height]
+                    for i, target in enumerate((mine, theirs)):
+                        held = slice(i * half, i * half + 2 * height)
+                        there = slice(rows + i * half, rows + i * half + 2 * height)
+                        new = slice(i * 2 * height, (i + 1) * 2 * height) if s == 0 else held
+                        part = PHASE_SCALE * (kept[s, j, held] * b[new] - kept[s, j, there] * a[new])
+                        target[place ^ s, :, lo - start : hi - start] = part[:, lo:hi]
                 if s > 0:
                     begin = 2 * (slices - s) * HALFCOL + j * COLBLK
                     c = cosine[s, :, begin : begin + COLBLK]

time: 49.7 us -> 49.6 us (level)
  no operation moved by 1% of the time
where the time goes in v6:
time: 49.6 us; the launch traced here: 49.4 us
  starting transfers between devices  19.3 us (39%)
  waiting for transfers between devices  13.7 us (28%)
  Pallas kernels  12.5 us (25%)
  local copies, waits for them, and re-layouts  2.52 us (5%)
  between operations  0.96 us (2%)
    ppermute x16, starting transfers between devices, swap(): return lax.ppermute(x, axis, [(i, i ^ step) for i in range(size)])  19.3 us
    ppermute x16, waiting for transfers between devices, swap(): return lax.ppermute(x, axis, [(i, i ^ step) for i in range(size)])  13.7 us
    pallas_call x1, Pallas kernels, window_body(): pl.pallas_call(functools.partial(sweep, sizes), out_shape=[jax.ShapeDtype...  11.8 us
    unnamed x14, local copies, waits for them, and re-layouts  2.31 us
  transfers between devices with their start and end apart: 16, of which 10 were waited for; matrix products, arithmetic and copies ran while one was open for 1% of the time, Pallas kernels for 0%

profile of v6, /device:TPU:0, one launch (start us, length us, event | category | flops | bytes accessed | tf_op | source)
XLA Modules:
  0.0 49.4 jit_solution(2412204247522360632)
XLA Ops:
  0.0 5.0 %collective-permute-start.3 = (bf16[16,2048]{1,0:T(8,128)(2,1)}, bf16[16,2048]{1,0:T(8,128)(2,1)S(1)}, u32[]{:S(2)}, u32[]{:S(2)}) collective-permute-start(bf16[16,2048]{1,0:T(8,128)(2,1)} %bitcast.47), channel_id=1, source_target_pairs={{0,6},{1,7},{2,4},{3,5},{4,2},{5,3},{6,0},{7,1},{8,14},{9,15},{10,... | collective-permute-start | bytes 196616 | tf_op jit(solution)/shard_map/ppermute | solution.py:494
  5.1 1.4 %collective-permute-start.2 = (bf16[16,1536]{1,0:T(8,128)(2,1)S(1)}, bf16[16,1536]{1,0:T(8,128)(2,1)S(1)}, u32[]{:S(2)}, u32[]{:S(2)}) collective-permute-start(bf16[16,1536]{1,0:T(8,128)(2,1)S(1)} %get-tuple-element.30), channel_id=1, source_target_pairs={{0,4},{1,5},{2,6},{3,7},{4,0},{5,1},{6,2},{7,3},{8,12},{9,13},{10,... | collective-permute-start | bytes 147464 | tf_op jit(solution)/shard_map/ppermute | solution.py:494
  7.3 0.6 %copy-done.6 = s32[2]{0:T(128)S(1)} copy-done((s32[2]{0:T(128)S(1)}, s32[2]{0:T(128)}, u32[]{:S(2)}) %copy-start.6) | copy-done | bytes 32
  8.1 0.8 %copy-done = bf16[256,128]{1,0:T(8,128)(2,1)S(1)} copy-done((bf16[256,128]{1,0:T(8,128)(2,1)S(1)}, bf16[256,128]{1,0:T(8,128)(2,1)}, u32[]{:S(2)}) %copy-start) | copy-done | bytes 65560
  9.0 0.8 %copy-done.5 = bf16[256,128]{1,0:T(8,128)(2,1)S(1)} copy-done((bf16[256,128]{1,0:T(8,128)(2,1)S(1)}, bf16[256,128]{1,0:T(8,128)(2,1)}, u32[]{:S(2)}) %copy-start.5) | copy-done | bytes 65560
  9.9 0.6 %collective-permute-done.2 = bf16[16,1536]{1,0:T(8,128)(2,1)S(1)} collective-permute-done((bf16[16,1536]{1,0:T(8,128)(2,1)S(1)}, bf16[16,1536]{1,0:T(8,128)(2,1)S(1)}, u32[]{:S(2)}, u32[]{:S(2)}) %collective-permute-start.2) | collective-permute-done | bytes 49184 | tf_op jit(solution)/shard_map/ppermute | solution.py:494
  10.6 1.6 %collective-permute-start.5 = (bf16[4,16,1408]{2,1,0:T(8,128)(2,1)S(1)}, bf16[4,16,1408]{2,1,0:T(8,128)(2,1)S(1)}, u32[]{:S(2)}, u32[]{:S(2)}) collective-permute-start(bf16[4,16,1408]{2,1,0:T(8,128)(2,1)S(1)} %concatenate.61), channel_id=1, source_target_pairs={{0,16},{8,24},{16,0},{24,8},{1,17},{9,25},{17,1},{25,9},{2,18},{10... | collective-permute-start | bytes 540680 | tf_op jit(solution)/shard_map/ppermute | solution.py:494
  12.1 1.4 %collective-permute-start.6 = (bf16[4,16,1408]{2,1,0:T(8,128)(2,1)S(1)}, bf16[4,16,1408]{2,1,0:T(8,128)(2,1)S(1)}, u32[]{:S(2)}, u32[]{:S(2)}) collective-permute-start(bf16[4,16,1408]{2,1,0:T(8,128)(2,1)S(1)} %concatenate.62), channel_id=1, source_target_pairs={{0,24},{8,16},{16,8},{24,0},{1,25},{9,17},{17,9},{25,1},{2,26},{10... | collective-permute-start | bytes 540680 | tf_op jit(solution)/shard_map/ppermute | solution.py:494
  13.6 0.6 %collective-permute-start.4 = (bf16[4,16,1408]{2,1,0:T(8,128)(2,1)S(1)}, bf16[4,16,1408]{2,1,0:T(8,128)(2,1)S(1)}, u32[]{:S(2)}, u32[]{:S(2)}) collective-permute-start(bf16[4,16,1408]{2,1,0:T(8,128)(2,1)S(1)} %concatenate.60), channel_id=1, source_target_pairs={{0,8},{8,0},{16,24},{24,16},{1,9},{9,1},{17,25},{25,17},{2,10},{10... | collective-permute-start | bytes 540680 | tf_op jit(solution)/shard_map/ppermute | solution.py:494
  14.2 1.7 %collective-permute-start.9 = (bf16[2,16,768]{2,1,0:T(8,128)(2,1)S(1)}, bf16[2,16,768]{2,1,0:T(8,128)(2,1)S(1)}, u32[]{:S(2)}, u32[]{:S(2)}) collective-permute-start(bf16[2,16,768]{2,1,0:T(8,128)(2,1)S(1)} %get-tuple-element.35), channel_id=1, source_target_pairs={{0,2},{1,3},{2,0},{3,1},{4,6},{5,7},{6,4},{7,5},{8,10},{9,11},{10,... | collective-permute-start | bytes 147464 | tf_op jit(solution)/shard_map/ppermute | solution.py:494
  15.9 2.3 %collective-permute-done.9 = bf16[2,16,768]{2,1,0:T(8,128)(2,1)S(1)} collective-permute-done((bf16[2,16,768]{2,1,0:T(8,128)(2,1)S(1)}, bf16[2,16,768]{2,1,0:T(8,128)(2,1)S(1)}, u32[]{:S(2)}, u32[]{:S(2)}) %collective-permute-start.9) | collective-permute-done | bytes 49184 | tf_op jit(solution)/shard_map/ppermute | solution.py:494
  18.3 1.8 %collective-permute-start.10 = (bf16[2,2,16,768]{3,2,1,0:T(8,128)(2,1)S(1)}, bf16[2,2,16,768]{3,2,1,0:T(8,128)(2,1)S(1)}, u32[]{:S(2)}, u32[]{:S(2)}) collective-permute-start(bf16[2,2,16,768]{3,2,1,0:T(8,128)(2,1)S(1)} %pad_maximum_fusion.12), channel_id=1, source_target_pairs={{0,4},{1,5},{2,6},{3,7},{4,0},{5,1},{6,2},{7,3},{8,12},{9,13},{10,... | collective-permute-start | bytes 294920 | tf_op jit(solution)/shard_map/ppermute | solution.py:494
  20.0 0.8 %collective-permute-done.5 = bf16[4,16,1408]{2,1,0:T(8,128)(2,1)S(1)} collective-permute-done((bf16[4,16,1408]{2,1,0:T(8,128)(2,1)S(1)}, bf16[4,16,1408]{2,1,0:T(8,128)(2,1)S(1)}, u32[]{:S(2)}, u32[]{:S(2)}) %collective-permute-start.5) | collective-permute-done | bytes 180256 | tf_op jit(solution)/shard_map/ppermute | solution.py:494
  20.9 1.2 %collective-permute-done.4 = bf16[4,16,1408]{2,1,0:T(8,128)(2,1)S(1)} collective-permute-done((bf16[4,16,1408]{2,1,0:T(8,128)(2,1)S(1)}, bf16[4,16,1408]{2,1,0:T(8,128)(2,1)S(1)}, u32[]{:S(2)}, u32[]{:S(2)}) %collective-permute-start.4) | collective-permute-done | bytes 180256 | tf_op jit(solution)/shard_map/ppermute | solution.py:494
  22.2 1.6 %collective-permute-done.10 = bf16[2,2,16,768]{3,2,1,0:T(8,128)(2,1)S(1)} collective-permute-done((bf16[2,2,16,768]{3,2,1,0:T(8,128)(2,1)S(1)}, bf16[2,2,16,768]{3,2,1,0:T(8,128)(2,1)S(1)}, u32[]{:S(2)}, u32[]{:S(2)}) %collective-permute-start.10) | collective-permute-done | bytes 98336 | tf_op jit(solution)/shard_map/ppermute | solution.py:494
  24.2 11.8 %shard_map.82 = (f32[4,32,256]{2,1,0:T(8,128)S(1)}, f32[4,32,256]{2,1,0:T(8,128)S(1)}) custom-call(s32[2,2]{1,0:T(2,128)S(1)} %pad_add_fusion.tilts, bf16[4,16,128]{2,1,0:T(8,128)(2,1)S(1)} %pad_maximum_fusion.14.tiles, bf16[4,64,1280]{2,1,0:T(8,128)(2,1)S(1)} %pad_maximum_fusion.8.own, bf16[4,64,1280]{2,1,0:T(8,128)(2,1)S(1)} %pad_maximum_fusion.9.other, ...), custom_call_target="tpu_custom_call" | custom-call | tf_op jit(solution)/shard_map/pallas_call | solution.py:551
  36.2 1.2 %collective-permute-done.11 = f32[4,32,256]{2,1,0:T(8,128)S(1)} collective-permute-done((f32[4,32,256]{2,1,0:T(8,128)S(1)}, f32[4,32,256]{2,1,0:T(8,128)S(1)}, u32[]{:S(2)}, u32[]{:S(2)}) %collective-permute-start.11) | collective-permute-done | bytes 131104 | tf_op jit(solution)/shard_map/ppermute | solution.py:494
  37.4 1.8 %collective-permute-start.12 = (f32[4,16,256]{2,1,0:T(8,128)S(1)}, f32[4,16,256]{2,1,0:T(8,128)S(1)}, u32[]{:S(2)}, u32[]{:S(2)}) collective-permute-start(f32[4,16,256]{2,1,0:T(8,128)S(1)} %get-tuple-element.53), channel_id=1, source_target_pairs={{0,2},{1,3},{2,0},{3,1},{4,6},{5,7},{6,4},{7,5},{8,10},{9,11},{10,... | collective-permute-start | bytes 196616 | tf_op jit(solution)/shard_map/ppermute | solution.py:494
  39.2 2.5 %collective-permute-done.12 = f32[4,16,256]{2,1,0:T(8,128)S(1)} collective-permute-done((f32[4,16,256]{2,1,0:T(8,128)S(1)}, f32[4,16,256]{2,1,0:T(8,128)S(1)}, u32[]{:S(2)}, u32[]{:S(2)}) %collective-permute-start.12) | collective-permute-done | bytes 65568 | tf_op jit(solution)/shard_map/ppermute | solution.py:494
  41.8 2.5 %collective-permute-start.15 = (f32[2,16,256]{2,1,0:T(8,128)S(1)}, f32[2,16,256]{2,1,0:T(8,128)S(1)}, u32[]{:S(2)}, u32[]{:S(2)}) collective-permute-start(f32[2,16,256]{2,1,0:T(8,128)S(1)} %get-tuple-element.49), channel_id=1, source_target_pairs={{0,24},{8,16},{16,8},{24,0},{1,25},{9,17},{17,9},{25,1},{2,26},{10... | collective-permute-start | bytes 98312 | tf_op jit(solution)/shard_map/ppermute | solution.py:494
  44.3 0.5 %collective-permute-start.13 = (f32[2,16,256]{2,1,0:T(8,128)S(1)}, f32[2,16,256]{2,1,0:T(8,128)S(1)}, u32[]{:S(2)}, u32[]{:S(2)}) collective-permute-start(f32[2,16,256]{2,1,0:T(8,128)S(1)} %get-tuple-element.51), channel_id=1, source_target_pairs={{0,8},{8,0},{16,24},{24,16},{1,9},{9,1},{17,25},{25,17},{2,10},{10... | collective-permute-start | bytes 98312 | tf_op jit(solution)/shard_map/ppermute | solution.py:494
  45.3 1.3 %collective-permute-done.15.refs_3_ = f32[2,16,256]{2,1,0:T(8,128)S(1)} collective-permute-done((f32[2,16,256]{2,1,0:T(8,128)S(1)}, f32[2,16,256]{2,1,0:T(8,128)S(1)}, u32[]{:S(2)}, u32[]{:S(2)}) %collective-permute-start.15) | collective-permute-done | bytes 32800 | tf_op jit(solution)/shard_map/ppermute | solution.py:494
  46.7 1.6 %collective-permute-done.13.refs_1_ = f32[2,16,256]{2,1,0:T(8,128)S(1)} collective-permute-done((f32[2,16,256]{2,1,0:T(8,128)S(1)}, f32[2,16,256]{2,1,0:T(8,128)S(1)}, u32[]{:S(2)}, u32[]{:S(2)}) %collective-permute-start.13) | collective-permute-done | bytes 32800 | tf_op jit(solution)/shard_map/ppermute | solution.py:494
  48.7 0.7 %shard_map.83 = f32[1,16,2048]{2,1,0:T(8,128)} custom-call(f32[2,16,256]{2,1,0:T(8,128)S(1)} %get-tuple-element.50.refs_0_, f32[2,16,256]{2,1,0:T(8,128)S(1)} %collective-permute-done.13.refs_1_, f32[2,16,256]{2,1,0:T(8,128)S(1)} %collective-permute-done.14.refs_2_, f32[2,16,256]{2,1,0:T(8,128)S(1)} %collective-permute-done.15.refs_3_), custom_call_target="tpu_custom_call" | custom-call | tf_op jit(solution)/shard_map/pallas_call | solution.py:568
  (54 shorter events, 2.2 us)
Async XLA Ops:
  0.0 5.1 %copy-start.2 = (bf16[1,16,2048]{2,1,0:T(8,128)(2,1)S(1)}, bf16[1,16,2048]{2,1,0:T(8,128)(2,1)}, u32[]{:S(2)}) copy-start(bf16[1,16,2048]{2,1,0:T(8,128)(2,1)} %param.8) | copy-start | bytes 196612
  0.0 8.9 %collective-permute-start.3 = (bf16[16,2048]{1,0:T(8,128)(2,1)}, bf16[16,2048]{1,0:T(8,128)(2,1)S(1)}, u32[]{:S(2)}, u32[]{:S(2)}) collective-permute-start(bf16[16,2048]{1,0:T(8,128)(2,1)} %bitcast.47), channel_id=1, source_target_pairs={{0,6},{1,7},{2,4},{3,5},{4,2},{5,3},{6,0},{7,1},{8,14},{9,15},{10,... | collective-permute-start | bytes 196616 | tf_op jit(solution)/shard_map/ppermute | solution.py:494
  5.1 1.5 %copy-start.3 = (bf16[2,16,2048]{2,1,0:T(8,128)(2,1)S(1)}, bf16[2,16,2048]{2,1,0:T(8,128)(2,1)}, u32[]{:S(2)}) copy-start(bf16[2,16,2048]{2,1,0:T(8,128)(2,1)} %param.11) | copy-start | bytes 393220
  5.1 4.8 %collective-permute-start.1 = (bf16[16,1536]{1,0:T(8,128)(2,1)S(1)}, bf16[16,1536]{1,0:T(8,128)(2,1)S(1)}, u32[]{:S(2)}, u32[]{:S(2)}) collective-permute-start(bf16[16,1536]{1,0:T(8,128)(2,1)S(1)} %get-tuple-element.57), channel_id=1, source_target_pairs={{0,2},{1,3},{2,0},{3,1},{4,6},{5,7},{6,4},{7,5},{8,10},{9,11},{10,... | collective-permute-start | bytes 147464 | tf_op jit(solution)/shard_map/ppermute | solution.py:494
  5.1 5.3 %collective-permute-start.2 = (bf16[16,1536]{1,0:T(8,128)(2,1)S(1)}, bf16[16,1536]{1,0:T(8,128)(2,1)S(1)}, u32[]{:S(2)}, u32[]{:S(2)}) collective-permute-start(bf16[16,1536]{1,0:T(8,128)(2,1)S(1)} %get-tuple-element.30), channel_id=1, source_target_pairs={{0,4},{1,5},{2,6},{3,7},{4,0},{5,1},{6,2},{7,3},{8,12},{9,13},{10,... | collective-permute-start | bytes 147464 | tf_op jit(solution)/shard_map/ppermute | solution.py:494
  6.5 1.4 %collective-permute-start = (bf16[16,2048]{1,0:T(8,128)(2,1)S(1)}, bf16[16,2048]{1,0:T(8,128)(2,1)S(1)}, u32[]{:S(2)}, u32[]{:S(2)}) collective-permute-start(bf16[16,2048]{1,0:T(8,128)(2,1)S(1)} %get-tuple-element.56), channel_id=1, source_target_pairs={{0,1},{1,0},{2,3},{3,2},{4,5},{5,4},{6,7},{7,6},{8,9},{9,8},{10,11... | collective-permute-start | bytes 196616 | tf_op jit(solution)/shard_map/ppermute | solution.py:494
  7.3 0.7 %copy-start.6 = (s32[2]{0:T(128)S(1)}, s32[2]{0:T(128)}, u32[]{:S(2)}) copy-start(s32[2]{0:T(128)} %param.9) | copy-start | bytes 28
  8.0 0.8 %copy-start = (bf16[256,128]{1,0:T(8,128)(2,1)S(1)}, bf16[256,128]{1,0:T(8,128)(2,1)}, u32[]{:S(2)}) copy-start(bf16[256,128]{1,0:T(8,128)(2,1)} %constant.93.clone) | copy-start | bytes 196612
  8.0 0.9 %copy-start.1 = (bf16[256,128]{1,0:T(8,128)(2,1)S(1)}, bf16[256,128]{1,0:T(8,128)(2,1)}, u32[]{:S(2)}) copy-start(bf16[256,128]{1,0:T(8,128)(2,1)} %constant.91.clone) | copy-start | bytes 196612
  8.9 0.8 %copy-start.5 = (bf16[256,128]{1,0:T(8,128)(2,1)S(1)}, bf16[256,128]{1,0:T(8,128)(2,1)}, u32[]{:S(2)}) copy-start(bf16[256,128]{1,0:T(8,128)(2,1)} %constant.90.clone) | copy-start | bytes 196612
  8.9 0.9 %copy-start.4 = (bf16[256,128]{1,0:T(8,128)(2,1)S(1)}, bf16[256,128]{1,0:T(8,128)(2,1)}, u32[]{:S(2)}) copy-start(bf16[256,128]{1,0:T(8,128)(2,1)} %constant.92.clone) | copy-start | bytes 196612
  10.6 10.3 %collective-permute-start.5 = (bf16[4,16,1408]{2,1,0:T(8,128)(2,1)S(1)}, bf16[4,16,1408]{2,1,0:T(8,128)(2,1)S(1)}, u32[]{:S(2)}, u32[]{:S(2)}) collective-permute-start(bf16[4,16,1408]{2,1,0:T(8,128)(2,1)S(1)} %concatenate.61), channel_id=1, source_target_pairs={{0,16},{8,24},{16,0},{24,8},{1,17},{9,25},{17,1},{25,9},{2,18},{10... | collective-permute-start | bytes 540680 | tf_op jit(solution)/shard_map/ppermute | solution.py:494
  12.1 8.7 %collective-permute-start.6 = (bf16[4,16,1408]{2,1,0:T(8,128)(2,1)S(1)}, bf16[4,16,1408]{2,1,0:T(8,128)(2,1)S(1)}, u32[]{:S(2)}, u32[]{:S(2)}) collective-permute-start(bf16[4,16,1408]{2,1,0:T(8,128)(2,1)S(1)} %concatenate.62), channel_id=1, source_target_pairs={{0,24},{8,16},{16,8},{24,0},{1,25},{9,17},{17,9},{25,1},{2,26},{10... | collective-permute-start | bytes 540680 | tf_op jit(solution)/shard_map/ppermute | solution.py:494
  13.6 8.5 %collective-permute-start.4 = (bf16[4,16,1408]{2,1,0:T(8,128)(2,1)S(1)}, bf16[4,16,1408]{2,1,0:T(8,128)(2,1)S(1)}, u32[]{:S(2)}, u32[]{:S(2)}) collective-permute-start(bf16[4,16,1408]{2,1,0:T(8,128)(2,1)S(1)} %concatenate.60), channel_id=1, source_target_pairs={{0,8},{8,0},{16,24},{24,16},{1,9},{9,1},{17,25},{25,17},{2,10},{10... | collective-permute-start | bytes 540680 | tf_op jit(solution)/shard_map/ppermute | solution.py:494
  14.2 4.1 %collective-permute-start.9 = (bf16[2,16,768]{2,1,0:T(8,128)(2,1)S(1)}, bf16[2,16,768]{2,1,0:T(8,128)(2,1)S(1)}, u32[]{:S(2)}, u32[]{:S(2)}) collective-permute-start(bf16[2,16,768]{2,1,0:T(8,128)(2,1)S(1)} %get-tuple-element.35), channel_id=1, source_target_pairs={{0,2},{1,3},{2,0},{3,1},{4,6},{5,7},{6,4},{7,5},{8,10},{9,11},{10,... | collective-permute-start | bytes 147464 | tf_op jit(solution)/shard_map/ppermute | solution.py:494
  15.9 8.2 %collective-permute-start.7 = (bf16[1,64,1280]{2,1,0:T(8,128)(2,1)S(1)}, bf16[1,64,1280]{2,1,0:T(8,128)(2,1)S(1)}, u32[]{:S(2)}, u32[]{:S(2)}) collective-permute-start(bf16[1,64,1280]{2,1,0:T(8,128)(2,1)S(1)} %bitcast.42), channel_id=1, source_target_pairs={{0,1},{1,0},{2,3},{3,2},{4,5},{5,4},{6,7},{7,6},{8,9},{9,8},{10,11... | collective-permute-start | bytes 491528 | tf_op jit(solution)/shard_map/ppermute | solution.py:494
  18.3 5.6 %collective-permute-start.10 = (bf16[2,2,16,768]{3,2,1,0:T(8,128)(2,1)S(1)}, bf16[2,2,16,768]{3,2,1,0:T(8,128)(2,1)S(1)}, u32[]{:S(2)}, u32[]{:S(2)}) collective-permute-start(bf16[2,2,16,768]{3,2,1,0:T(8,128)(2,1)S(1)} %pad_maximum_fusion.12), channel_id=1, source_target_pairs={{0,4},{1,5},{2,6},{3,7},{4,0},{5,1},{6,2},{7,3},{8,12},{9,13},{10,... | collective-permute-start | bytes 294920 | tf_op jit(solution)/shard_map/ppermute | solution.py:494
  22.2 1.9 %collective-permute-start.8 = (bf16[3,64,1280]{2,1,0:T(8,128)(2,1)S(1)}, bf16[3,64,1280]{2,1,0:T(8,128)(2,1)S(1)}, u32[]{:S(2)}, u32[]{:S(2)}) collective-permute-start(bf16[3,64,1280]{2,1,0:T(8,128)(2,1)S(1)} %pad_maximum_fusion.10), channel_id=1, source_target_pairs={{0,1},{1,0},{2,3},{3,2},{4,5},{5,4},{6,7},{7,6},{8,9},{9,8},{10,11... | collective-permute-start | bytes 1474568 | tf_op jit(solution)/shard_map/ppermute | solution.py:494
  36.0 1.4 %collective-permute-start.11 = (f32[4,32,256]{2,1,0:T(8,128)S(1)}, f32[4,32,256]{2,1,0:T(8,128)S(1)}, u32[]{:S(2)}, u32[]{:S(2)}) collective-permute-start(f32[4,32,256]{2,1,0:T(8,128)S(1)} %get-tuple-element.40), channel_id=1, source_target_pairs={{0,1},{1,0},{2,3},{3,2},{4,5},{5,4},{6,7},{7,6},{8,9},{9,8},{10,11... | collective-permute-start | bytes 393224 | tf_op jit(solution)/shard_map/ppermute | solution.py:494
  37.4 4.3 %collective-permute-start.12 = (f32[4,16,256]{2,1,0:T(8,128)S(1)}, f32[4,16,256]{2,1,0:T(8,128)S(1)}, u32[]{:S(2)}, u32[]{:S(2)}) collective-permute-start(f32[4,16,256]{2,1,0:T(8,128)S(1)} %get-tuple-element.53), channel_id=1, source_target_pairs={{0,2},{1,3},{2,0},{3,1},{4,6},{5,7},{6,4},{7,5},{8,10},{9,11},{10,... | collective-permute-start | bytes 196616 | tf_op jit(solution)/shard_map/ppermute | solution.py:494
  41.8 4.9 %collective-permute-start.15 = (f32[2,16,256]{2,1,0:T(8,128)S(1)}, f32[2,16,256]{2,1,0:T(8,128)S(1)}, u32[]{:S(2)}, u32[]{:S(2)}) collective-permute-start(f32[2,16,256]{2,1,0:T(8,128)S(1)} %get-tuple-element.49), channel_id=1, source_target_pairs={{0,24},{8,16},{16,8},{24,0},{1,25},{9,17},{17,9},{25,1},{2,26},{10... | collective-permute-start | bytes 98312 | tf_op jit(solution)/shard_map/ppermute | solution.py:494
  44.3 3.9 %collective-permute-start.13 = (f32[2,16,256]{2,1,0:T(8,128)S(1)}, f32[2,16,256]{2,1,0:T(8,128)S(1)}, u32[]{:S(2)}, u32[]{:S(2)}) collective-permute-start(f32[2,16,256]{2,1,0:T(8,128)S(1)} %get-tuple-element.51), channel_id=1, source_target_pairs={{0,8},{8,0},{16,24},{24,16},{1,9},{9,1},{17,25},{25,17},{2,10},{10... | collective-permute-start | bytes 98312 | tf_op jit(solution)/shard_map/ppermute | solution.py:494
  44.8 3.9 %collective-permute-start.14 = (f32[2,16,256]{2,1,0:T(8,128)S(1)}, f32[2,16,256]{2,1,0:T(8,128)S(1)}, u32[]{:S(2)}, u32[]{:S(2)}) collective-permute-start(f32[2,16,256]{2,1,0:T(8,128)S(1)} %get-tuple-element.52), channel_id=1, source_target_pairs={{0,16},{8,24},{16,0},{24,8},{1,17},{9,25},{17,1},{25,9},{2,18},{10... | collective-permute-start | bytes 98312 | tf_op jit(solution)/shard_map/ppermute | solution.py:494

commit v7 on v6

--- a/solution.py
+++ b/solution.py
@@ -334,6 +334,7 @@
     walk_off = [tiles[place ^ s, :1].astype(jnp.int32) for s in range(slices)]
     factors = [[split(part) for part in row_factor(rows_of, rows_across, offset)] for offset in walk_off]
     width = blocks * COLBLK
+    cone = 2 * slices * HALFCOL
     first = block * broad - 2 * slices * HALFCOL
     lane = first + lax.broadcasted_iota(jnp.int32, (1, width), 1)
     inside = (lane >= 0) & (lane < columns)
@@ -399,9 +400,11 @@
                 elif j + 1 < blocks - s:
                     ahead = index_block(s // 2 + j + 1)
                 square = x * x
-                seen = inside[:, begin : begin + COLBLK]
-                c = jnp.where(seen, evaluate(COS_SERIES, square), 0.0)
-                d = jnp.where(seen, evaluate(SIN_SERIES, square) * x, 0.0)
+                c = evaluate(COS_SERIES, square)
+                d = evaluate(SIN_SERIES, square) * x
+                if begin < cone or begin + COLBLK > cone + broad:
+                    seen = inside[:, begin : begin + COLBLK]
+                    c, d = jnp.where(seen, c, 0.0), jnp.where(seen, d, 0.0)
                 if s > 0:
                     cosine[s, :, j * COLBLK : (j + 1) * COLBLK] = c
                     sine[s, :, j * COLBLK : (j + 1) * COLBLK] = d
@@ -435,7 +438,8 @@
                 seen = jnp.concatenate(seen, axis=0).astype(jnp.float32)
                 begin = slices * HALFCOL + j * COLBLK
                 error = 2.0 * (a * a + b * b - seen)
-                error = jnp.where(inside[:, begin : begin + COLBLK], error, 0.0)
+                if begin < cone or begin + COLBLK > cone + broad:
+                    error = jnp.where(inside[:, begin : begin + COLBLK], error, 0.0)
                 parts = operand(error * a, error * b)
                 if j > 0:
                     mix_cols(slices, j - 1, last, parts, adjoint_cols)

time: 49.6 us -> 49.7 us (level)
  no operation moved by 1% of the time
where the time goes in v7:
time: 49.7 us; the launch traced here: 49.5 us
  starting transfers between devices  19.3 us (39%)
  waiting for transfers between devices  13.7 us (28%)
  Pallas kernels  12.5 us (25%)
  local copies, waits for them, and re-layouts  2.52 us (5%)
  between operations  0.96 us (2%)
    ppermute x16, starting transfers between devices, swap(): return lax.ppermute(x, axis, [(i, i ^ step) for i in range(size)])  19.3 us
    ppermute x16, waiting for transfers between devices, swap(): return lax.ppermute(x, axis, [(i, i ^ step) for i in range(size)])  13.7 us
    pallas_call x1, Pallas kernels, window_body(): pl.pallas_call(functools.partial(sweep, sizes), out_shape=[jax.ShapeDtype...  11.9 us
    unnamed x14, local copies, waits for them, and re-layouts  2.31 us
  transfers between devices with their start and end apart: 16, of which 10 were waited for; matrix products, arithmetic and copies ran while one was open for 1% of the time, Pallas kernels for 0%

profile of v7, /device:TPU:0, one launch (start us, length us, event | category | flops | bytes accessed | tf_op | source)
XLA Modules:
  0.0 49.5 jit_solution(8078308806445847422)
XLA Ops:
  0.0 5.0 %collective-permute-start.3 = (bf16[16,2048]{1,0:T(8,128)(2,1)}, bf16[16,2048]{1,0:T(8,128)(2,1)S(1)}, u32[]{:S(2)}, u32[]{:S(2)}) collective-permute-start(bf16[16,2048]{1,0:T(8,128)(2,1)} %bitcast.47), channel_id=1, source_target_pairs={{0,6},{1,7},{2,4},{3,5},{4,2},{5,3},{6,0},{7,1},{8,14},{9,15},{10,... | collective-permute-start | bytes 196616 | tf_op jit(solution)/shard_map/ppermute | solution.py:498
  5.1 1.4 %collective-permute-start.2 = (bf16[16,1536]{1,0:T(8,128)(2,1)S(1)}, bf16[16,1536]{1,0:T(8,128)(2,1)S(1)}, u32[]{:S(2)}, u32[]{:S(2)}) collective-permute-start(bf16[16,1536]{1,0:T(8,128)(2,1)S(1)} %get-tuple-element.30), channel_id=1, source_target_pairs={{0,4},{1,5},{2,6},{3,7},{4,0},{5,1},{6,2},{7,3},{8,12},{9,13},{10,... | collective-permute-start | bytes 147464 | tf_op jit(solution)/shard_map/ppermute | solution.py:498
  7.3 0.6 %copy-done.6 = s32[2]{0:T(128)S(1)} copy-done((s32[2]{0:T(128)S(1)}, s32[2]{0:T(128)}, u32[]{:S(2)}) %copy-start.6) | copy-done | bytes 32
  8.1 0.8 %copy-done = bf16[256,128]{1,0:T(8,128)(2,1)S(1)} copy-done((bf16[256,128]{1,0:T(8,128)(2,1)S(1)}, bf16[256,128]{1,0:T(8,128)(2,1)}, u32[]{:S(2)}) %copy-start) | copy-done | bytes 65560
  9.0 0.8 %copy-done.5 = bf16[256,128]{1,0:T(8,128)(2,1)S(1)} copy-done((bf16[256,128]{1,0:T(8,128)(2,1)S(1)}, bf16[256,128]{1,0:T(8,128)(2,1)}, u32[]{:S(2)}) %copy-start.5) | copy-done | bytes 65560
  9.9 0.6 %collective-permute-done.2 = bf16[16,1536]{1,0:T(8,128)(2,1)S(1)} collective-permute-done((bf16[16,1536]{1,0:T(8,128)(2,1)S(1)}, bf16[16,1536]{1,0:T(8,128)(2,1)S(1)}, u32[]{:S(2)}, u32[]{:S(2)}) %collective-permute-start.2) | collective-permute-done | bytes 49184 | tf_op jit(solution)/shard_map/ppermute | solution.py:498
  10.6 1.6 %collective-permute-start.5 = (bf16[4,16,1408]{2,1,0:T(8,128)(2,1)S(1)}, bf16[4,16,1408]{2,1,0:T(8,128)(2,1)S(1)}, u32[]{:S(2)}, u32[]{:S(2)}) collective-permute-start(bf16[4,16,1408]{2,1,0:T(8,128)(2,1)S(1)} %concatenate.61), channel_id=1, source_target_pairs={{0,16},{8,24},{16,0},{24,8},{1,17},{9,25},{17,1},{25,9},{2,18},{10... | collective-permute-start | bytes 540680 | tf_op jit(solution)/shard_map/ppermute | solution.py:498
  12.1 1.4 %collective-permute-start.6 = (bf16[4,16,1408]{2,1,0:T(8,128)(2,1)S(1)}, bf16[4,16,1408]{2,1,0:T(8,128)(2,1)S(1)}, u32[]{:S(2)}, u32[]{:S(2)}) collective-permute-start(bf16[4,16,1408]{2,1,0:T(8,128)(2,1)S(1)} %concatenate.62), channel_id=1, source_target_pairs={{0,24},{8,16},{16,8},{24,0},{1,25},{9,17},{17,9},{25,1},{2,26},{10... | collective-permute-start | bytes 540680 | tf_op jit(solution)/shard_map/ppermute | solution.py:498
  13.6 0.6 %collective-permute-start.4 = (bf16[4,16,1408]{2,1,0:T(8,128)(2,1)S(1)}, bf16[4,16,1408]{2,1,0:T(8,128)(2,1)S(1)}, u32[]{:S(2)}, u32[]{:S(2)}) collective-permute-start(bf16[4,16,1408]{2,1,0:T(8,128)(2,1)S(1)} %concatenate.60), channel_id=1, source_target_pairs={{0,8},{8,0},{16,24},{24,16},{1,9},{9,1},{17,25},{25,17},{2,10},{10... | collective-permute-start | bytes 540680 | tf_op jit(solution)/shard_map/ppermute | solution.py:498
  14.2 1.7 %collective-permute-start.9 = (bf16[2,16,768]{2,1,0:T(8,128)(2,1)S(1)}, bf16[2,16,768]{2,1,0:T(8,128)(2,1)S(1)}, u32[]{:S(2)}, u32[]{:S(2)}) collective-permute-start(bf16[2,16,768]{2,1,0:T(8,128)(2,1)S(1)} %get-tuple-element.35), channel_id=1, source_target_pairs={{0,2},{1,3},{2,0},{3,1},{4,6},{5,7},{6,4},{7,5},{8,10},{9,11},{10,... | collective-permute-start | bytes 147464 | tf_op jit(solution)/shard_map/ppermute | solution.py:498
  15.9 2.3 %collective-permute-done.9 = bf16[2,16,768]{2,1,0:T(8,128)(2,1)S(1)} collective-permute-done((bf16[2,16,768]{2,1,0:T(8,128)(2,1)S(1)}, bf16[2,16,768]{2,1,0:T(8,128)(2,1)S(1)}, u32[]{:S(2)}, u32[]{:S(2)}) %collective-permute-start.9) | collective-permute-done | bytes 49184 | tf_op jit(solution)/shard_map/ppermute | solution.py:498
  18.3 1.8 %collective-permute-start.10 = (bf16[2,2,16,768]{3,2,1,0:T(8,128)(2,1)S(1)}, bf16[2,2,16,768]{3,2,1,0:T(8,128)(2,1)S(1)}, u32[]{:S(2)}, u32[]{:S(2)}) collective-permute-start(bf16[2,2,16,768]{3,2,1,0:T(8,128)(2,1)S(1)} %pad_maximum_fusion.12), channel_id=1, source_target_pairs={{0,4},{1,5},{2,6},{3,7},{4,0},{5,1},{6,2},{7,3},{8,12},{9,13},{10,... | collective-permute-start | bytes 294920 | tf_op jit(solution)/shard_map/ppermute | solution.py:498
  20.0 0.8 %collective-permute-done.5 = bf16[4,16,1408]{2,1,0:T(8,128)(2,1)S(1)} collective-permute-done((bf16[4,16,1408]{2,1,0:T(8,128)(2,1)S(1)}, bf16[4,16,1408]{2,1,0:T(8,128)(2,1)S(1)}, u32[]{:S(2)}, u32[]{:S(2)}) %collective-permute-start.5) | collective-permute-done | bytes 180256 | tf_op jit(solution)/shard_map/ppermute | solution.py:498
  20.9 1.2 %collective-permute-done.4 = bf16[4,16,1408]{2,1,0:T(8,128)(2,1)S(1)} collective-permute-done((bf16[4,16,1408]{2,1,0:T(8,128)(2,1)S(1)}, bf16[4,16,1408]{2,1,0:T(8,128)(2,1)S(1)}, u32[]{:S(2)}, u32[]{:S(2)}) %collective-permute-start.4) | collective-permute-done | bytes 180256 | tf_op jit(solution)/shard_map/ppermute | solution.py:498
  22.2 1.6 %collective-permute-done.10 = bf16[2,2,16,768]{3,2,1,0:T(8,128)(2,1)S(1)} collective-permute-done((bf16[2,2,16,768]{3,2,1,0:T(8,128)(2,1)S(1)}, bf16[2,2,16,768]{3,2,1,0:T(8,128)(2,1)S(1)}, u32[]{:S(2)}, u32[]{:S(2)}) %collective-permute-start.10) | collective-permute-done | bytes 98336 | tf_op jit(solution)/shard_map/ppermute | solution.py:498
  24.2 11.9 %shard_map.82 = (f32[4,32,256]{2,1,0:T(8,128)S(1)}, f32[4,32,256]{2,1,0:T(8,128)S(1)}) custom-call(s32[2,2]{1,0:T(2,128)S(1)} %pad_add_fusion.tilts, bf16[4,16,128]{2,1,0:T(8,128)(2,1)S(1)} %pad_maximum_fusion.14.tiles, bf16[4,64,1280]{2,1,0:T(8,128)(2,1)S(1)} %pad_maximum_fusion.8.own, bf16[4,64,1280]{2,1,0:T(8,128)(2,1)S(1)} %pad_maximum_fusion.9.other, ...), custom_call_target="tpu_custom_call" | custom-call | tf_op jit(solution)/shard_map/pallas_call | solution.py:555
  36.2 1.2 %collective-permute-done.11 = f32[4,32,256]{2,1,0:T(8,128)S(1)} collective-permute-done((f32[4,32,256]{2,1,0:T(8,128)S(1)}, f32[4,32,256]{2,1,0:T(8,128)S(1)}, u32[]{:S(2)}, u32[]{:S(2)}) %collective-permute-start.11) | collective-permute-done | bytes 131104 | tf_op jit(solution)/shard_map/ppermute | solution.py:498
  37.5 1.8 %collective-permute-start.12 = (f32[4,16,256]{2,1,0:T(8,128)S(1)}, f32[4,16,256]{2,1,0:T(8,128)S(1)}, u32[]{:S(2)}, u32[]{:S(2)}) collective-permute-start(f32[4,16,256]{2,1,0:T(8,128)S(1)} %get-tuple-element.53), channel_id=1, source_target_pairs={{0,2},{1,3},{2,0},{3,1},{4,6},{5,7},{6,4},{7,5},{8,10},{9,11},{10,... | collective-permute-start | bytes 196616 | tf_op jit(solution)/shard_map/ppermute | solution.py:498
  39.3 2.5 %collective-permute-done.12 = f32[4,16,256]{2,1,0:T(8,128)S(1)} collective-permute-done((f32[4,16,256]{2,1,0:T(8,128)S(1)}, f32[4,16,256]{2,1,0:T(8,128)S(1)}, u32[]{:S(2)}, u32[]{:S(2)}) %collective-permute-start.12) | collective-permute-done | bytes 65568 | tf_op jit(solution)/shard_map/ppermute | solution.py:498
  41.8 2.5 %collective-permute-start.15 = (f32[2,16,256]{2,1,0:T(8,128)S(1)}, f32[2,16,256]{2,1,0:T(8,128)S(1)}, u32[]{:S(2)}, u32[]{:S(2)}) collective-permute-start(f32[2,16,256]{2,1,0:T(8,128)S(1)} %get-tuple-element.49), channel_id=1, source_target_pairs={{0,24},{8,16},{16,8},{24,0},{1,25},{9,17},{17,9},{25,1},{2,26},{10... | collective-permute-start | bytes 98312 | tf_op jit(solution)/shard_map/ppermute | solution.py:498
  45.4 1.3 %collective-permute-done.15.refs_3_ = f32[2,16,256]{2,1,0:T(8,128)S(1)} collective-permute-done((f32[2,16,256]{2,1,0:T(8,128)S(1)}, f32[2,16,256]{2,1,0:T(8,128)S(1)}, u32[]{:S(2)}, u32[]{:S(2)}) %collective-permute-start.15) | collective-permute-done | bytes 32800 | tf_op jit(solution)/shard_map/ppermute | solution.py:498
  46.7 1.5 %collective-permute-done.13.refs_1_ = f32[2,16,256]{2,1,0:T(8,128)S(1)} collective-permute-done((f32[2,16,256]{2,1,0:T(8,128)S(1)}, f32[2,16,256]{2,1,0:T(8,128)S(1)}, u32[]{:S(2)}, u32[]{:S(2)}) %collective-permute-start.13) | collective-permute-done | bytes 32800 | tf_op jit(solution)/shard_map/ppermute | solution.py:498
  48.3 0.5 %collective-permute-done.14.refs_2_ = f32[2,16,256]{2,1,0:T(8,128)S(1)} collective-permute-done((f32[2,16,256]{2,1,0:T(8,128)S(1)}, f32[2,16,256]{2,1,0:T(8,128)S(1)}, u32[]{:S(2)}, u32[]{:S(2)}) %collective-permute-start.14) | collective-permute-done | bytes 32800 | tf_op jit(solution)/shard_map/ppermute | solution.py:498
  48.8 0.7 %shard_map.83 = f32[1,16,2048]{2,1,0:T(8,128)} custom-call(f32[2,16,256]{2,1,0:T(8,128)S(1)} %get-tuple-element.50.refs_0_, f32[2,16,256]{2,1,0:T(8,128)S(1)} %collective-permute-done.13.refs_1_, f32[2,16,256]{2,1,0:T(8,128)S(1)} %collective-permute-done.14.refs_2_, f32[2,16,256]{2,1,0:T(8,128)S(1)} %collective-permute-done.15.refs_3_), custom_call_target="tpu_custom_call" | custom-call | tf_op jit(solution)/shard_map/pallas_call | solution.py:572
  (54 shorter events, 2.2 us)
Async XLA Ops:
  0.0 5.1 %copy-start.2 = (bf16[1,16,2048]{2,1,0:T(8,128)(2,1)S(1)}, bf16[1,16,2048]{2,1,0:T(8,128)(2,1)}, u32[]{:S(2)}) copy-start(bf16[1,16,2048]{2,1,0:T(8,128)(2,1)} %param.8) | copy-start | bytes 196612
  0.0 8.9 %collective-permute-start.3 = (bf16[16,2048]{1,0:T(8,128)(2,1)}, bf16[16,2048]{1,0:T(8,128)(2,1)S(1)}, u32[]{:S(2)}, u32[]{:S(2)}) collective-permute-start(bf16[16,2048]{1,0:T(8,128)(2,1)} %bitcast.47), channel_id=1, source_target_pairs={{0,6},{1,7},{2,4},{3,5},{4,2},{5,3},{6,0},{7,1},{8,14},{9,15},{10,... | collective-permute-start | bytes 196616 | tf_op jit(solution)/shard_map/ppermute | solution.py:498
  5.1 1.5 %copy-start.3 = (bf16[2,16,2048]{2,1,0:T(8,128)(2,1)S(1)}, bf16[2,16,2048]{2,1,0:T(8,128)(2,1)}, u32[]{:S(2)}) copy-start(bf16[2,16,2048]{2,1,0:T(8,128)(2,1)} %param.11) | copy-start | bytes 393220
  5.1 4.8 %collective-permute-start.1 = (bf16[16,1536]{1,0:T(8,128)(2,1)S(1)}, bf16[16,1536]{1,0:T(8,128)(2,1)S(1)}, u32[]{:S(2)}, u32[]{:S(2)}) collective-permute-start(bf16[16,1536]{1,0:T(8,128)(2,1)S(1)} %get-tuple-element.57), channel_id=1, source_target_pairs={{0,2},{1,3},{2,0},{3,1},{4,6},{5,7},{6,4},{7,5},{8,10},{9,11},{10,... | collective-permute-start | bytes 147464 | tf_op jit(solution)/shard_map/ppermute | solution.py:498
  5.1 5.3 %collective-permute-start.2 = (bf16[16,1536]{1,0:T(8,128)(2,1)S(1)}, bf16[16,1536]{1,0:T(8,128)(2,1)S(1)}, u32[]{:S(2)}, u32[]{:S(2)}) collective-permute-start(bf16[16,1536]{1,0:T(8,128)(2,1)S(1)} %get-tuple-element.30), channel_id=1, source_target_pairs={{0,4},{1,5},{2,6},{3,7},{4,0},{5,1},{6,2},{7,3},{8,12},{9,13},{10,... | collective-permute-start | bytes 147464 | tf_op jit(solution)/shard_map/ppermute | solution.py:498
  6.5 1.4 %collective-permute-start = (bf16[16,2048]{1,0:T(8,128)(2,1)S(1)}, bf16[16,2048]{1,0:T(8,128)(2,1)S(1)}, u32[]{:S(2)}, u32[]{:S(2)}) collective-permute-start(bf16[16,2048]{1,0:T(8,128)(2,1)S(1)} %get-tuple-element.56), channel_id=1, source_target_pairs={{0,1},{1,0},{2,3},{3,2},{4,5},{5,4},{6,7},{7,6},{8,9},{9,8},{10,11... | collective-permute-start | bytes 196616 | tf_op jit(solution)/shard_map/ppermute | solution.py:498
  7.3 0.7 %copy-start.6 = (s32[2]{0:T(128)S(1)}, s32[2]{0:T(128)}, u32[]{:S(2)}) copy-start(s32[2]{0:T(128)} %param.9) | copy-start | bytes 28
  8.0 0.8 %copy-start = (bf16[256,128]{1,0:T(8,128)(2,1)S(1)}, bf16[256,128]{1,0:T(8,128)(2,1)}, u32[]{:S(2)}) copy-start(bf16[256,128]{1,0:T(8,128)(2,1)} %constant.93.clone) | copy-start | bytes 196612
  8.0 0.9 %copy-start.1 = (bf16[256,128]{1,0:T(8,128)(2,1)S(1)}, bf16[256,128]{1,0:T(8,128)(2,1)}, u32[]{:S(2)}) copy-start(bf16[256,128]{1,0:T(8,128)(2,1)} %constant.91.clone) | copy-start | bytes 196612
  8.9 0.8 %copy-start.5 = (bf16[256,128]{1,0:T(8,128)(2,1)S(1)}, bf16[256,128]{1,0:T(8,128)(2,1)}, u32[]{:S(2)}) copy-start(bf16[256,128]{1,0:T(8,128)(2,1)} %constant.90.clone) | copy-start | bytes 196612
  8.9 0.9 %copy-start.4 = (bf16[256,128]{1,0:T(8,128)(2,1)S(1)}, bf16[256,128]{1,0:T(8,128)(2,1)}, u32[]{:S(2)}) copy-start(bf16[256,128]{1,0:T(8,128)(2,1)} %constant.92.clone) | copy-start | bytes 196612
  10.6 10.3 %collective-permute-start.5 = (bf16[4,16,1408]{2,1,0:T(8,128)(2,1)S(1)}, bf16[4,16,1408]{2,1,0:T(8,128)(2,1)S(1)}, u32[]{:S(2)}, u32[]{:S(2)}) collective-permute-start(bf16[4,16,1408]{2,1,0:T(8,128)(2,1)S(1)} %concatenate.61), channel_id=1, source_target_pairs={{0,16},{8,24},{16,0},{24,8},{1,17},{9,25},{17,1},{25,9},{2,18},{10... | collective-permute-start | bytes 540680 | tf_op jit(solution)/shard_map/ppermute | solution.py:498
  12.1 8.7 %collective-permute-start.6 = (bf16[4,16,1408]{2,1,0:T(8,128)(2,1)S(1)}, bf16[4,16,1408]{2,1,0:T(8,128)(2,1)S(1)}, u32[]{:S(2)}, u32[]{:S(2)}) collective-permute-start(bf16[4,16,1408]{2,1,0:T(8,128)(2,1)S(1)} %concatenate.62), channel_id=1, source_target_pairs={{0,24},{8,16},{16,8},{24,0},{1,25},{9,17},{17,9},{25,1},{2,26},{10... | collective-permute-start | bytes 540680 | tf_op jit(solution)/shard_map/ppermute | solution.py:498
  13.6 8.5 %collective-permute-start.4 = (bf16[4,16,1408]{2,1,0:T(8,128)(2,1)S(1)}, bf16[4,16,1408]{2,1,0:T(8,128)(2,1)S(1)}, u32[]{:S(2)}, u32[]{:S(2)}) collective-permute-start(bf16[4,16,1408]{2,1,0:T(8,128)(2,1)S(1)} %concatenate.60), channel_id=1, source_target_pairs={{0,8},{8,0},{16,24},{24,16},{1,9},{9,1},{17,25},{25,17},{2,10},{10... | collective-permute-start | bytes 540680 | tf_op jit(solution)/shard_map/ppermute | solution.py:498
  14.2 4.1 %collective-permute-start.9 = (bf16[2,16,768]{2,1,0:T(8,128)(2,1)S(1)}, bf16[2,16,768]{2,1,0:T(8,128)(2,1)S(1)}, u32[]{:S(2)}, u32[]{:S(2)}) collective-permute-start(bf16[2,16,768]{2,1,0:T(8,128)(2,1)S(1)} %get-tuple-element.35), channel_id=1, source_target_pairs={{0,2},{1,3},{2,0},{3,1},{4,6},{5,7},{6,4},{7,5},{8,10},{9,11},{10,... | collective-permute-start | bytes 147464 | tf_op jit(solution)/shard_map/ppermute | solution.py:498
  15.9 8.2 %collective-permute-start.7 = (bf16[1,64,1280]{2,1,0:T(8,128)(2,1)S(1)}, bf16[1,64,1280]{2,1,0:T(8,128)(2,1)S(1)}, u32[]{:S(2)}, u32[]{:S(2)}) collective-permute-start(bf16[1,64,1280]{2,1,0:T(8,128)(2,1)S(1)} %bitcast.42), channel_id=1, source_target_pairs={{0,1},{1,0},{2,3},{3,2},{4,5},{5,4},{6,7},{7,6},{8,9},{9,8},{10,11... | collective-permute-start | bytes 491528 | tf_op jit(solution)/shard_map/ppermute | solution.py:498
  18.3 5.6 %collective-permute-start.10 = (bf16[2,2,16,768]{3,2,1,0:T(8,128)(2,1)S(1)}, bf16[2,2,16,768]{3,2,1,0:T(8,128)(2,1)S(1)}, u32[]{:S(2)}, u32[]{:S(2)}) collective-permute-start(bf16[2,2,16,768]{3,2,1,0:T(8,128)(2,1)S(1)} %pad_maximum_fusion.12), channel_id=1, source_target_pairs={{0,4},{1,5},{2,6},{3,7},{4,0},{5,1},{6,2},{7,3},{8,12},{9,13},{10,... | collective-permute-start | bytes 294920 | tf_op jit(solution)/shard_map/ppermute | solution.py:498
  22.2 1.9 %collective-permute-start.8 = (bf16[3,64,1280]{2,1,0:T(8,128)(2,1)S(1)}, bf16[3,64,1280]{2,1,0:T(8,128)(2,1)S(1)}, u32[]{:S(2)}, u32[]{:S(2)}) collective-permute-start(bf16[3,64,1280]{2,1,0:T(8,128)(2,1)S(1)} %pad_maximum_fusion.10), channel_id=1, source_target_pairs={{0,1},{1,0},{2,3},{3,2},{4,5},{5,4},{6,7},{7,6},{8,9},{9,8},{10,11... | collective-permute-start | bytes 1474568 | tf_op jit(solution)/shard_map/ppermute | solution.py:498
  36.0 1.4 %collective-permute-start.11 = (f32[4,32,256]{2,1,0:T(8,128)S(1)}, f32[4,32,256]{2,1,0:T(8,128)S(1)}, u32[]{:S(2)}, u32[]{:S(2)}) collective-permute-start(f32[4,32,256]{2,1,0:T(8,128)S(1)} %get-tuple-element.40), channel_id=1, source_target_pairs={{0,1},{1,0},{2,3},{3,2},{4,5},{5,4},{6,7},{7,6},{8,9},{9,8},{10,11... | collective-permute-start | bytes 393224 | tf_op jit(solution)/shard_map/ppermute | solution.py:498
  37.5 4.3 %collective-permute-start.12 = (f32[4,16,256]{2,1,0:T(8,128)S(1)}, f32[4,16,256]{2,1,0:T(8,128)S(1)}, u32[]{:S(2)}, u32[]{:S(2)}) collective-permute-start(f32[4,16,256]{2,1,0:T(8,128)S(1)} %get-tuple-element.53), channel_id=1, source_target_pairs={{0,2},{1,3},{2,0},{3,1},{4,6},{5,7},{6,4},{7,5},{8,10},{9,11},{10,... | collective-permute-start | bytes 196616 | tf_op jit(solution)/shard_map/ppermute | solution.py:498
  41.8 4.9 %collective-permute-start.15 = (f32[2,16,256]{2,1,0:T(8,128)S(1)}, f32[2,16,256]{2,1,0:T(8,128)S(1)}, u32[]{:S(2)}, u32[]{:S(2)}) collective-permute-start(f32[2,16,256]{2,1,0:T(8,128)S(1)} %get-tuple-element.49), channel_id=1, source_target_pairs={{0,24},{8,16},{16,8},{24,0},{1,25},{9,17},{17,9},{25,1},{2,26},{10... | collective-permute-start | bytes 98312 | tf_op jit(solution)/shard_map/ppermute | solution.py:498
  44.4 3.9 %collective-permute-start.13 = (f32[2,16,256]{2,1,0:T(8,128)S(1)}, f32[2,16,256]{2,1,0:T(8,128)S(1)}, u32[]{:S(2)}, u32[]{:S(2)}) collective-permute-start(f32[2,16,256]{2,1,0:T(8,128)S(1)} %get-tuple-element.51), channel_id=1, source_target_pairs={{0,8},{8,0},{16,24},{24,16},{1,9},{9,1},{17,25},{25,17},{2,10},{10... | collective-permute-start | bytes 98312 | tf_op jit(solution)/shard_map/ppermute | solution.py:498
  44.9 3.9 %collective-permute-start.14 = (f32[2,16,256]{2,1,0:T(8,128)S(1)}, f32[2,16,256]{2,1,0:T(8,128)S(1)}, u32[]{:S(2)}, u32[]{:S(2)}) collective-permute-start(f32[2,16,256]{2,1,0:T(8,128)S(1)} %get-tuple-element.52), channel_id=1, source_target_pairs={{0,16},{8,24},{16,0},{24,8},{1,17},{9,25},{17,1},{25,9},{2,18},{10... | collective-permute-start | bytes 98312 | tf_op jit(solution)/shard_map/ppermute | solution.py:498
